TPU v7x, 32 devices: a whole 2x2x4 slice. The times are simulated.
32 devices in a mesh: gx: 2 (over x), gy: 4 (over z), gz: 4 (over y, core).
Axes of the slice: x: 2, y: 2, z: 4, core: 2. Of those that a mesh axis runs over, the one named last changes fastest.
Arguments:
- right_side: float32 [16, 64, 512], P('gx', 'gy', 'gz'), may hold values from -6 to 6
- coefficient: float32 [16, 64, 512], P('gx', 'gy', 'gz'), may hold values from 0.25 to 4
Outputs:
- solution: float32 [16, 64, 512], P('gx', 'gy', 'gz')
- residual: float32 [16, 64, 512], P('gx', 'gy', 'gz')
All inputs are finite; a program needn't handle non-finite values.
Results may differ from a plain program's by a relative error of at most 0.0003.
Values sent between devices are 32-bit elements; how exact they have to be, the bound alone decides.
No kernel may reach another device: no remote copies, remote signals or barrier semaphores. Data moves between devices by JAX's collectives and lax.ppermute only.
A program may use at most 64 MiB of HBM per device.

v0:
```python
import jax
import jax.numpy as jnp
from jax import lax
from jax.sharding import PartitionSpec as P

LEVELS = 3
DEGREE = 4


cheb_low = 0.3
cheb_high = 2.0


def extended(block, sides, width):
    for axis, dim in sides:
        count = lax.axis_size(axis)
        forward = [(i, i + 1) for i in range(count - 1)]
        backward = [(target, source) for source, target in forward]
        low = lax.ppermute(
            lax.slice_in_dim(block, block.shape[dim] - width, None, axis=dim), axis, forward
        )
        high = lax.ppermute(lax.slice_in_dim(block, 0, width, axis=dim), axis, backward)
        block = jnp.concatenate([low, block, high], axis=dim)
    return block


def face_terms(padded):
    face_x = 0.5 * (padded[1:, 1:-1, 1:-1] + padded[:-1, 1:-1, 1:-1])
    face_y = 0.5 * (padded[1:-1, 1:, 1:-1] + padded[1:-1, :-1, 1:-1])
    face_z = 0.5 * (padded[1:-1, 1:-1, 1:] + padded[1:-1, 1:-1, :-1])
    diagonal = (
        face_x[1:]
        + face_x[:-1]
        + face_y[:, 1:]
        + face_y[:, :-1]
        + face_z[:, :, 1:]
        + face_z[:, :, :-1]
    )
    return (face_x, face_y, face_z, diagonal)


def apply_padded(padded, face_set, factor):
    face_x, face_y, face_z, diagonal = face_set
    flux_x = face_x * (padded[1:, 1:-1, 1:-1] - padded[:-1, 1:-1, 1:-1])
    flux_y = face_y * (padded[1:-1, 1:, 1:-1] - padded[1:-1, :-1, 1:-1])
    flux_z = face_z * (padded[1:-1, 1:-1, 1:] - padded[1:-1, 1:-1, :-1])
    result = (
        flux_x[:-1]
        - flux_x[1:]
        + (flux_y[:, :-1] - flux_y[:, 1:])
        + (flux_z[:, :, :-1] - flux_z[:, :, 1:])
    )
    return factor * result


def fine_halo(values):
    return extended(values, (("gx", 0), ("gy", 1), ("gz", 2)), 1)


def spread_halo(values):
    return extended(values, (("gx", 0), ("gy", 1), ("gz", 2)), 1)


def restrict(values):
    size_x, size_y, size_z = values.shape
    blocks = values.reshape(size_x // 2, 2, size_y // 2, 2, size_z // 2, 2)
    return jnp.mean(blocks, axis=(1, 3, 5))


def prolong(values):
    size_x, size_y, size_z = values.shape
    spread = jnp.broadcast_to(values[:, None, :, None, :, None], (size_x, 2, size_y, 2, size_z, 2))
    return spread.reshape(2 * size_x, 2 * size_y, 2 * size_z)


def trim_cells(values, layers):
    return values[
        layers : values.shape[0] - layers,
        layers : values.shape[1] - layers,
        layers : values.shape[2] - layers,
    ]


def trim_faces(face_set, layers):
    return tuple((trim_cells(member, layers) for member in face_set))


def inside_mask(shape, margin):
    count_x = shape[0]
    count_y = shape[1]
    count_z = shape[2]
    along_x = lax.axis_index("gx") * count_x + jnp.arange(
        -margin, count_x + margin, dtype=jnp.int32
    )
    along_y = lax.axis_index("gy") * count_y + jnp.arange(
        -margin, count_y + margin, dtype=jnp.int32
    )
    along_z = lax.axis_index("gz") * count_z + jnp.arange(
        -margin, count_z + margin, dtype=jnp.int32
    )
    valid_x = (along_x >= 0) & (along_x < count_x * lax.axis_size("gx"))
    valid_y = (along_y >= 0) & (along_y < count_y * lax.axis_size("gy"))
    valid_z = (along_z >= 0) & (along_z < count_z * lax.axis_size("gz"))
    return valid_x[:, None, None] & valid_y[None, :, None] & valid_z[None, None, :]


def deep_smooth(right_wide, start_wide, face_wide, valid_wide):
    centre = 0.5 * (cheb_high + cheb_low)
    half_width = 0.5 * (cheb_high - cheb_low)
    sigma_val = centre / half_width
    rho_now = 1.0 / sigma_val
    safe_diag = jnp.where(valid_wide, face_wide[3], 1.0)
    if start_wide is None:
        update = jnp.where(valid_wide, right_wide / (1.0 * safe_diag) / centre, 0.0)
        iterate = update
        lost = 0
    else:
        leftover = trim_cells(right_wide, 1) - apply_padded(
            start_wide, trim_faces(face_wide, 1), 1.0
        )
        update = jnp.where(
            trim_cells(valid_wide, 1), leftover / (1.0 * trim_cells(safe_diag, 1)) / centre, 0.0
        )
        iterate = trim_cells(start_wide, 1) + update
        lost = 1
    for sweep_no in range(DEGREE - 1):
        lost = lost + 1
        leftover = trim_cells(right_wide, lost) - apply_padded(
            iterate, trim_faces(face_wide, lost), 1.0
        )
        rho_next = 1.0 / (2.0 * sigma_val - rho_now)
        fresh = rho_next * rho_now * trim_cells(update, 1) + 2.0 * rho_next / half_width * (
            leftover / (1.0 * trim_cells(safe_diag, lost))
        )
        update = jnp.where(trim_cells(valid_wide, lost), fresh, 0.0)
        iterate = trim_cells(iterate, 1) + update
        rho_now = rho_next
    return (iterate, lost)


def smooth(right, initial, face_set, factor, padder):
    diagonal = face_set[3]
    centre = 0.5 * (cheb_high + cheb_low)
    half_width = 0.5 * (cheb_high - cheb_low)
    sigma_val = centre / half_width
    rho_now = 1.0 / sigma_val
    if initial is None:
        iterate = jnp.zeros_like(right)
        leftover = right
    else:
        iterate = initial
        leftover = right - apply_padded(padder(initial), face_set, factor)
    update = leftover / (factor * diagonal) / centre
    iterate = iterate + update
    for sweep_no in range(DEGREE - 1):
        leftover = right - apply_padded(padder(iterate), face_set, factor)
        rho_next = 1.0 / (2.0 * sigma_val - rho_now)
        update = rho_next * rho_now * update + 2.0 * rho_next / half_width * (
            leftover / (factor * diagonal)
        )
        iterate = iterate + update
        rho_now = rho_next
    return iterate


def per_device(right_side, coefficient):
    depth = DEGREE
    stacked = jnp.stack([right_side, coefficient])
    widened = extended(stacked, (("gx", 1), ("gy", 2), ("gz", 3)), depth + 1)
    right_wide = trim_cells(widened[0], 1)
    face_wide = face_terms(widened[1])
    valid_wide = inside_mask(right_side.shape, depth)
    fine_set = trim_faces(face_wide, depth)
    partial_value, lost = deep_smooth(right_wide, None, face_wide, valid_wide)
    leftover = right_side - apply_padded(partial_value, trim_faces(face_wide, depth), 1.0)
    iterate = trim_cells(partial_value, 1)
    coarse_right = restrict(leftover)
    coarse_coef = restrict(coefficient)
    rights = [coarse_right]
    face_sets = []
    iterates = []
    for level_no in range(1, LEVELS):
        factor = 0.25**level_no
        face_set = face_terms(spread_halo(coarse_coef))
        face_sets.append(face_set)
        current = smooth(rights[-1], None, face_set, factor, spread_halo)
        iterates.append(current)
        if level_no < LEVELS - 1:
            remains = rights[-1] - apply_padded(spread_halo(current), face_set, factor)
            rights.append(restrict(remains))
            coarse_coef = restrict(coarse_coef)
    level_no = 1
    slot_no = level_no - 1
    iterates[slot_no] = smooth(
        rights[slot_no],
        iterates[slot_no] + prolong(iterates[slot_no + 1]),
        face_sets[slot_no],
        0.25**level_no,
        spread_halo,
    )
    correction = iterates[0]
    start = iterate + prolong(correction)
    start_wide = extended(start, (("gx", 0), ("gy", 1), ("gz", 2)), depth)
    solution, lost = deep_smooth(right_wide, start_wide, face_wide, valid_wide)
    residual = right_side - apply_padded(fine_halo(solution), fine_set, 1.0)
    return (solution, residual)


def solution(mesh):
    in_specs = (P("gx", "gy", "gz"), P("gx", "gy", "gz"))
    out_specs = (P("gx", "gy", "gz"), P("gx", "gy", "gz"))
    return jax.shard_map(
        per_device, mesh=mesh, in_specs=in_specs, out_specs=out_specs, check_vma=False
    )
```

profile of v0, /device:TPU:1, one launch (start us, length us, event | category | flops | bytes accessed | tf_op | source)
XLA Modules:
  0.0 390.5 jit_solution(13580570350909755775)
XLA Ops:
  1.5 3.9 %collective-permute-start = (f32[2,5,16,128]{3,2,1,0:T(8,128)S(1)}, f32[2,5,16,128]{3,2,1,0:T(8,128)S(1)}, u32[]{:S(2)}, u32[]{:S(2)}) collective-permute-start(f32[2,5,16,128]{3,2,1,0:T(8,128)S(1)} %get-tuple-element.42), channel_id=1, source_target_pairs={{0,16},{1,17},{2,18},{3,19},{4,20},{5,21},{6,22},{7,23},{8,24},{9,... | collective-permute-start | bytes 245768 | tf_op jit(solution)/shard_map/ppermute | solution.py:19
  6.8 6.3 %reshape.82 = f32[4,2,8,2,64,2]{5,4,3,2,1,0:T(8,128)} reshape(f32[8,16,128]{2,1,0:T(8,128)} %param.3) | data formatting | bytes 131072 | tf_op jit(solution)/shard_map/reshape | solution.py:66
  15.6 4.1 %collective-permute-start.7 = (f32[1,8,64]{2,1,0:T(8,128)S(1)}, f32[1,8,64]{2,1,0:T(8,128)S(1)}, u32[]{:S(2)}, u32[]{:S(2)}) collective-permute-start(f32[1,8,64]{2,1,0:T(8,128)S(1)} %get-tuple-element.112), channel_id=1, source_target_pairs={{0,16},{1,17},{2,18},{3,19},{4,20},{5,21},{6,22},{7,23},{8,24},{9,... | collective-permute-start | bytes 6152 | tf_op jit(solution)/shard_map/ppermute | solution.py:19
  37.6 6.3 %collective-permute-start.10 = (f32[6,10,1]{2,1,0:T(8,128)S(1)}, f32[6,10,1]{2,1,0:T(8,128)S(1)}, u32[]{:S(2)}, u32[]{:S(2)}) collective-permute-start(f32[6,10,1]{2,1,0:T(8,128)S(1)} %get-tuple-element.68), channel_id=1, source_target_pairs={{1,0},{2,1},{3,2},{5,4},{6,5},{7,6},{9,8},{10,9},{11,10},{13,12},{... | collective-permute-start | bytes 728 | tf_op jit(solution)/shard_map/ppermute | solution.py:22
  50.7 3.5 collective-permute-start.11
  70.5 5.5 %reshape.81 = f32[4,2,8,2,64,2]{5,4,3,2,1,0:T(8,128)} reshape(f32[8,16,128]{2,1,0:T(8,128)S(1)} %fusion.89) | data formatting | bytes 131072 | tf_op jit(solution)/shard_map/reshape | solution.py:66
  84.7 3.5 collective-permute-start.15
  95.6 6.2 %collective-permute-start.17 = (f32[6,10,1]{2,1,0:T(8,128)S(1)}, f32[6,10,1]{2,1,0:T(8,128)S(1)}, u32[]{:S(2)}, u32[]{:S(2)}) collective-permute-start(f32[6,10,1]{2,1,0:T(8,128)S(1)} %get-tuple-element.67), channel_id=1, source_target_pairs={{0,1},{1,2},{2,3},{4,5},{5,6},{6,7},{8,9},{9,10},{10,11},{12,13},{... | collective-permute-start | bytes 728 | tf_op jit(solution)/shard_map/ppermute | solution.py:19
  107.8 4.5 %collective-permute-start.41 = (f32[4,6,1]{2,1,0:T(8,128)S(1)}, f32[4,6,1]{2,1,0:T(8,128)S(1)}, u32[]{:S(2)}, u32[]{:S(2)}) collective-permute-start(f32[4,6,1]{2,1,0:T(8,128)S(1)} %get-tuple-element.103), channel_id=1, source_target_pairs={{0,1},{1,2},{2,3},{4,5},{5,6},{6,7},{8,9},{9,10},{10,11},{12,13},{... | collective-permute-start | bytes 296 | tf_op jit(solution)/shard_map/ppermute | solution.py:19
  121.2 3.8 collective-permute-start.23
  126.4 4.3 %collective-permute-start.25 = (f32[1,8,64]{2,1,0:T(8,128)S(1)}, f32[1,8,64]{2,1,0:T(8,128)S(1)}, u32[]{:S(2)}, u32[]{:S(2)}) collective-permute-start(f32[1,8,64]{2,1,0:T(8,128)S(1)} %get-tuple-element.106), channel_id=1, source_target_pairs={{0,16},{1,17},{2,18},{3,19},{4,20},{5,21},{6,22},{7,23},{8,24},{9,... | collective-permute-start | bytes 6152 | tf_op jit(solution)/shard_map/ppermute | solution.py:19
  145.7 6.0 %collective-permute-start.29 = (f32[6,10,1]{2,1,0:T(8,128)S(1)}, f32[6,10,1]{2,1,0:T(8,128)S(1)}, u32[]{:S(2)}, u32[]{:S(2)}) collective-permute-start(f32[6,10,1]{2,1,0:T(8,128)S(1)} %get-tuple-element.63), channel_id=1, source_target_pairs={{0,1},{1,2},{2,3},{4,5},{5,6},{6,7},{8,9},{9,10},{10,11},{12,13},{... | collective-permute-start | bytes 728 | tf_op jit(solution)/shard_map/ppermute | solution.py:19
  166.9 7.1 %collective-permute-start.35 = (f32[6,10,1]{2,1,0:T(8,128)S(1)}, f32[6,10,1]{2,1,0:T(8,128)S(1)}, u32[]{:S(2)}, u32[]{:S(2)}) collective-permute-start(f32[6,10,1]{2,1,0:T(8,128)S(1)} %get-tuple-element.61), channel_id=1, source_target_pairs={{0,1},{1,2},{2,3},{4,5},{5,6},{6,7},{8,9},{9,10},{10,11},{12,13},{... | collective-permute-start | bytes 728 | tf_op jit(solution)/shard_map/ppermute | solution.py:19
  189.8 7.1 %collective-permute-start.47 = (f32[4,6,1]{2,1,0:T(8,128)S(1)}, f32[4,6,1]{2,1,0:T(8,128)S(1)}, u32[]{:S(2)}, u32[]{:S(2)}) collective-permute-start(f32[4,6,1]{2,1,0:T(8,128)S(1)} %get-tuple-element.101), channel_id=1, source_target_pairs={{0,1},{1,2},{2,3},{4,5},{5,6},{6,7},{8,9},{9,10},{10,11},{12,13},{... | collective-permute-start | bytes 296 | tf_op jit(solution)/shard_map/ppermute | solution.py:19
  211.7 7.3 %collective-permute-start.53 = (f32[4,6,1]{2,1,0:T(8,128)S(1)}, f32[4,6,1]{2,1,0:T(8,128)S(1)}, u32[]{:S(2)}, u32[]{:S(2)}) collective-permute-start(f32[4,6,1]{2,1,0:T(8,128)S(1)} %get-tuple-element.99), channel_id=1, source_target_pairs={{0,1},{1,2},{2,3},{4,5},{5,6},{6,7},{8,9},{9,10},{10,11},{12,13},{... | collective-permute-start | bytes 296 | tf_op jit(solution)/shard_map/ppermute | solution.py:19
  233.4 7.1 %collective-permute-start.59 = (f32[4,6,1]{2,1,0:T(8,128)S(1)}, f32[4,6,1]{2,1,0:T(8,128)S(1)}, u32[]{:S(2)}, u32[]{:S(2)}) collective-permute-start(f32[4,6,1]{2,1,0:T(8,128)S(1)} %get-tuple-element.97), channel_id=1, source_target_pairs={{0,1},{1,2},{2,3},{4,5},{5,6},{6,7},{8,9},{9,10},{10,11},{12,13},{... | collective-permute-start | bytes 296 | tf_op jit(solution)/shard_map/ppermute | solution.py:19
  255.7 7.1 %collective-permute-start.65 = (f32[6,10,1]{2,1,0:T(8,128)S(1)}, f32[6,10,1]{2,1,0:T(8,128)S(1)}, u32[]{:S(2)}, u32[]{:S(2)}) collective-permute-start(f32[6,10,1]{2,1,0:T(8,128)S(1)} %get-tuple-element.59), channel_id=1, source_target_pairs={{0,1},{1,2},{2,3},{4,5},{5,6},{6,7},{8,9},{9,10},{10,11},{12,13},{... | collective-permute-start | bytes 728 | tf_op jit(solution)/shard_map/ppermute | solution.py:19
  277.9 7.1 %collective-permute-start.71 = (f32[6,10,1]{2,1,0:T(8,128)S(1)}, f32[6,10,1]{2,1,0:T(8,128)S(1)}, u32[]{:S(2)}, u32[]{:S(2)}) collective-permute-start(f32[6,10,1]{2,1,0:T(8,128)S(1)} %get-tuple-element.57), channel_id=1, source_target_pairs={{0,1},{1,2},{2,3},{4,5},{5,6},{6,7},{8,9},{9,10},{10,11},{12,13},{... | collective-permute-start | bytes 728 | tf_op jit(solution)/shard_map/ppermute | solution.py:19
  300.0 7.1 %collective-permute-start.77 = (f32[6,10,1]{2,1,0:T(8,128)S(1)}, f32[6,10,1]{2,1,0:T(8,128)S(1)}, u32[]{:S(2)}, u32[]{:S(2)}) collective-permute-start(f32[6,10,1]{2,1,0:T(8,128)S(1)} %get-tuple-element.55), channel_id=1, source_target_pairs={{0,1},{1,2},{2,3},{4,5},{5,6},{6,7},{8,9},{9,10},{10,11},{12,13},{... | collective-permute-start | bytes 728 | tf_op jit(solution)/shard_map/ppermute | solution.py:19
  322.2 7.1 %collective-permute-start.83 = (f32[6,10,1]{2,1,0:T(8,128)S(1)}, f32[6,10,1]{2,1,0:T(8,128)S(1)}, u32[]{:S(2)}, u32[]{:S(2)}) collective-permute-start(f32[6,10,1]{2,1,0:T(8,128)S(1)} %get-tuple-element.53), channel_id=1, source_target_pairs={{0,1},{1,2},{2,3},{4,5},{5,6},{6,7},{8,9},{9,10},{10,11},{12,13},{... | collective-permute-start | bytes 728 | tf_op jit(solution)/shard_map/ppermute | solution.py:19
  333.3 4.0 %reshape.85 = f32[8,16,128]{2,1,0:T(8,128)S(1)} reshape(f32[4,2,8,2,64,2]{5,4,3,2,1,0:T(8,128)} %broadcast_in_dim.48) | data formatting | bytes 131072 | tf_op jit(solution)/shard_map/reshape | solution.py:73
  350.0 7.1 %collective-permute-start.88 = (f32[16,24,4]{2,1,0:T(8,128)S(1)}, f32[16,24,4]{2,1,0:T(8,128)S(1)}, u32[]{:S(2)}, u32[]{:S(2)}) collective-permute-start(f32[16,24,4]{2,1,0:T(8,128)S(1)} %get-tuple-element.38), channel_id=1, source_target_pairs={{0,1},{1,2},{2,3},{4,5},{5,6},{6,7},{8,9},{9,10},{10,11},{12,13},{... | collective-permute-start | bytes 18440 | tf_op jit(solution)/shard_map/ppermute | solution.py:19
  359.7 4.4 %collective-permute-done.89 = f32[16,24,4]{2,1,0:T(8,128)S(1)} collective-permute-done((f32[16,24,4]{2,1,0:T(8,128)S(1)}, f32[16,24,4]{2,1,0:T(8,128)S(1)}, u32[]{:S(2)}, u32[]{:S(2)}) %collective-permute-start.89) | collective-permute-done | bytes 6176 | tf_op jit(solution)/shard_map/ppermute | solution.py:22
  383.1 4.6 %collective-permute-start.95 = (f32[10,18,1]{2,1,0:T(8,128)S(1)}, f32[10,18,1]{2,1,0:T(8,128)S(1)}, u32[]{:S(2)}, u32[]{:S(2)}) collective-permute-start(f32[10,18,1]{2,1,0:T(8,128)S(1)} %get-tuple-element.45), channel_id=1, source_target_pairs={{0,1},{1,2},{2,3},{4,5},{5,6},{6,7},{8,9},{9,10},{10,11},{12,13},{... | collective-permute-start | bytes 2168 | tf_op jit(solution)/shard_map/ppermute | solution.py:19
  (361 shorter events, 252.9 us)
Async XLA Ops:
  1.5 42.4 %collective-permute-start = (f32[2,5,16,128]{3,2,1,0:T(8,128)S(1)}, f32[2,5,16,128]{3,2,1,0:T(8,128)S(1)}, u32[]{:S(2)}, u32[]{:S(2)}) collective-permute-start(f32[2,5,16,128]{3,2,1,0:T(8,128)S(1)} %get-tuple-element.42), channel_id=1, source_target_pairs={{0,16},{1,17},{2,18},{3,19},{4,20},{5,21},{6,22},{7,23},{8,24},{9,... | collective-permute-start | bytes 245768 | tf_op jit(solution)/shard_map/ppermute | solution.py:19
  5.5 38.4 %collective-permute-start.1 = (f32[2,5,16,128]{3,2,1,0:T(8,128)S(1)}, f32[2,5,16,128]{3,2,1,0:T(8,128)S(1)}, u32[]{:S(2)}, u32[]{:S(2)}) collective-permute-start(f32[2,5,16,128]{3,2,1,0:T(8,128)S(1)} %get-tuple-element.43), channel_id=1, source_target_pairs={{16,0},{17,1},{18,2},{19,3},{20,4},{21,5},{22,6},{23,7},{24,8},{25... | collective-permute-start | bytes 245768 | tf_op jit(solution)/shard_map/ppermute | solution.py:22
  15.6 14.3 %collective-permute-start.7 = (f32[1,8,64]{2,1,0:T(8,128)S(1)}, f32[1,8,64]{2,1,0:T(8,128)S(1)}, u32[]{:S(2)}, u32[]{:S(2)}) collective-permute-start(f32[1,8,64]{2,1,0:T(8,128)S(1)} %get-tuple-element.112), channel_id=1, source_target_pairs={{0,16},{1,17},{2,18},{3,19},{4,20},{5,21},{6,22},{7,23},{8,24},{9,... | collective-permute-start | bytes 6152 | tf_op jit(solution)/shard_map/ppermute | solution.py:19
  26.1 55.5 %collective-permute-start.39 = (f32[4,1,32]{2,1,0:T(1,128)S(1)}, f32[4,1,32]{2,1,0:T(1,128)S(1)}, u32[]{:S(2)}, u32[]{:S(2)}) collective-permute-start(f32[4,1,32]{2,1,0:T(1,128)S(1)} %get-tuple-element.120), channel_id=1, source_target_pairs={{0,4},{4,8},{8,12},{1,5},{5,9},{9,13},{2,6},{6,10},{10,14},{3,7},{... | collective-permute-start | bytes 1544 | tf_op jit(solution)/shard_map/ppermute | solution.py:19
  34.5 47.2 %collective-permute-start.38 = (f32[4,1,32]{2,1,0:T(1,128)S(1)}, f32[4,1,32]{2,1,0:T(1,128)S(1)}, u32[]{:S(2)}, u32[]{:S(2)}) collective-permute-start(f32[4,1,32]{2,1,0:T(1,128)S(1)} %get-tuple-element.121), channel_id=1, source_target_pairs={{4,0},{8,4},{12,8},{5,1},{9,5},{13,9},{6,2},{10,6},{14,10},{7,3},{... | collective-permute-start | bytes 1544 | tf_op jit(solution)/shard_map/ppermute | solution.py:22
  37.6 20.7 %collective-permute-start.10 = (f32[6,10,1]{2,1,0:T(8,128)S(1)}, f32[6,10,1]{2,1,0:T(8,128)S(1)}, u32[]{:S(2)}, u32[]{:S(2)}) collective-permute-start(f32[6,10,1]{2,1,0:T(8,128)S(1)} %get-tuple-element.68), channel_id=1, source_target_pairs={{1,0},{2,1},{3,2},{5,4},{6,5},{7,6},{9,8},{10,9},{11,10},{13,12},{... | collective-permute-start | bytes 728 | tf_op jit(solution)/shard_map/ppermute | solution.py:22
  50.7 10.8 %collective-permute-start.11 = (f32[6,10,1]{2,1,0:T(8,128)S(1)}, f32[6,10,1]{2,1,0:T(8,128)S(1)}, u32[]{:S(2)}, u32[]{:S(2)}) collective-permute-start(f32[6,10,1]{2,1,0:T(8,128)S(1)} %get-tuple-element.69), channel_id=1, source_target_pairs={{0,1},{1,2},{2,3},{4,5},{5,6},{6,7},{8,9},{9,10},{10,11},{12,13},{... | collective-permute-start | bytes 728 | tf_op jit(solution)/shard_map/ppermute | solution.py:19
  92.7 9.1 %collective-permute-start.16 = (f32[6,10,1]{2,1,0:T(8,128)S(1)}, f32[6,10,1]{2,1,0:T(8,128)S(1)}, u32[]{:S(2)}, u32[]{:S(2)}) collective-permute-start(f32[6,10,1]{2,1,0:T(8,128)S(1)} %get-tuple-element.66), channel_id=1, source_target_pairs={{1,0},{2,1},{3,2},{5,4},{6,5},{7,6},{9,8},{10,9},{11,10},{13,12},{... | collective-permute-start | bytes 728 | tf_op jit(solution)/shard_map/ppermute | solution.py:22
  103.1 9.2 %collective-permute-start.19 = (f32[1,8,64]{2,1,0:T(8,128)S(1)}, f32[1,8,64]{2,1,0:T(8,128)S(1)}, u32[]{:S(2)}, u32[]{:S(2)}) collective-permute-start(f32[1,8,64]{2,1,0:T(8,128)S(1)} %get-tuple-element.108), channel_id=1, source_target_pairs={{0,16},{1,17},{2,18},{3,19},{4,20},{5,21},{6,22},{7,23},{8,24},{9,... | collective-permute-start | bytes 6152 | tf_op jit(solution)/shard_map/ppermute | solution.py:19
  105.9 49.9 %collective-permute-start.40 = (f32[4,6,1]{2,1,0:T(8,128)S(1)}, f32[4,6,1]{2,1,0:T(8,128)S(1)}, u32[]{:S(2)}, u32[]{:S(2)}) collective-permute-start(f32[4,6,1]{2,1,0:T(8,128)S(1)} %get-tuple-element.102), channel_id=1, source_target_pairs={{1,0},{2,1},{3,2},{5,4},{6,5},{7,6},{9,8},{10,9},{11,10},{13,12},{... | collective-permute-start | bytes 296 | tf_op jit(solution)/shard_map/ppermute | solution.py:22
  107.8 47.9 %collective-permute-start.41 = (f32[4,6,1]{2,1,0:T(8,128)S(1)}, f32[4,6,1]{2,1,0:T(8,128)S(1)}, u32[]{:S(2)}, u32[]{:S(2)}) collective-permute-start(f32[4,6,1]{2,1,0:T(8,128)S(1)} %get-tuple-element.103), channel_id=1, source_target_pairs={{0,1},{1,2},{2,3},{4,5},{5,6},{6,7},{8,9},{9,10},{10,11},{12,13},{... | collective-permute-start | bytes 296 | tf_op jit(solution)/shard_map/ppermute | solution.py:19
  142.7 9.1 %collective-permute-start.28 = (f32[6,10,1]{2,1,0:T(8,128)S(1)}, f32[6,10,1]{2,1,0:T(8,128)S(1)}, u32[]{:S(2)}, u32[]{:S(2)}) collective-permute-start(f32[6,10,1]{2,1,0:T(8,128)S(1)} %get-tuple-element.62), channel_id=1, source_target_pairs={{1,0},{2,1},{3,2},{5,4},{6,5},{7,6},{9,8},{10,9},{11,10},{13,12},{... | collective-permute-start | bytes 728 | tf_op jit(solution)/shard_map/ppermute | solution.py:22
  165.0 9.1 %collective-permute-start.34 = (f32[6,10,1]{2,1,0:T(8,128)S(1)}, f32[6,10,1]{2,1,0:T(8,128)S(1)}, u32[]{:S(2)}, u32[]{:S(2)}) collective-permute-start(f32[6,10,1]{2,1,0:T(8,128)S(1)} %get-tuple-element.60), channel_id=1, source_target_pairs={{1,0},{2,1},{3,2},{5,4},{6,5},{7,6},{9,8},{10,9},{11,10},{13,12},{... | collective-permute-start | bytes 728 | tf_op jit(solution)/shard_map/ppermute | solution.py:22
  166.9 8.3 %collective-permute-start.35 = (f32[6,10,1]{2,1,0:T(8,128)S(1)}, f32[6,10,1]{2,1,0:T(8,128)S(1)}, u32[]{:S(2)}, u32[]{:S(2)}) collective-permute-start(f32[6,10,1]{2,1,0:T(8,128)S(1)} %get-tuple-element.61), channel_id=1, source_target_pairs={{0,1},{1,2},{2,3},{4,5},{5,6},{6,7},{8,9},{9,10},{10,11},{12,13},{... | collective-permute-start | bytes 728 | tf_op jit(solution)/shard_map/ppermute | solution.py:19
  187.9 9.1 %collective-permute-start.46 = (f32[4,6,1]{2,1,0:T(8,128)S(1)}, f32[4,6,1]{2,1,0:T(8,128)S(1)}, u32[]{:S(2)}, u32[]{:S(2)}) collective-permute-start(f32[4,6,1]{2,1,0:T(8,128)S(1)} %get-tuple-element.100), channel_id=1, source_target_pairs={{1,0},{2,1},{3,2},{5,4},{6,5},{7,6},{9,8},{10,9},{11,10},{13,12},{... | collective-permute-start | bytes 296 | tf_op jit(solution)/shard_map/ppermute | solution.py:22
  209.7 9.2 %collective-permute-start.52 = (f32[4,6,1]{2,1,0:T(8,128)S(1)}, f32[4,6,1]{2,1,0:T(8,128)S(1)}, u32[]{:S(2)}, u32[]{:S(2)}) collective-permute-start(f32[4,6,1]{2,1,0:T(8,128)S(1)} %get-tuple-element.98), channel_id=1, source_target_pairs={{1,0},{2,1},{3,2},{5,4},{6,5},{7,6},{9,8},{10,9},{11,10},{13,12},{... | collective-permute-start | bytes 296 | tf_op jit(solution)/shard_map/ppermute | solution.py:22
  231.5 9.0 %collective-permute-start.58 = (f32[4,6,1]{2,1,0:T(8,128)S(1)}, f32[4,6,1]{2,1,0:T(8,128)S(1)}, u32[]{:S(2)}, u32[]{:S(2)}) collective-permute-start(f32[4,6,1]{2,1,0:T(8,128)S(1)} %get-tuple-element.96), channel_id=1, source_target_pairs={{1,0},{2,1},{3,2},{5,4},{6,5},{7,6},{9,8},{10,9},{11,10},{13,12},{... | collective-permute-start | bytes 296 | tf_op jit(solution)/shard_map/ppermute | solution.py:22
  253.8 9.0 %collective-permute-start.64 = (f32[6,10,1]{2,1,0:T(8,128)S(1)}, f32[6,10,1]{2,1,0:T(8,128)S(1)}, u32[]{:S(2)}, u32[]{:S(2)}) collective-permute-start(f32[6,10,1]{2,1,0:T(8,128)S(1)} %get-tuple-element.58), channel_id=1, source_target_pairs={{1,0},{2,1},{3,2},{5,4},{6,5},{7,6},{9,8},{10,9},{11,10},{13,12},{... | collective-permute-start | bytes 728 | tf_op jit(solution)/shard_map/ppermute | solution.py:22
  275.9 9.1 %collective-permute-start.70 = (f32[6,10,1]{2,1,0:T(8,128)S(1)}, f32[6,10,1]{2,1,0:T(8,128)S(1)}, u32[]{:S(2)}, u32[]{:S(2)}) collective-permute-start(f32[6,10,1]{2,1,0:T(8,128)S(1)} %get-tuple-element.56), channel_id=1, source_target_pairs={{1,0},{2,1},{3,2},{5,4},{6,5},{7,6},{9,8},{10,9},{11,10},{13,12},{... | collective-permute-start | bytes 728 | tf_op jit(solution)/shard_map/ppermute | solution.py:22
  277.9 8.3 %collective-permute-start.71 = (f32[6,10,1]{2,1,0:T(8,128)S(1)}, f32[6,10,1]{2,1,0:T(8,128)S(1)}, u32[]{:S(2)}, u32[]{:S(2)}) collective-permute-start(f32[6,10,1]{2,1,0:T(8,128)S(1)} %get-tuple-element.57), channel_id=1, source_target_pairs={{0,1},{1,2},{2,3},{4,5},{5,6},{6,7},{8,9},{9,10},{10,11},{12,13},{... | collective-permute-start | bytes 728 | tf_op jit(solution)/shard_map/ppermute | solution.py:19
  298.1 9.1 %collective-permute-start.76 = (f32[6,10,1]{2,1,0:T(8,128)S(1)}, f32[6,10,1]{2,1,0:T(8,128)S(1)}, u32[]{:S(2)}, u32[]{:S(2)}) collective-permute-start(f32[6,10,1]{2,1,0:T(8,128)S(1)} %get-tuple-element.54), channel_id=1, source_target_pairs={{1,0},{2,1},{3,2},{5,4},{6,5},{7,6},{9,8},{10,9},{11,10},{13,12},{... | collective-permute-start | bytes 728 | tf_op jit(solution)/shard_map/ppermute | solution.py:22
  300.0 8.3 %collective-permute-start.77 = (f32[6,10,1]{2,1,0:T(8,128)S(1)}, f32[6,10,1]{2,1,0:T(8,128)S(1)}, u32[]{:S(2)}, u32[]{:S(2)}) collective-permute-start(f32[6,10,1]{2,1,0:T(8,128)S(1)} %get-tuple-element.55), channel_id=1, source_target_pairs={{0,1},{1,2},{2,3},{4,5},{5,6},{6,7},{8,9},{9,10},{10,11},{12,13},{... | collective-permute-start | bytes 728 | tf_op jit(solution)/shard_map/ppermute | solution.py:19
  320.3 9.1 %collective-permute-start.82 = (f32[6,10,1]{2,1,0:T(8,128)S(1)}, f32[6,10,1]{2,1,0:T(8,128)S(1)}, u32[]{:S(2)}, u32[]{:S(2)}) collective-permute-start(f32[6,10,1]{2,1,0:T(8,128)S(1)} %get-tuple-element.52), channel_id=1, source_target_pairs={{1,0},{2,1},{3,2},{5,4},{6,5},{7,6},{9,8},{10,9},{11,10},{13,12},{... | collective-permute-start | bytes 728 | tf_op jit(solution)/shard_map/ppermute | solution.py:22
  350.0 9.7 %collective-permute-start.88 = (f32[16,24,4]{2,1,0:T(8,128)S(1)}, f32[16,24,4]{2,1,0:T(8,128)S(1)}, u32[]{:S(2)}, u32[]{:S(2)}) collective-permute-start(f32[16,24,4]{2,1,0:T(8,128)S(1)} %get-tuple-element.38), channel_id=1, source_target_pairs={{0,1},{1,2},{2,3},{4,5},{5,6},{6,7},{8,9},{9,10},{10,11},{12,13},{... | collective-permute-start | bytes 18440 | tf_op jit(solution)/shard_map/ppermute | solution.py:19
  (76 other events, 433.0 us)
where the time goes:
time: 393 us; the launch traced here: 390 us
  starting transfers between devices  241 us (61%)
  waiting for transfers between devices  101 us (26%)
  other arithmetic  23.1 us (6%)
  local copies, waits for them, and re-layouts  22.9 us (6%)
    ppermute x48, starting transfers between devices, extended(): lax.ppermute(lax.slice_in_dim(block, block.shape[dim] - width, None, axis...  162 us
    ppermute x48, waiting for transfers between devices, extended(): lax.ppermute(lax.slice_in_dim(block, 0, width, axis=dim), axis, backward)  84.7 us
    ppermute x48, starting transfers between devices, extended(): lax.ppermute(lax.slice_in_dim(block, 0, width, axis=dim), axis, backward)  79 us
    ppermute x48, waiting for transfers between devices, extended(): lax.ppermute(lax.slice_in_dim(block, block.shape[dim] - width, None, axis...  16.6 us
    reshape x3, local copies, waits for them, and re-layouts, restrict(): blocks = values.reshape(size_x // 2, 2, size_y // 2, 2, size_z // 2, 2)  12.4 us
  transfers between devices with their start and end apart: 96, of which 45 were waited for; matrix products, arithmetic and copies ran while one was open for 7% of the time, Pallas kernels for 0%

commit v1 on v0

--- a/solution.py
+++ b/solution.py
@@ -1,6 +1,8 @@
 import jax
 import jax.numpy as jnp
 from jax import lax
+from jax.experimental import pallas as pl
+from jax.experimental.pallas import tpu as pltpu
 from jax.sharding import PartitionSpec as P
 
 LEVELS = 3
@@ -206,9 +208,426 @@
     return (solution, residual)
 
 
+def smoothing_weights():
+    centre = 0.5 * (cheb_high + cheb_low)
+    half_width = 0.5 * (cheb_high - cheb_low)
+    sigma_val = centre / half_width
+    rho_now = 1.0 / sigma_val
+    weights = [(0.0, 1.0 / centre)]
+    for _ in range(DEGREE - 1):
+        rho_next = 1.0 / (2.0 * sigma_val - rho_now)
+        weights.append((rho_next * rho_now, 2.0 * rho_next / half_width))
+        rho_now = rho_next
+    return weights
+
+
+def turn(values, shift, axis):
+    return pltpu.roll(values, shift % values.shape[axis], axis)
+
+
+def set_faces(coef, face_x, face_y, face_z, inverse, count, scale):
+    half = 0.5 * scale
+
+    def body(i, below):
+        here = coef[i + 1]
+        above = half * (here + coef[i + 2])
+        along_y = half * (here + turn(here, -1, 0))
+        along_z = half * (here + turn(here, -1, 1))
+        face_x[i + 1] = above
+        face_y[i] = along_y
+        face_z[i] = along_z
+        diagonal = (below + above) + (along_y + turn(along_y, 1, 0)) + (along_z + turn(along_z, 1, 1))
+        inverse[i] = jnp.where(here > 0.0, 1.0 / jnp.where(here > 0.0, diagonal, 1.0), 0.0)
+        return above
+
+    first = half * coef[1]
+    face_x[0] = first
+    lax.fori_loop(0, count, body, first)
+
+
+def sweep_over(low, high, values, face_x, face_y, face_z, use):
+    def body(i, carry):
+        here, flux_low = carry
+        above = values[i + 2]
+        flux_high = face_x[i + 1] * (above - here)
+        flux_y = face_y[i] * (turn(here, -1, 0) - here)
+        flux_z = face_z[i] * (turn(here, -1, 1) - here)
+        applied = (flux_low - flux_high) + (turn(flux_y, 1, 0) - flux_y) + (turn(flux_z, 1, 1) - flux_z)
+        use(i, applied, here)
+        return above, flux_high
+
+    here = values[low + 1]
+    lax.fori_loop(low, high, body, (here, face_x[low] * (here - values[low])))
+
+
+def smooth_from_zero(count, right, values, update, inverse):
+    first = smoothing_weights()[0][1]
+
+    def body(i, carry):
+        step = right[i] * (inverse[i] * first)
+        update[i] = step
+        values[i + 1] = step
+        return carry
+
+    lax.fori_loop(0, count, body, 0)
+
+
+def smooth_sweep(low, high, weight, right, values, update, faces, inverse):
+    keep, gain = weight
+
+    def use(i, applied, here):
+        step = (right[i] - applied) * (inverse[i] * gain)
+        if keep:
+            step = keep * update[i] + step
+        update[i] = step
+        values[i + 1] = here + step
+
+    sweep_over(low, high, values, *faces, use)
+
+
+def exact_dot(left, right):
+    return jnp.dot(left, right, precision=lax.Precision.HIGHEST, preferred_element_type=jnp.float32)
+
+
+def pairing(rows, columns, weight, period, along_rows):
+    row = lax.broadcasted_iota(jnp.int32, (rows, columns), 0)
+    column = lax.broadcasted_iota(jnp.int32, (rows, columns), 1)
+    if along_rows:
+        hit = row // 2 == column % period
+    else:
+        hit = column // 2 == row
+    return jnp.where(hit, weight, 0.0).astype(jnp.float32)
+
+
+def pair_rows(ref, count):
+    return ref[pl.ds(0, count, stride=2), :] + ref[pl.ds(1, count, stride=2), :]
+
+
+def down_kernel(
+    pos, own, prev, nxt, sib, mid,
+    start_out, right_out, coef_out, pay_out, edge_out,
+    coef, right, face_x, face_y, face_z, inverse, values, update, sums0, sums1, coarse
+):
+    count_x, rows, lanes = right.shape
+    by = rows // 3
+    bz = lanes // 2
+    core, odd, _, _ = pos[0], pos[1], pos[2], pos[3]
+    from_sib = (lax.broadcasted_iota(jnp.int32, (rows, bz), 1) < bz // 2) == (core == 0)
+    zero = jnp.zeros((rows, lanes), jnp.float32)
+    coef[0] = zero
+    coef[count_x + 1] = zero
+    values[0] = zero
+    values[count_x + 1] = zero
+
+    def assemble(i, carry):
+        middle = mid[i]
+        for which in (0, 1):
+            main = jnp.concatenate([prev[which, i], own[which, i], nxt[which, i]], axis=0)
+            far = middle if which == 0 else turn(middle, bz // 2, 1)
+            side = jnp.where(from_sib, sib[which, i], far)
+            if which == 0:
+                right[i, :, :bz] = main
+                right[i, :, bz:] = side
+            else:
+                coef[i + 1, :, :bz] = main
+                coef[i + 1, :, bz:] = side
+        return carry
+
+    lax.fori_loop(0, count_x, assemble, 0)
+    set_faces(coef, face_x, face_y, face_z, inverse, count_x, 1.0)
+    faces = (face_x, face_y, face_z)
+    weights = smoothing_weights()
+    smooth_from_zero(count_x, right, values, update, inverse)
+    for weight in weights[1:]:
+        smooth_sweep(0, count_x, weight, right, values, update, faces, inverse)
+
+    def leftover(i, applied, here):
+        left = right[i] - applied
+        update[i] = left
+
+    sweep_over(0, count_x, values, *faces, leftover)
+
+    half = rows // 2
+    for j in range(count_x // 2):
+        for slot, pair in enumerate(
+            (update[2 * j] + update[2 * j + 1], coef[2 * j + 1] + coef[2 * j + 2])
+        ):
+            at = slot * (count_x // 2) + j
+            sums0[at * rows : (at + 1) * rows, :] = pair[:, :bz]
+            sums1[at * rows : (at + 1) * rows, :] = pair[:, bz:]
+    matrix = pairing(lanes, bz, 0.125, bz, True)
+    total = count_x * half
+    coarse[...] = exact_dot(pair_rows(sums0, total), matrix[:bz]) + exact_dot(
+        pair_rows(sums1, total), matrix[bz:]
+    )
+    edge = by // 4
+    for slot in (0, 1):
+        for j in range(count_x // 2):
+            at = (slot * (count_x // 2) + j) * half
+            block = coarse[at + edge : at + edge + by, :]
+            pay_out[slot, j] = block
+            edge_out[slot, j] = jnp.where(odd == 1, block[by // 2 :], block[: by // 2])
+
+    def copy_out(i, carry):
+        window = pl.ds(by // 2, 2 * by)
+        start_out[i] = values[i + 1, window, :]
+        right_out[i] = right[i, window, :]
+        coef_out[i] = coef[i + 1, window, :]
+        return carry
+
+    lax.fori_loop(0, count_x, copy_out, 0)
+
+
+def up_kernel(
+    pos, pay, far, near, start, right, coef_in,
+    solution_out, residual_out,
+    coef1, right1, fx1, fy1, fz1, inverse1, values1, update1,
+    coef2, right2, fx2, fy2, fz2, inverse2, values2, update2,
+    sums, wide0, wide1,
+    coef, face_x, face_y, face_z, inverse, values, update,
+):
+    count_x, rows, lanes = right.shape
+    by = rows // 2
+    bz = lanes // 2
+    n1, rows1, _ = right1.shape
+    n2, rows2, _ = right2.shape
+    odd, upper, at_x = pos[1], pos[2], pos[3]
+    weights = smoothing_weights()
+    zero1 = jnp.zeros((rows1, bz), jnp.float32)
+    zero2 = jnp.zeros((rows2, bz), jnp.float32)
+    zero = jnp.zeros((rows, lanes), jnp.float32)
+    for ref in (coef1, values1):
+        ref[0] = zero1
+        ref[n1 + 1] = zero1
+    for ref in (coef2, values2):
+        ref[0] = zero2
+        ref[n2 + 1] = zero2
+    for ref in (coef, values):
+        ref[0] = zero
+        ref[count_x + 1] = zero
+
+    blank = jnp.zeros((by // 2, bz), jnp.float32)
+    for j in range(n1):
+        for which in (0, 1):
+            mine, other, side = pay[which, j], far[which, j], near[which, j]
+            whole = jnp.concatenate(
+                [
+                    jnp.where(upper == 1, other, mine),
+                    jnp.where(upper == 1, mine, other),
+                    jnp.where(odd == 1, blank, side),
+                    jnp.where(odd == 1, side, blank),
+                ],
+                axis=0,
+            )
+            if which == 0:
+                right1[j] = whole
+            else:
+                coef1[j + 1] = whole
+
+    faces1 = (fx1, fy1, fz1)
+    set_faces(coef1, fx1, fy1, fz1, inverse1, n1, 0.25)
+    smooth_from_zero(n1, right1, values1, update1, inverse1)
+    for weight in weights[1:]:
+        smooth_sweep(0, n1, weight, right1, values1, update1, faces1, inverse1)
+
+    def leftover1(i, applied, here):
+        update1[i] = right1[i] - applied
+
+    sweep_over(0, n1, values1, *faces1, leftover1)
+    for j in range(n2):
+        for slot, pair in enumerate(
+            (update1[2 * j] + update1[2 * j + 1], coef1[2 * j + 1] + coef1[2 * j + 2])
+        ):
+            at = slot * n2 + j
+            sums[at * rows1 : (at + 1) * rows1, :] = pair
+    lower = exact_dot(pair_rows(sums, n1 * rows2), pairing(bz, bz, 0.125, bz // 2, True))
+    for j in range(n2):
+        right2[j] = lower[j * rows2 : (j + 1) * rows2]
+        coef2[j + 1] = lower[(n2 + j) * rows2 : (n2 + j + 1) * rows2]
+
+    faces2 = (fx2, fy2, fz2)
+    set_faces(coef2, fx2, fy2, fz2, inverse2, n2, 0.0625)
+    smooth_from_zero(n2, right2, values2, update2, inverse2)
+    for weight in weights[1:]:
+        smooth_sweep(0, n2, weight, right2, values2, update2, faces2, inverse2)
+
+    stacked = jnp.concatenate([values2[j + 1] for j in range(n2)], axis=0)
+    spread = exact_dot(stacked, pairing(bz, bz, 1.0, bz, False))
+    sums[pl.ds(0, n2 * rows2, stride=2), :] = spread
+    sums[pl.ds(1, n2 * rows2, stride=2), :] = spread
+    for j in range(n1):
+        values1[j + 1] = values1[j + 1] + sums[(j // 2) * rows1 : (j // 2 + 1) * rows1, :]
+    for weight in weights:
+        smooth_sweep(0, n1, weight, right1, values1, update1, faces1, inverse1)
+
+    def copy_in(i, carry):
+        coef[i + 1] = coef_in[i]
+        return carry
+
+    lax.fori_loop(0, count_x, copy_in, 0)
+    faces = (face_x, face_y, face_z)
+    set_faces(coef, face_x, face_y, face_z, inverse, count_x, 1.0)
+    stacked = jnp.concatenate(
+        [
+            jnp.where(upper == 1, values1[j + 1, by : 2 * by, :], values1[j + 1, :by, :])
+            for j in range(n1)
+        ],
+        axis=0,
+    )
+    matrix = pairing(bz, lanes, 1.0, bz, False)
+    spread0 = exact_dot(stacked, matrix[:, :bz])
+    spread1 = exact_dot(stacked, matrix[:, bz:])
+    for wide, spread in ((wide0, spread0), (wide1, spread1)):
+        wide[pl.ds(0, n1 * by, stride=2), :] = spread
+        wide[pl.ds(1, n1 * by, stride=2), :] = spread
+    for j in range(n1):
+        part = slice(j * rows, (j + 1) * rows)
+        for i in (2 * j, 2 * j + 1):
+            values[i + 1, :, :bz] = start[i, :, :bz] + wide0[part, :]
+            values[i + 1, :, bz:] = start[i, :, bz:] + wide1[part, :]
+    bx = count_x // 2
+    for number, weight in enumerate(weights):
+        reach = DEGREE - number
+        low = jnp.where(at_x == 0, 0, bx - reach)
+        high = jnp.where(at_x == 0, bx + reach, count_x)
+        smooth_sweep(low, high, weight, right, values, update, faces, inverse)
+
+    inner = slice(by // 2, by // 2 + by)
+    base = at_x * bx
+
+    def finish(i, applied, here):
+        left = right[i] - applied
+        solution_out[i - base] = here[inner, :bz]
+        residual_out[i - base] = left[inner, :bz]
+
+    sweep_over(base, base + bx, values, *faces, finish)
+
+
+def vmem(*shape):
+    return pltpu.VMEM(shape, jnp.float32)
+
+
+def per_device_two_rounds(right_side, coefficient):
+    bx, by, bz = right_side.shape
+    at_x, at_y, at_z = (lax.axis_index(name) for name in ("gx", "gy", "gz"))
+    core = at_z % 2
+    pos = jnp.stack([core, at_y % 2, at_y // 2, at_x]).astype(jnp.int32)
+    mine = jnp.stack([right_side, coefficient])
+    other = lax.ppermute(mine, "gx", [(0, 1), (1, 0)])
+    own = jnp.where(
+        at_x == 0,
+        jnp.concatenate([mine, other], axis=1),
+        jnp.concatenate([other, mine], axis=1),
+    )
+    count_y = lax.axis_size("gy")
+    forward = [(i, i + 1) for i in range(count_y - 1)]
+    prev = lax.ppermute(own, "gy", forward)
+    nxt = lax.ppermute(own, "gy", [(b, a) for a, b in forward])
+    tall = jnp.concatenate([prev, own, nxt], axis=2)
+    half = bz // 2
+    packed = jnp.where(
+        core == 0,
+        jnp.concatenate([tall[0, :, :, :half], tall[1, :, :, :half]], axis=2),
+        jnp.concatenate([tall[1, :, :, half:], tall[0, :, :, half:]], axis=2),
+    )
+    mid = lax.ppermute(packed, "gz", [(1, 2), (2, 1)])
+    sib = lax.ppermute(tall, "gz", [(0, 1), (1, 0), (2, 3), (3, 2)])
+    nx = 2 * bx
+    rows = 3 * by
+    lanes = 2 * bz
+    in_smem = pl.BlockSpec(memory_space=pltpu.SMEM)
+    in_vmem = pl.BlockSpec(memory_space=pltpu.VMEM)
+    window = jax.ShapeDtypeStruct((nx, 2 * by, lanes), jnp.float32)
+    start, right_wide, coef_wide, pay, edge = pl.pallas_call(
+        down_kernel,
+        out_shape=(
+            window,
+            window,
+            window,
+            jax.ShapeDtypeStruct((2, bx, by, bz), jnp.float32),
+            jax.ShapeDtypeStruct((2, bx, by // 2, bz), jnp.float32),
+        ),
+        in_specs=[in_smem] + [in_vmem] * 5,
+        out_specs=(in_vmem,) * 5,
+        scratch_shapes=[
+            vmem(nx + 2, rows, lanes),
+            vmem(nx, rows, lanes),
+            vmem(nx + 1, rows, lanes),
+            vmem(nx, rows, lanes),
+            vmem(nx, rows, lanes),
+            vmem(nx, rows, lanes),
+            vmem(nx + 2, rows, lanes),
+            vmem(nx, rows, lanes),
+            vmem(nx * rows, bz),
+            vmem(nx * rows, bz),
+            vmem(nx * rows // 2, bz),
+        ],
+        compiler_params=pltpu.CompilerParams(vmem_limit_bytes=40 * 2**20),
+        name="down",
+    )(pos, own, prev, nxt, sib, mid)
+    far = lax.ppermute(pay, "gy", [(0, 2), (2, 0), (1, 3), (3, 1)])
+    near = lax.ppermute(edge, "gy", [(0, 1), (3, 2)])
+
+    def level_scratch(n, r, l, with_right):
+        return [
+            vmem(n + 2, r, l),
+            *([vmem(n, r, l)] if with_right else []),
+            vmem(n + 1, r, l),
+            vmem(n, r, l),
+            vmem(n, r, l),
+            vmem(n, r, l),
+            vmem(n + 2, r, l),
+            vmem(n, r, l),
+        ]
+
+    return pl.pallas_call(
+        up_kernel,
+        out_shape=(jax.ShapeDtypeStruct((bx, by, bz), jnp.float32),) * 2,
+        in_specs=[in_smem] + [in_vmem] * 6,
+        out_specs=(in_vmem,) * 2,
+        scratch_shapes=[
+            *level_scratch(bx, rows, bz, True),
+            *level_scratch(bx // 2, rows // 2, bz, True),
+            vmem(bx * rows, bz),
+            vmem(bx * 2 * by, bz),
+            vmem(bx * 2 * by, bz),
+            *level_scratch(nx, 2 * by, lanes, False),
+        ],
+        compiler_params=pltpu.CompilerParams(vmem_limit_bytes=40 * 2**20),
+        name="up",
+    )(pos, pay, far, near, start, right_wide, coef_wide)
+
+
+def two_rounds_fit(mesh, shape):
+    counts = tuple(mesh.shape[name] for name in ("gx", "gy", "gz"))
+    bx, by, bz = (size // count for size, count in zip(shape, counts))
+    edge = by // 4
+    reach_coarse = 4 * DEGREE + 2
+    return (
+        counts == (2, 4, 4)
+        and LEVELS == 3
+        and bx % 4 == 0
+        and by % 16 == 0
+        and bz % 128 == 0
+        and bz == 128
+        and 2 * edge + DEGREE + 1 <= by
+        and by // 2 + reach_coarse <= 2 * by - edge
+        and 2 * reach_coarse + DEGREE + 1 <= bz // 2
+    )
+
+
 def solution(mesh):
     in_specs = (P("gx", "gy", "gz"), P("gx", "gy", "gz"))
     out_specs = (P("gx", "gy", "gz"), P("gx", "gy", "gz"))
-    return jax.shard_map(
-        per_device, mesh=mesh, in_specs=in_specs, out_specs=out_specs, check_vma=False
-    )
+
+    def whole(right_side, coefficient):
+        fits = two_rounds_fit(mesh, right_side.shape)
+        return jax.shard_map(
+            per_device_two_rounds if fits else per_device,
+            mesh=mesh,
+            in_specs=in_specs,
+            out_specs=out_specs,
+            check_vma=False,
+        )(right_side, coefficient)
+
+    return whole

time: 393 us -> 78.8 us (0.20)
  starting transfers between devices: 241 us -> 16.1 us
  waiting for transfers between devices: 101 us -> 18.3 us
  Pallas kernels: 0 us -> 41.9 us
  local copies, waits for them, and re-layouts: 22.9 us -> 0.28 us
  other arithmetic: 23.1 us -> 1.34 us
    ppermute x96 -> x7, starting transfers between devices: 241 us -> 16.1 us  [the longest x1 3.15 us: per_device_two_rounds(): prev = lax.ppermute(own, 'gy', forward)]
    ppermute x96 -> x7, waiting for transfers between devices: 101 us -> 18.3 us  [the longest x1 5.94 us: per_device_two_rounds(): mid = lax.ppermute(packed, 'gz', [(1, 2), (2, 1)])]
    pallas_call x0 -> x2, Pallas kernels: none -> 41.9 us  [the longest x1 25.9 us: per_device_two_rounds(): pl.pallas_call(up_kernel, out_shape=(jax.ShapeDtypeStruct((bx, by, bz), j...]
    reshape x5 -> x0, local copies, waits for them, and re-layouts: 16.6 us -> none  [the longest x3 12.4 us: restrict(): blocks = values.reshape(size_x // 2, 2, size_y // 2, 2, size_z // 2, 2)]
    mul x69 -> x0, other arithmetic: 9.4 us -> none  [the longest x20 2.91 us: apply_padded(): flux_z = face_z * (padded[1:-1, 1:-1, 1:] - padded[1:-1, 1:-1, :-1])]
    reduce_sum x4 -> x0, other arithmetic: 5.34 us -> none  [restrict(): return jnp.mean(blocks, axis=(1, 3, 5))]
    add x19 -> x0, other arithmetic: 4.4 us -> none  [the longest x6 2.91 us: deep_smooth(): iterate = trim_cells(iterate, 1) + update]
  transfers between devices with their start and end apart: 96 -> 7, of which waited for: 45 -> 6; matrix products, arithmetic and copies ran while one was open for 7% -> 1% of each run, Pallas kernels for 0% -> 0%
where the time goes in v1:
time: 78.8 us; the launch traced here: 78.5 us
  Pallas kernels  41.9 us (53%)
  waiting for transfers between devices  18.3 us (23%)
  starting transfers between devices  16.1 us (20%)
  other arithmetic  1.34 us (2%)
    pallas_call x1, Pallas kernels, per_device_two_rounds(): pl.pallas_call(up_kernel, out_shape=(jax.ShapeDtypeStruct((bx, by, bz), j...  25.9 us
    pallas_call x1, Pallas kernels, per_device_two_rounds(): pl.pallas_call(down_kernel, out_shape=(window, window, window, jax.ShapeD...  16 us
    ppermute x1, waiting for transfers between devices, per_device_two_rounds(): mid = lax.ppermute(packed, 'gz', [(1, 2), (2, 1)])  5.94 us
    ppermute x1, waiting for transfers between devices, per_device_two_rounds(): nxt = lax.ppermute(own, 'gy', [(b, a) for a, b in forward])  3.85 us
    ppermute x1, waiting for transfers between devices, per_device_two_rounds(): other = lax.ppermute(mine, 'gx', [(0, 1), (1, 0)])  3.22 us
    ppermute x1, starting transfers between devices, per_device_two_rounds(): prev = lax.ppermute(own, 'gy', forward)  3.15 us
    ppermute x1, starting transfers between devices, per_device_two_rounds(): mid = lax.ppermute(packed, 'gz', [(1, 2), (2, 1)])  3.05 us
    ppermute x1, starting transfers between devices, per_device_two_rounds(): sib = lax.ppermute(tall, 'gz', [(0, 1), (1, 0), (2, 3), (3, 2)])  2.81 us
  transfers between devices with their start and end apart: 7, of which 6 were waited for; matrix products, arithmetic and copies ran while one was open for 1% of the time, Pallas kernels for 0%

profile of v1, /device:TPU:1, one launch (start us, length us, event | category | flops | bytes accessed | tf_op | source)
XLA Modules:
  0.0 78.5 jit_solution(14969151784128820544)
XLA Ops:
  0.6 0.0 copy-start
  0.6 0.0 copy-start.1
  0.6 0.9 %pad_maximum_fusion.1 = f32[2,8,16,128]{3,2,1,0:T(8,128)S(1)} fusion(f32[1,8,16,128]{3,2,1,0:T(8,128)} %bitcast.14, f32[1,8,16,128]{3,2,1,0:T(8,128)} %bitcast.16), kind=kLoop, calls=%fused_computation.7 | loop fusion | flops 32768 | bytes 262144 | tf_op jit(solution)/shard_map/stack | solution.py:515
  1.6 2.1 %collective-permute-start = (f32[2,8,16,128]{3,2,1,0:T(8,128)S(1)}, f32[2,8,16,128]{3,2,1,0:T(8,128)S(1)}, u32[]{:S(2)}, u32[]{:S(2)}) collective-permute-start(f32[2,8,16,128]{3,2,1,0:T(8,128)S(1)} %pad_maximum_fusion.1), channel_id=1, source_target_pairs={{0,16},{16,0},{1,17},{17,1},{2,18},{18,2},{3,19},{19,3},{4,20},{20... | collective-permute-start | bytes 393224 | tf_op jit(solution)/shard_map/ppermute | solution.py:516
  3.7 3.2 %collective-permute-done = f32[2,8,16,128]{3,2,1,0:T(8,128)S(1)} collective-permute-done((f32[2,8,16,128]{3,2,1,0:T(8,128)S(1)}, f32[2,8,16,128]{3,2,1,0:T(8,128)S(1)}, u32[]{:S(2)}, u32[]{:S(2)}) %collective-permute-start) | collective-permute-done | bytes 131104 | tf_op jit(solution)/shard_map/ppermute | solution.py:516
  6.9 0.0 copy-done
  6.9 3.1 %collective-permute-start.1 = (f32[2,16,16,128]{3,2,1,0:T(8,128)S(1)}, f32[2,16,16,128]{3,2,1,0:T(8,128)S(1)}, u32[]{:S(2)}, u32[]{:S(2)}) collective-permute-start(f32[2,16,16,128]{3,2,1,0:T(8,128)S(1)} %maximum_select_fusion.1.own), channel_id=1, source_target_pairs={{0,4},{4,8},{8,12},{1,5},{5,9},{9,13},{2,6},{6,10},{10,14},{3,7},{... | collective-permute-start | bytes 786440 | tf_op jit(solution)/shard_map/ppermute | solution.py:524
  10.1 1.3 %collective-permute-start.2 = (f32[2,16,16,128]{3,2,1,0:T(8,128)S(1)}, f32[2,16,16,128]{3,2,1,0:T(8,128)S(1)}, u32[]{:S(2)}, u32[]{:S(2)}) collective-permute-start(f32[2,16,16,128]{3,2,1,0:T(8,128)S(1)} %maximum_select_fusion.1.own), channel_id=1, source_target_pairs={{4,0},{8,4},{12,8},{5,1},{9,5},{13,9},{6,2},{10,6},{14,10},{7,3},{... | collective-permute-start | bytes 786440 | tf_op jit(solution)/shard_map/ppermute | solution.py:525
  11.4 2.7 %collective-permute-done.1.prev = f32[2,16,16,128]{3,2,1,0:T(8,128)S(1)} collective-permute-done((f32[2,16,16,128]{3,2,1,0:T(8,128)S(1)}, f32[2,16,16,128]{3,2,1,0:T(8,128)S(1)}, u32[]{:S(2)}, u32[]{:S(2)}) %collective-permute-start.1) | collective-permute-done | bytes 262176 | tf_op jit(solution)/shard_map/ppermute | solution.py:524
  14.1 3.8 %collective-permute-done.2.nxt = f32[2,16,16,128]{3,2,1,0:T(8,128)S(1)} collective-permute-done((f32[2,16,16,128]{3,2,1,0:T(8,128)S(1)}, f32[2,16,16,128]{3,2,1,0:T(8,128)S(1)}, u32[]{:S(2)}, u32[]{:S(2)}) %collective-permute-start.2) | collective-permute-done | bytes 262176 | tf_op jit(solution)/shard_map/ppermute | solution.py:525
  18.0 0.1 pad_maximum_fusion
  18.0 2.8 %collective-permute-start.3 = (f32[2,16,48,128]{3,2,1,0:T(8,128)S(1)}, f32[2,16,48,128]{3,2,1,0:T(8,128)S(1)}, u32[]{:S(2)}, u32[]{:S(2)}) collective-permute-start(f32[2,16,48,128]{3,2,1,0:T(8,128)S(1)} %pad_maximum_fusion), channel_id=1, source_target_pairs={{0,1},{1,0},{2,3},{3,2},{4,5},{5,4},{6,7},{7,6},{8,9},{9,8},{10,11... | collective-permute-start | bytes 2359304 | tf_op jit(solution)/shard_map/ppermute | solution.py:534
  20.8 0.3 slice_bitcast_fusion.1
  21.1 0.3 maximum_select_fusion
  21.4 3.0 %collective-permute-start.4 = (f32[16,48,128]{2,1,0:T(8,128)S(1)}, f32[16,48,128]{2,1,0:T(8,128)S(1)}, u32[]{:S(2)}, u32[]{:S(2)}) collective-permute-start(f32[16,48,128]{2,1,0:T(8,128)S(1)} %maximum_select_fusion), channel_id=1, source_target_pairs={{1,2},{2,1},{5,6},{6,5},{9,10},{10,9},{13,14},{14,13},{17,18},{18,... | collective-permute-start | bytes 1179656 | tf_op jit(solution)/shard_map/ppermute | solution.py:533
  24.4 0.1 pad_add_fusion.pos
  24.5 5.9 %collective-permute-done.4.mid = f32[16,48,128]{2,1,0:T(8,128)S(1)} collective-permute-done((f32[16,48,128]{2,1,0:T(8,128)S(1)}, f32[16,48,128]{2,1,0:T(8,128)S(1)}, u32[]{:S(2)}, u32[]{:S(2)}) %collective-permute-start.4) | collective-permute-done | bytes 393248 | tf_op jit(solution)/shard_map/ppermute | solution.py:533
  30.5 0.0 collective-permute-done.3.sib
  30.5 16.0 %down.1 = (f32[16,32,256]{2,1,0:T(8,128)S(1)}, f32[16,32,256]{2,1,0:T(8,128)S(1)}, f32[16,32,256]{2,1,0:T(8,128)S(1)}, f32[2,8,16,128]{3,2,1,0:T(8,128)S(1)}, f32[2,8,8,128]{3,2,1,0:T(8,128)S(1)}) custom-call(s32[4]{0:T(128)S(1)} %pad_add_fusion.pos, f32[2,16,16,128]{3,2,1,0:T(8,128)S(1)} %maximum_select_fusion.1.own, ...), custom_call_target="tpu_custom_call" | custom-call | tf_op jit(solution)/shard_map/down/pallas_call | solution.py:541
  46.5 2.4 %collective-permute-start.5 = (f32[2,8,16,128]{3,2,1,0:T(8,128)S(1)}, f32[2,8,16,128]{3,2,1,0:T(8,128)S(1)}, u32[]{:S(2)}, u32[]{:S(2)}) collective-permute-start(f32[2,8,16,128]{3,2,1,0:T(8,128)S(1)} %get-tuple-element.7.pay), channel_id=1, source_target_pairs={{0,8},{8,0},{4,12},{12,4},{1,9},{9,1},{5,13},{13,5},{2,10},{10,2},... | collective-permute-start | bytes 393224 | tf_op jit(solution)/shard_map/ppermute | solution.py:568
  48.8 1.3 %collective-permute-start.6 = (f32[2,8,8,128]{3,2,1,0:T(8,128)S(1)}, f32[2,8,8,128]{3,2,1,0:T(8,128)S(1)}, u32[]{:S(2)}, u32[]{:S(2)}) collective-permute-start(f32[2,8,8,128]{3,2,1,0:T(8,128)S(1)} %get-tuple-element.8), channel_id=1, source_target_pairs={{0,4},{12,8},{1,5},{13,9},{2,6},{14,10},{3,7},{15,11},{16,20},{28,... | collective-permute-start | bytes 196616 | tf_op jit(solution)/shard_map/ppermute | solution.py:569
  50.1 1.3 %collective-permute-done.6.near = f32[2,8,8,128]{3,2,1,0:T(8,128)S(1)} collective-permute-done((f32[2,8,8,128]{3,2,1,0:T(8,128)S(1)}, f32[2,8,8,128]{3,2,1,0:T(8,128)S(1)}, u32[]{:S(2)}, u32[]{:S(2)}) %collective-permute-start.6) | collective-permute-done | bytes 65568 | tf_op jit(solution)/shard_map/ppermute | solution.py:569
  51.4 1.2 %collective-permute-done.5.far = f32[2,8,16,128]{3,2,1,0:T(8,128)S(1)} collective-permute-done((f32[2,8,16,128]{3,2,1,0:T(8,128)S(1)}, f32[2,8,16,128]{3,2,1,0:T(8,128)S(1)}, u32[]{:S(2)}, u32[]{:S(2)}) %collective-permute-start.5) | collective-permute-done | bytes 131104 | tf_op jit(solution)/shard_map/ppermute | solution.py:568
  52.6 25.9 %up.1 = (f32[8,16,128]{2,1,0:T(8,128)}, f32[8,16,128]{2,1,0:T(8,128)}) custom-call(s32[4]{0:T(128)S(1)} %pad_add_fusion.pos, f32[2,8,16,128]{3,2,1,0:T(8,128)S(1)} %get-tuple-element.7.pay, f32[2,8,16,128]{3,2,1,0:T(8,128)S(1)} %collective-permute-done.5.far, f32[2,8,8,128]{3,2,1,0:T(8,128)S(1)} %collective-permute-done.6.near, ...), custom_call_target="tpu_custom_call" | custom-call | tf_op jit(solution)/shard_map/up/pallas_call | solution.py:583
  (2 shorter events, 0.0 us)
Async XLA Ops:
  0.6 6.3 %copy-start = (f32[8,16,128]{2,1,0:T(8,128)S(1)}, f32[8,16,128]{2,1,0:T(8,128)}, u32[]{:S(2)}) copy-start(f32[8,16,128]{2,1,0:T(8,128)} %param.3) | copy-start | bytes 196612
  0.6 6.3 %copy-start.1 = (f32[8,16,128]{2,1,0:T(8,128)S(1)}, f32[8,16,128]{2,1,0:T(8,128)}, u32[]{:S(2)}) copy-start(f32[8,16,128]{2,1,0:T(8,128)} %param.2) | copy-start | bytes 196612
  1.6 5.3 %collective-permute-start = (f32[2,8,16,128]{3,2,1,0:T(8,128)S(1)}, f32[2,8,16,128]{3,2,1,0:T(8,128)S(1)}, u32[]{:S(2)}, u32[]{:S(2)}) collective-permute-start(f32[2,8,16,128]{3,2,1,0:T(8,128)S(1)} %pad_maximum_fusion.1), channel_id=1, source_target_pairs={{0,16},{16,0},{1,17},{17,1},{2,18},{18,2},{3,19},{19,3},{4,20},{20... | collective-permute-start | bytes 393224 | tf_op jit(solution)/shard_map/ppermute | solution.py:516
  6.9 7.2 %collective-permute-start.1 = (f32[2,16,16,128]{3,2,1,0:T(8,128)S(1)}, f32[2,16,16,128]{3,2,1,0:T(8,128)S(1)}, u32[]{:S(2)}, u32[]{:S(2)}) collective-permute-start(f32[2,16,16,128]{3,2,1,0:T(8,128)S(1)} %maximum_select_fusion.1.own), channel_id=1, source_target_pairs={{0,4},{4,8},{8,12},{1,5},{5,9},{9,13},{2,6},{6,10},{10,14},{3,7},{... | collective-permute-start | bytes 786440 | tf_op jit(solution)/shard_map/ppermute | solution.py:524
  10.1 7.9 %collective-permute-start.2 = (f32[2,16,16,128]{3,2,1,0:T(8,128)S(1)}, f32[2,16,16,128]{3,2,1,0:T(8,128)S(1)}, u32[]{:S(2)}, u32[]{:S(2)}) collective-permute-start(f32[2,16,16,128]{3,2,1,0:T(8,128)S(1)} %maximum_select_fusion.1.own), channel_id=1, source_target_pairs={{4,0},{8,4},{12,8},{5,1},{9,5},{13,9},{6,2},{10,6},{14,10},{7,3},{... | collective-permute-start | bytes 786440 | tf_op jit(solution)/shard_map/ppermute | solution.py:525
  18.0 12.5 %collective-permute-start.3 = (f32[2,16,48,128]{3,2,1,0:T(8,128)S(1)}, f32[2,16,48,128]{3,2,1,0:T(8,128)S(1)}, u32[]{:S(2)}, u32[]{:S(2)}) collective-permute-start(f32[2,16,48,128]{3,2,1,0:T(8,128)S(1)} %pad_maximum_fusion), channel_id=1, source_target_pairs={{0,1},{1,0},{2,3},{3,2},{4,5},{5,4},{6,7},{7,6},{8,9},{9,8},{10,11... | collective-permute-start | bytes 2359304 | tf_op jit(solution)/shard_map/ppermute | solution.py:534
  21.4 9.1 %collective-permute-start.4 = (f32[16,48,128]{2,1,0:T(8,128)S(1)}, f32[16,48,128]{2,1,0:T(8,128)S(1)}, u32[]{:S(2)}, u32[]{:S(2)}) collective-permute-start(f32[16,48,128]{2,1,0:T(8,128)S(1)} %maximum_select_fusion), channel_id=1, source_target_pairs={{1,2},{2,1},{5,6},{6,5},{9,10},{10,9},{13,14},{14,13},{17,18},{18,... | collective-permute-start | bytes 1179656 | tf_op jit(solution)/shard_map/ppermute | solution.py:533
  46.5 6.2 %collective-permute-start.5 = (f32[2,8,16,128]{3,2,1,0:T(8,128)S(1)}, f32[2,8,16,128]{3,2,1,0:T(8,128)S(1)}, u32[]{:S(2)}, u32[]{:S(2)}) collective-permute-start(f32[2,8,16,128]{3,2,1,0:T(8,128)S(1)} %get-tuple-element.7.pay), channel_id=1, source_target_pairs={{0,8},{8,0},{4,12},{12,4},{1,9},{9,1},{5,13},{13,5},{2,10},{10,2},... | collective-permute-start | bytes 393224 | tf_op jit(solution)/shard_map/ppermute | solution.py:568
  48.8 2.6 %collective-permute-start.6 = (f32[2,8,8,128]{3,2,1,0:T(8,128)S(1)}, f32[2,8,8,128]{3,2,1,0:T(8,128)S(1)}, u32[]{:S(2)}, u32[]{:S(2)}) collective-permute-start(f32[2,8,8,128]{3,2,1,0:T(8,128)S(1)} %get-tuple-element.8), channel_id=1, source_target_pairs={{0,4},{12,8},{1,5},{13,9},{2,6},{14,10},{3,7},{15,11},{16,20},{28,... | collective-permute-start | bytes 196616 | tf_op jit(solution)/shard_map/ppermute | solution.py:569

commit v2 on v0

--- a/solution.py
+++ b/solution.py
@@ -1,6 +1,8 @@
 import jax
 import jax.numpy as jnp
 from jax import lax
+from jax.experimental import pallas as pl
+from jax.experimental.pallas import tpu as pltpu
 from jax.sharding import PartitionSpec as P
 
 LEVELS = 3
@@ -206,9 +208,518 @@
     return (solution, residual)
 
 
+UNROLL_FINE = 4
+UNROLL_COARSE = 16
+
+
+def smoothing_weights():
+    centre = 0.5 * (cheb_high + cheb_low)
+    half_width = 0.5 * (cheb_high - cheb_low)
+    sigma_val = centre / half_width
+    rho_now = 1.0 / sigma_val
+    weights = [(0.0, 1.0 / centre)]
+    for _ in range(DEGREE - 1):
+        rho_next = 1.0 / (2.0 * sigma_val - rho_now)
+        weights.append((rho_next * rho_now, 2.0 * rho_next / half_width))
+        rho_now = rho_next
+    return weights
+
+
+def turn(values, shift, axis):
+    return pltpu.roll(values, shift % values.shape[axis], axis)
+
+
+def run(low, count, body, carry, unroll):
+    unroll = min(unroll, count)
+
+    def several(step, state):
+        for k in range(unroll):
+            state = body(low + step * unroll + k, state)
+        return state
+
+    if count // unroll == 1:
+        carry = several(0, carry)
+    else:
+        carry = lax.fori_loop(0, count // unroll, several, carry)
+    for k in range(count // unroll * unroll, count):
+        carry = body(low + k, carry)
+    return carry
+
+
+class Level:
+    def __init__(self, refs, split_y, split_z, step, scale, unroll):
+        self.coef, self.right, self.face_x, self.face_y, self.face_z, self.inverse, self.values, self.update = refs
+        self.count = self.face_y.shape[1]
+        self.parts = self.face_y.shape[0]
+        self.split_y, self.split_z, self.step = split_y, split_z, step
+        self.half, self.unroll = 0.5 * scale, unroll
+        self.pairs_z = 2 if split_z else 1
+
+    def read(self, ref, i):
+        return [ref[part, i] for part in range(self.parts)]
+
+    def write(self, ref, i, values):
+        for part in range(self.parts):
+            ref[part, i] = values[part]
+
+    def clear_ends(self):
+        zero = jnp.zeros(self.coef.shape[2:], jnp.float32)
+        for part in range(self.parts):
+            for ref in (self.coef, self.values):
+                ref[part, 0] = zero
+                ref[part, self.count + 1] = zero
+
+    def next_y(self, v, part):
+        if not self.split_y:
+            return turn(v[part], -1, 0)
+        if part < self.pairs_z:
+            return v[part + self.pairs_z]
+        return turn(v[part - self.pairs_z], -1, 0)
+
+    def last_y(self, v, part):
+        if not self.split_y:
+            return turn(v[part], 1, 0)
+        if part < self.pairs_z:
+            return turn(v[part + self.pairs_z], 1, 0)
+        return v[part - self.pairs_z]
+
+    def next_z(self, v, part):
+        if not self.split_z:
+            return turn(v[part], -self.step, 1)
+        if part % 2 == 0:
+            return v[part + 1]
+        return turn(v[part - 1], -1, 1)
+
+    def last_z(self, v, part):
+        if not self.split_z:
+            return turn(v[part], self.step, 1)
+        if part % 2 == 0:
+            return turn(v[part + 1], 1, 1)
+        return v[part - 1]
+
+    def set_faces(self, use):
+        half = self.half
+        parts = range(self.parts)
+
+        def body(i, carry):
+            here, below = carry
+            above = self.read(self.coef, i + 2)
+            upper = [half * (here[p] + above[p]) for p in parts]
+            along_y = [half * (here[p] + self.next_y(here, p)) for p in parts]
+            along_z = [half * (here[p] + self.next_z(here, p)) for p in parts]
+            inverse = []
+            for p in parts:
+                diagonal = (
+                    (below[p] + upper[p])
+                    + (along_y[p] + self.last_y(along_y, p))
+                    + (along_z[p] + self.last_z(along_z, p))
+                )
+                inside = here[p] > 0.0
+                inverse.append(jnp.where(inside, 1.0 / jnp.where(inside, diagonal, 1.0), 0.0))
+            self.write(self.face_x, i + 1, upper)
+            self.write(self.face_y, i, along_y)
+            self.write(self.face_z, i, along_z)
+            self.write(self.inverse, i, inverse)
+            use(i, here, inverse)
+            return above, upper
+
+        here = self.read(self.coef, 1)
+        first = [half * here[p] for p in parts]
+        self.write(self.face_x, 0, first)
+        run(0, self.count, body, (here, first), self.unroll)
+
+    def sweep(self, low, count, use):
+        parts = range(self.parts)
+
+        def body(i, carry):
+            here, flux_low = carry
+            above = self.read(self.values, i + 2)
+            face_x, face_y, face_z = (self.read(ref, at) for ref, at in ((self.face_x, i + 1), (self.face_y, i), (self.face_z, i)))
+            flux_high = [face_x[p] * (above[p] - here[p]) for p in parts]
+            flux_y = [face_y[p] * (self.next_y(here, p) - here[p]) for p in parts]
+            flux_z = [face_z[p] * (self.next_z(here, p) - here[p]) for p in parts]
+            applied = [
+                (flux_low[p] - flux_high[p])
+                + (self.last_y(flux_y, p) - flux_y[p])
+                + (self.last_z(flux_z, p) - flux_z[p])
+                for p in parts
+            ]
+            use(i, applied, here)
+            return above, flux_high
+
+        here = self.read(self.values, low + 1)
+        before = self.read(self.values, low)
+        face = self.read(self.face_x, low)
+        run(low, count, body, (here, [face[p] * (here[p] - before[p]) for p in parts]), self.unroll)
+
+    def from_zero(self, i, inverse):
+        first = smoothing_weights()[0][1]
+        right = self.read(self.right, i)
+        step = [right[p] * (inverse[p] * first) for p in range(self.parts)]
+        self.write(self.update, i, step)
+        self.write(self.values, i + 1, step)
+
+    def smooth(self, low, count, weight):
+        keep, gain = weight
+
+        def use(i, applied, here):
+            right = self.read(self.right, i)
+            inverse = self.read(self.inverse, i)
+            step = [(right[p] - applied[p]) * (inverse[p] * gain) for p in range(self.parts)]
+            if keep:
+                update = self.read(self.update, i)
+                step = [keep * update[p] + step[p] for p in range(self.parts)]
+            self.write(self.update, i, step)
+            self.write(self.values, i + 1, [here[p] + step[p] for p in range(self.parts)])
+
+        self.sweep(low, count, use)
+
+
+def total(items):
+    items = list(items)
+    while len(items) > 1:
+        items = [sum(items[k : k + 2][1:], items[k]) for k in range(0, len(items), 2)]
+    return items[0]
+
+
+def exact_dot(left, right):
+    return jnp.dot(left, right, precision=lax.Precision.HIGHEST, preferred_element_type=jnp.float32)
+
+
+def parity_matrix(size, back):
+    row = lax.broadcasted_iota(jnp.int32, (size, size), 0)
+    column = lax.broadcasted_iota(jnp.int32, (size, size), 1)
+    if back:
+        row, column = column, row
+    hit = column == row // 2 + (row % 2) * (size // 2)
+    return jnp.where(hit, 1.0, 0.0).astype(jnp.float32)
+
+
+def split_kernel(right_side, coefficient, out, rows):
+    bx, by, bz = right_side.shape
+    matrix = parity_matrix(bz, False)
+    for which, ref in enumerate((right_side, coefficient)):
+        rows[...] = exact_dot(ref[...].reshape(bx * by, bz), matrix)
+        for odd in (0, 1):
+            out[which, odd] = rows[pl.ds(odd, bx * by // 2, stride=2), :].reshape(bx, by // 2, bz)
+
+
+def down_kernel(pos, own, sib, mid, start_out, right_out, coef_out, pay_out, edge_out, *refs):
+    level = Level(refs[:8], True, True, 1, 1.0, UNROLL_FINE)
+    sums, coefs = refs[8:]
+    bx, rows, bz = own.shape[3:]
+    core, odd, at_x, middle_valid, next_valid = (pos[k] for k in (0, 1, 3, 4, 5))
+    lane = lax.broadcasted_iota(jnp.int32, (rows, bz), 1)
+    quarter = bz // 4
+    is_own = lane < bz // 2
+    is_sib = (lane < 3 * quarter) == (core == 0)
+    level.clear_ends()
+
+    for block in range(6):
+        at = at_x * bx if block in (0, 2, 3) else (1 - at_x) * bx
+        row = {0: 1, 1: 1, 2: 2 * (1 - odd), 4: 2 * (1 - odd), 3: 2 * odd, 5: 2 * odd}[block] * rows
+        if block > 1:
+            row = pl.multiple_of(row, rows)
+        window = pl.ds(row, rows)
+
+        def assemble(x, carry, block=block, at=at, window=window):
+            for odd_y in (0, 1):
+                packed = mid[block, odd_y, x]
+                once, back = turn(packed, quarter, 1), turn(packed, -quarter, 1)
+                swapped = turn(packed, bz // 2, 1)
+                for which in (0, 1):
+                    mine = own[block, which, odd_y, x]
+                    side = sib[block, which, odd_y, x]
+                    if which == 0:
+                        far = (swapped, packed)
+                    else:
+                        far = (jnp.where(core == 1, once, back), jnp.where(core == 1, back, once))
+                        far = [jnp.where(middle_valid == 1, value, 0.0) for value in far]
+                    for odd_z in (0, 1):
+                        value = jnp.where(
+                            is_own,
+                            turn(mine, bz // 2, 1) if odd_z else mine,
+                            jnp.where(is_sib, side if odd_z else turn(side, bz // 2, 1), far[odd_z]),
+                        )
+                        if which == 1 and block in (3, 5):
+                            value = jnp.where(next_valid == 1, value, 0.0)
+                        ref, shift = ((level.right, 0), (level.coef, 1))[which]
+                        ref[2 * odd_y + odd_z, at + x + shift, window, :] = value
+            return carry
+
+        lax.fori_loop(0, bx, assemble, 0)
+
+    def begin(i, here, inverse):
+        level.from_zero(i, inverse)
+        coefs[i] = total(here)
+
+    level.set_faces(begin)
+    for weight in smoothing_weights()[1:]:
+        level.smooth(0, level.count, weight)
+
+    def leftover(i, applied, here):
+        right = level.read(level.right, i)
+        sums[i] = total(right[p] - applied[p] for p in range(level.parts))
+
+    level.sweep(0, level.count, leftover)
+
+    edge = rows // 2
+    upper_half = lax.broadcasted_iota(jnp.int32, (rows, bz), 0) < edge
+    for which, ref in enumerate((sums, coefs)):
+        for x in range(bx):
+            ref[x] = 0.125 * (ref[2 * x] + ref[2 * x + 1])
+            halves = [ref[x, pl.ds(edge + parity, rows, stride=2), :] for parity in (0, 1)]
+            for parity in (0, 1):
+                pay_out[which, parity, x] = halves[parity]
+            edge_out[which, x] = jnp.where(
+                upper_half,
+                jnp.where(odd == 1, turn(halves[0], edge, 0), halves[0]),
+                jnp.where(odd == 1, halves[1], turn(halves[1], edge, 0)),
+            )
+
+    window = pl.ds(edge, 2 * rows)
+
+    def copy_out(i, carry):
+        for part in range(level.parts):
+            start_out[part, i] = turn(level.values[part, i + 1, window, :], -edge, 0)
+            right_out[part, i] = turn(level.right[part, i, window, :], -edge, 0)
+            coef_out[part, i] = turn(level.coef[part, i + 1, window, :], -edge, 0)
+        return carry
+
+    lax.fori_loop(0, level.count, copy_out, 0)
+
+
+def up_kernel(pos, pay, far, near, start, right, coef_in, solution_out, residual_out, *refs):
+    level1 = Level(refs[:8], True, False, 1, 0.25, UNROLL_COARSE)
+    level2 = Level(refs[8:16], False, False, 2, 0.0625, UNROLL_COARSE)
+    fine = Level((refs[16], right, *refs[17:23]), True, True, 1, 1.0, UNROLL_FINE)
+    window, rows_out = refs[23:]
+    n1, rows, bz = pay.shape[2:]
+    edge = rows // 2
+    odd, upper, at_x, near_valid = (pos[k] for k in (1, 2, 3, 6))
+    weights = smoothing_weights()
+    for level in (level1, level2, fine):
+        level.clear_ends()
+
+    top = lax.broadcasted_iota(jnp.int32, (rows, bz), 0) < edge
+    near_here = (top == (odd == 0)) & (near_valid == 1)
+    for j in range(n1):
+        for which, (ref, shift) in enumerate(((level1.right, 0), (level1.coef, 1))):
+            piece = near[which, j]
+            other = turn(piece, edge, 0)
+            for parity in (0, 1):
+                mine, theirs = pay[which, parity, j], far[which, parity, j]
+                ref[parity, j + shift, :rows] = jnp.where(upper == 1, theirs, mine)
+                ref[parity, j + shift, rows : 2 * rows] = jnp.where(upper == 1, mine, theirs)
+                if parity == 0:
+                    side = jnp.where(odd == 0, piece, other)
+                else:
+                    side = jnp.where(odd == 0, other, piece)
+                ref[parity, j + shift, 2 * rows :] = jnp.where(near_here, side, 0.0)
+
+    even_lane = lax.broadcasted_iota(jnp.int32, (3 * rows, bz), 1) % 2 == 0
+
+    def pair_lanes(values):
+        return values + jnp.where(even_lane, turn(values, -1, 1), turn(values, 1, 1))
+
+    coefs, sums = [], []
+
+    def begin1(i, here, inverse):
+        level1.from_zero(i, inverse)
+        coefs.append(total(here))
+
+    level1.set_faces(begin1)
+    for weight in weights[1:]:
+        level1.smooth(0, n1, weight)
+
+    def leftover1(i, applied, here):
+        values = level1.read(level1.right, i)
+        sums.append(total(values[p] - applied[p] for p in range(level1.parts)))
+
+    level1.sweep(0, n1, leftover1)
+    for j in range(n1 // 2):
+        level2.right[0, j] = 0.125 * pair_lanes(sums[2 * j] + sums[2 * j + 1])
+        level2.coef[0, j + 1] = 0.125 * pair_lanes(coefs[2 * j] + coefs[2 * j + 1])
+
+    level2.set_faces(lambda i, here, inverse: level2.from_zero(i, inverse))
+    for weight in weights[1:]:
+        level2.smooth(0, n1 // 2, weight)
+
+    for j in range(n1):
+        for parity in (0, 1):
+            level1.values[parity, j + 1] = level1.values[parity, j + 1] + level2.values[0, j // 2 + 1]
+    for weight in weights:
+        level1.smooth(0, n1, weight)
+
+    def copy_in(i, carry):
+        for part in range(fine.parts):
+            fine.coef[part, i + 1] = coef_in[part, i]
+        return carry
+
+    lax.fori_loop(0, fine.count, copy_in, 0)
+    fine.set_faces(lambda i, here, inverse: None)
+    for j in range(n1):
+        for parity in (0, 1):
+            rows_of = level1.values[parity, j + 1, :rows], level1.values[parity, j + 1, rows : 2 * rows]
+            window[j, pl.ds(parity, rows, stride=2), :] = jnp.where(upper == 1, rows_of[1], rows_of[0])
+        spread = turn(window[j], -edge, 0)
+        for i in (2 * j, 2 * j + 1):
+            for part in range(fine.parts):
+                fine.values[part, i + 1] = start[part, i] + spread
+    bx = fine.count // 2
+    for number, weight in enumerate(weights):
+        reach = DEGREE - number
+        fine.smooth(jnp.where(at_x == 0, 0, bx - reach), bx + reach, weight)
+
+    base = at_x * bx
+    own_lane = lax.broadcasted_iota(jnp.int32, (rows, bz), 1) < bz // 2
+
+    def finish(i, applied, here):
+        values = fine.read(right, i)
+        for slot, field in enumerate((here, [values[p] - applied[p] for p in range(fine.parts)])):
+            for odd_y in (0, 1):
+                even, other = field[2 * odd_y][:rows], field[2 * odd_y + 1][:rows]
+                rows_out[slot, i - base, pl.ds(odd_y, rows, stride=2), :] = jnp.where(
+                    own_lane, even, turn(other, bz // 2, 1)
+                )
+
+    fine.sweep(base, bx, finish)
+    matrix = parity_matrix(bz, True)
+    for slot, ref in enumerate((solution_out, residual_out)):
+        ref[...] = exact_dot(rows_out[slot].reshape(bx * 2 * rows, bz), matrix).reshape(ref.shape)
+
+
+def vmem(*shape):
+    return pltpu.VMEM(shape, jnp.float32)
+
+
+def level_scratch(parts, n, rows, lanes, with_right):
+    tall, plain = vmem(parts, n + 2, rows, lanes), vmem(parts, n, rows, lanes)
+    return [
+        tall,
+        *([plain] if with_right else []),
+        vmem(parts, n + 1, rows, lanes),
+        plain,
+        plain,
+        plain,
+        tall,
+        plain,
+    ]
+
+
+def per_device_two_rounds(right_side, coefficient):
+    bx, by, bz = right_side.shape
+    rows = by // 2
+    at_x, at_y, at_z = (lax.axis_index(name) for name in ("gx", "gy", "gz"))
+    core = at_z % 2
+    middle_y, middle_z = ((at == 1) | (at == 2) for at in (at_y, at_z))
+    pos = jnp.stack([core, at_y % 2, at_y // 2, at_x, middle_z, middle_y, middle_y]).astype(jnp.int32)
+    in_smem = pl.BlockSpec(memory_space=pltpu.SMEM)
+    in_vmem = pl.BlockSpec(memory_space=pltpu.VMEM)
+    params = pltpu.CompilerParams(vmem_limit_bytes=24 * 2**20)
+    shape = lambda *sizes: jax.ShapeDtypeStruct(sizes, jnp.float32)
+
+    mine = pl.pallas_call(
+        split_kernel,
+        out_shape=shape(2, 2, bx, rows, bz),
+        in_specs=[in_vmem] * 2,
+        out_specs=in_vmem,
+        scratch_shapes=[vmem(bx * by, bz)],
+        compiler_params=params,
+        name="split",
+    )(right_side, coefficient)
+
+    pairs = [1, 0, 3, 2]
+    inner = [0, 2, 1, 3]
+    across = [(0, 1), (1, 0)]
+
+    def both(partner):
+        return [(4 * x + y, 4 * (1 - x) + partner[y]) for x in (0, 1) for y in range(4)]
+
+    blocks = jnp.stack(
+        [
+            mine,
+            lax.ppermute(mine, "gx", across),
+            lax.ppermute(mine, "gy", list(enumerate(pairs))),
+            lax.ppermute(mine, "gy", list(enumerate(inner))),
+            lax.ppermute(mine, ("gx", "gy"), both(pairs)),
+            lax.ppermute(mine, ("gx", "gy"), both(inner)),
+        ]
+    )
+    quarter = bz // 4
+    low_quarter = jnp.arange(bz) % (bz // 2) < quarter
+    right_blocks, coef_blocks = blocks[:, 0], blocks[:, 1]
+    packed = jnp.where(
+        core == 0,
+        jnp.where(low_quarter, right_blocks, jnp.roll(coef_blocks, quarter, axis=-1)),
+        jnp.where(low_quarter, jnp.roll(coef_blocks, -quarter, axis=-1), right_blocks),
+    )
+    mid = lax.ppermute(packed, "gz", list(enumerate(inner)))
+    sib = lax.ppermute(blocks, "gz", list(enumerate(pairs)))
+
+    nx = 2 * bx
+    window = shape(4, nx, 2 * rows, bz)
+    start, right_wide, coef_wide, pay, edge = pl.pallas_call(
+        down_kernel,
+        out_shape=(window, window, window, shape(2, 2, bx, rows, bz), shape(2, bx, rows, bz)),
+        in_specs=[in_smem] + [in_vmem] * 3,
+        out_specs=(in_vmem,) * 5,
+        scratch_shapes=[
+            *level_scratch(4, nx, 3 * rows, bz, True),
+            vmem(nx, 3 * rows, bz),
+            vmem(nx, 3 * rows, bz),
+        ],
+        compiler_params=params,
+        name="down",
+    )(pos, blocks, sib, mid)
+    far = lax.ppermute(pay, "gy", [(0, 2), (2, 0), (1, 3), (3, 1)])
+    near = lax.ppermute(edge, "gy", list(enumerate(pairs)))
+    return pl.pallas_call(
+        up_kernel,
+        out_shape=(shape(bx, by, bz),) * 2,
+        in_specs=[in_smem] + [in_vmem] * 6,
+        out_specs=(in_vmem,) * 2,
+        scratch_shapes=[
+            *level_scratch(2, bx, 3 * rows, bz, True),
+            *level_scratch(1, bx // 2, 3 * rows, bz, True),
+            *level_scratch(4, nx, 2 * rows, bz, False),
+            vmem(bx, 2 * rows, bz),
+            vmem(2, bx, by, bz),
+        ],
+        compiler_params=params,
+        name="up",
+    )(pos, pay, far, near, start, right_wide, coef_wide)
+
+
+def two_rounds_fit(mesh, shape):
+    counts = tuple(mesh.shape[name] for name in ("gx", "gy", "gz"))
+    bx, by, bz = (size // count for size, count in zip(shape, counts))
+    edge = by // 4
+    reach_coarse = 4 * DEGREE + 2
+    return (
+        counts == (2, 4, 4)
+        and LEVELS == 3
+        and bx % 4 == 0
+        and by == 16
+        and bz == 128
+        and 2 * edge + DEGREE + 1 <= by
+        and by // 2 + reach_coarse <= 2 * by - edge
+        and 2 * reach_coarse + DEGREE + 1 <= bz // 2
+    )
+
+
 def solution(mesh):
     in_specs = (P("gx", "gy", "gz"), P("gx", "gy", "gz"))
     out_specs = (P("gx", "gy", "gz"), P("gx", "gy", "gz"))
-    return jax.shard_map(
-        per_device, mesh=mesh, in_specs=in_specs, out_specs=out_specs, check_vma=False
-    )
+
+    def whole(right_side, coefficient):
+        fits = two_rounds_fit(mesh, right_side.shape)
+        return jax.shard_map(
+            per_device_two_rounds if fits else per_device,
+            mesh=mesh,
+            in_specs=in_specs,
+            out_specs=out_specs,
+            check_vma=False,
+        )(right_side, coefficient)
+
+    return whole

time: 393 us -> 48.3 us (0.12)
  starting transfers between devices: 241 us -> 16.3 us
  waiting for transfers between devices: 101 us -> 13.1 us
  other arithmetic: 23.1 us -> 0.28 us
  local copies, waits for them, and re-layouts: 22.9 us -> 2.32 us
  Pallas kernels: 0 us -> 15.2 us
    ppermute x96 -> x9, starting transfers between devices: 241 us -> 16.3 us  [the longest x1 3.05 us: per_device_two_rounds(): mid = lax.ppermute(packed, 'gz', list(enumerate(inner)))]
    ppermute x96 -> x9, waiting for transfers between devices: 101 us -> 13.1 us  [the longest x1 5.79 us: per_device_two_rounds(): mid = lax.ppermute(packed, 'gz', list(enumerate(inner)))]
    reshape x5 -> x0, local copies, waits for them, and re-layouts: 16.6 us -> none  [the longest x3 12.4 us: restrict(): blocks = values.reshape(size_x // 2, 2, size_y // 2, 2, size_z // 2, 2)]
    pallas_call x0 -> x3, Pallas kernels: none -> 15.2 us  [the longest x1 8.24 us: per_device_two_rounds(): pl.pallas_call(down_kernel, out_shape=(window, window, window, shape(2, 2...]
    mul x69 -> x0, other arithmetic: 9.4 us -> none  [the longest x20 2.91 us: apply_padded(): flux_z = face_z * (padded[1:-1, 1:-1, 1:] - padded[1:-1, 1:-1, :-1])]
    reduce_sum x4 -> x0, other arithmetic: 5.34 us -> none  [restrict(): return jnp.mean(blocks, axis=(1, 3, 5))]
    add x19 -> x0, other arithmetic: 4.4 us -> none  [the longest x6 2.91 us: deep_smooth(): iterate = trim_cells(iterate, 1) + update]
  transfers between devices with their start and end apart: 96 -> 9, of which waited for: 45 -> 4; matrix products, arithmetic and copies ran while one was open for 7% -> 2% of each run, Pallas kernels for 0% -> 0%
where the time goes in v2:
time: 48.3 us; the launch traced here: 48.1 us
  starting transfers between devices  16.3 us (34%)
  Pallas kernels  15.2 us (31%)
  waiting for transfers between devices  13.1 us (27%)
  local copies, waits for them, and re-layouts  2.32 us (5%)
  between operations  0.83 us (2%)
    pallas_call x1, Pallas kernels, per_device_two_rounds(): pl.pallas_call(down_kernel, out_shape=(window, window, window, shape(2, 2...  8.24 us
    pallas_call x1, Pallas kernels, per_device_two_rounds(): pl.pallas_call(up_kernel, out_shape=(shape(bx, by, bz),) * 2, in_specs=[i...  6.72 us
    ppermute x1, waiting for transfers between devices, per_device_two_rounds(): mid = lax.ppermute(packed, 'gz', list(enumerate(inner)))  5.79 us
    ppermute x1, starting transfers between devices, per_device_two_rounds(): mid = lax.ppermute(packed, 'gz', list(enumerate(inner)))  3.05 us
    ppermute x1, starting transfers between devices, per_device_two_rounds(): lax.ppermute(mine, 'gy', list(enumerate(pairs)))  2.89 us
    ppermute x1, waiting for transfers between devices, per_device_two_rounds(): lax.ppermute(mine, 'gx', across)  2.87 us
    ppermute x1, waiting for transfers between devices, per_device_two_rounds(): near = lax.ppermute(edge, 'gy', list(enumerate(pairs)))  2.79 us
    ppermute x1, starting transfers between devices, per_device_two_rounds(): sib = lax.ppermute(blocks, 'gz', list(enumerate(pairs)))  2.71 us
  transfers between devices with their start and end apart: 9, of which 4 were waited for; matrix products, arithmetic and copies ran while one was open for 2% of the time, Pallas kernels for 0%

profile of v2, /device:TPU:1, one launch (start us, length us, event | category | flops | bytes accessed | tf_op | source)
XLA Modules:
  0.0 48.1 jit_solution(9973927311193975388)
XLA Ops:
  0.6 0.8 %copy-done = f32[8,16,128]{2,1,0:T(8,128)S(1)} copy-done((f32[8,16,128]{2,1,0:T(8,128)S(1)}, f32[8,16,128]{2,1,0:T(8,128)}, u32[]{:S(2)}) %copy-start) | copy-done | bytes 65560
  1.5 0.8 %copy-done.1 = f32[8,16,128]{2,1,0:T(8,128)S(1)} copy-done((f32[8,16,128]{2,1,0:T(8,128)S(1)}, f32[8,16,128]{2,1,0:T(8,128)}, u32[]{:S(2)}) %copy-start.1) | copy-done | bytes 65560
  2.3 0.3 split.1
  2.6 2.1 %collective-permute-start.4 = (f32[2,2,8,8,128]{4,3,2,1,0:T(8,128)S(1)}, f32[2,2,8,8,128]{4,3,2,1,0:T(8,128)S(1)}, u32[]{:S(2)}, u32[]{:S(2)}) collective-permute-start(f32[2,2,8,8,128]{4,3,2,1,0:T(8,128)S(1)} %split.1), channel_id=1, source_target_pairs={{0,16},{4,24},{8,20},{12,28},{16,0},{20,8},{24,4},{28,12},{1,17},{... | collective-permute-start | bytes 393224 | tf_op jit(solution)/shard_map/ppermute | solution.py:646
  4.7 2.3 %collective-permute-start.3 = (f32[2,2,8,8,128]{4,3,2,1,0:T(8,128)S(1)}, f32[2,2,8,8,128]{4,3,2,1,0:T(8,128)S(1)}, u32[]{:S(2)}, u32[]{:S(2)}) collective-permute-start(f32[2,2,8,8,128]{4,3,2,1,0:T(8,128)S(1)} %split.1), channel_id=1, source_target_pairs={{0,20},{4,16},{8,28},{12,24},{16,4},{20,0},{24,12},{28,8},{1,21},{... | collective-permute-start | bytes 393224 | tf_op jit(solution)/shard_map/ppermute | solution.py:645
  7.0 0.7 %collective-permute-start.2 = (f32[2,2,8,8,128]{4,3,2,1,0:T(8,128)S(1)}, f32[2,2,8,8,128]{4,3,2,1,0:T(8,128)S(1)}, u32[]{:S(2)}, u32[]{:S(2)}) collective-permute-start(f32[2,2,8,8,128]{4,3,2,1,0:T(8,128)S(1)} %split.1), channel_id=1, source_target_pairs={{0,0},{4,8},{8,4},{12,12},{1,1},{5,9},{9,5},{13,13},{2,2},{6,10},{... | collective-permute-start | bytes 393224 | tf_op jit(solution)/shard_map/ppermute | solution.py:644
  7.6 2.9 %collective-permute-start.1 = (f32[2,2,8,8,128]{4,3,2,1,0:T(8,128)S(1)}, f32[2,2,8,8,128]{4,3,2,1,0:T(8,128)S(1)}, u32[]{:S(2)}, u32[]{:S(2)}) collective-permute-start(f32[2,2,8,8,128]{4,3,2,1,0:T(8,128)S(1)} %split.1), channel_id=1, source_target_pairs={{0,4},{4,0},{8,12},{12,8},{1,5},{5,1},{9,13},{13,9},{2,6},{6,2},{1... | collective-permute-start | bytes 393224 | tf_op jit(solution)/shard_map/ppermute | solution.py:643
  10.5 1.2 %collective-permute-start = (f32[2,2,8,8,128]{4,3,2,1,0:T(8,128)S(1)}, f32[2,2,8,8,128]{4,3,2,1,0:T(8,128)S(1)}, u32[]{:S(2)}, u32[]{:S(2)}) collective-permute-start(f32[2,2,8,8,128]{4,3,2,1,0:T(8,128)S(1)} %split.1), channel_id=1, source_target_pairs={{0,16},{16,0},{1,17},{17,1},{2,18},{18,2},{3,19},{19,3},{4,20},{20... | collective-permute-start | bytes 393224 | tf_op jit(solution)/shard_map/ppermute | solution.py:642
  11.8 2.9 %collective-permute-done = f32[2,2,8,8,128]{4,3,2,1,0:T(8,128)S(1)} collective-permute-done((f32[2,2,8,8,128]{4,3,2,1,0:T(8,128)S(1)}, f32[2,2,8,8,128]{4,3,2,1,0:T(8,128)S(1)}, u32[]{:S(2)}, u32[]{:S(2)}) %collective-permute-start) | collective-permute-done | bytes 131104 | tf_op jit(solution)/shard_map/ppermute | solution.py:642
  14.8 2.7 %collective-permute-start.5 = (f32[6,2,2,8,8,128]{5,4,3,2,0,1:T(8,128)S(1)}, f32[6,2,2,8,8,128]{5,4,3,2,0,1:T(8,128)S(1)}, u32[]{:S(2)}, u32[]{:S(2)}) collective-permute-start(f32[6,2,2,8,8,128]{5,4,3,2,0,1:T(8,128)S(1)} %bitcast_dynamic-update-slice_fusion), channel_id=1, source_target_pairs={{0,1},{1,0},{2,3},{3,2},{4,5},{5,4},{6,7},{7,6},{8,9},{9,8},{10,11... | collective-permute-start | bytes 2359304 | tf_op jit(solution)/shard_map/ppermute | solution.py:658
  17.5 0.2 fusion.3
  17.7 0.2 fusion.2
  17.9 0.3 fusion
  18.2 3.0 %collective-permute-start.6 = (f32[6,2,8,8,128]{4,3,2,1,0:T(8,128)S(1)}, f32[6,2,8,8,128]{4,3,2,1,0:T(8,128)S(1)}, u32[]{:S(2)}, u32[]{:S(2)}) collective-permute-start(f32[6,2,8,8,128]{4,3,2,1,0:T(8,128)S(1)} %fusion), channel_id=1, source_target_pairs={{0,0},{1,2},{2,1},{3,3},{4,4},{5,6},{6,5},{7,7},{8,8},{9,10},{10,9... | collective-permute-start | bytes 1179656 | tf_op jit(solution)/shard_map/ppermute | solution.py:657
  21.3 0.1 stack.57.pos
  21.4 0.1 copy.4.own
  21.4 0.1 copy.5.sib
  21.5 5.8 %collective-permute-done.6.mid = f32[6,2,8,8,128]{4,3,2,1,0:T(8,128)S(1)} collective-permute-done((f32[6,2,8,8,128]{4,3,2,1,0:T(8,128)S(1)}, f32[6,2,8,8,128]{4,3,2,1,0:T(8,128)S(1)}, u32[]{:S(2)}, u32[]{:S(2)}) %collective-permute-start.6) | collective-permute-done | bytes 393248 | tf_op jit(solution)/shard_map/ppermute | solution.py:657
  27.3 8.2 %down.1 = (f32[4,16,16,128]{3,2,1,0:T(8,128)S(1)}, f32[4,16,16,128]{3,2,1,0:T(8,128)S(1)}, f32[4,16,16,128]{3,2,1,0:T(8,128)S(1)}, f32[2,2,8,8,128]{4,3,2,1,0:T(8,128)S(1)}, f32[2,8,8,128]{3,2,1,0:T(8,128)S(1)}) custom-call(s32[7]{0:T(128)S(1)} %stack.57.pos, f32[6,2,2,8,8,128]{5,4,3,2,1,0:T(8,128)S(1)} %copy.4.own, f32[6,2,2,8,8,128]{5,4,3,2,1,0:T(8,128)S(1)} %copy.5.sib, ...), custom_call_target="tpu_custom_call" | custom-call | tf_op jit(solution)/shard_map/down/pallas_call | solution.py:662
  35.5 1.0 %collective-permute-start.7 = (f32[2,2,8,8,128]{4,3,2,1,0:T(8,128)S(1)}, f32[2,2,8,8,128]{4,3,2,1,0:T(8,128)S(1)}, u32[]{:S(2)}, u32[]{:S(2)}) collective-permute-start(f32[2,2,8,8,128]{4,3,2,1,0:T(8,128)S(1)} %get-tuple-element.7.pay), channel_id=1, source_target_pairs={{0,8},{8,0},{4,12},{12,4},{1,9},{9,1},{5,13},{13,5},{2,10},{10,2},... | collective-permute-start | bytes 393224 | tf_op jit(solution)/shard_map/ppermute | solution.py:675
  36.5 0.4 collective-permute-start.8
  36.9 2.8 %collective-permute-done.8.near = f32[2,8,8,128]{3,2,1,0:T(8,128)S(1)} collective-permute-done((f32[2,8,8,128]{3,2,1,0:T(8,128)S(1)}, f32[2,8,8,128]{3,2,1,0:T(8,128)S(1)}, u32[]{:S(2)}, u32[]{:S(2)}) %collective-permute-start.8) | collective-permute-done | bytes 65568 | tf_op jit(solution)/shard_map/ppermute | solution.py:676
  39.7 1.6 %collective-permute-done.7.far = f32[2,2,8,8,128]{4,3,2,1,0:T(8,128)S(1)} collective-permute-done((f32[2,2,8,8,128]{4,3,2,1,0:T(8,128)S(1)}, f32[2,2,8,8,128]{4,3,2,1,0:T(8,128)S(1)}, u32[]{:S(2)}, u32[]{:S(2)}) %collective-permute-start.7) | collective-permute-done | bytes 131104 | tf_op jit(solution)/shard_map/ppermute | solution.py:675
  41.4 6.7 %up.1 = (f32[8,16,128]{2,1,0:T(8,128)}, f32[8,16,128]{2,1,0:T(8,128)}) custom-call(s32[7]{0:T(128)S(1)} %stack.57.pos, f32[2,2,8,8,128]{4,3,2,1,0:T(8,128)S(1)} %get-tuple-element.7.pay, f32[2,2,8,8,128]{4,3,2,1,0:T(8,128)S(1)} %collective-permute-done.7.far, f32[2,8,8,128]{3,2,1,0:T(8,128)S(1)} %collective-permute-done.8.near, ...), custom_call_target="tpu_custom_call" | custom-call | tf_op jit(solution)/shard_map/up/pallas_call | solution.py:677
  (15 shorter events, 0.1 us)
Async XLA Ops:
  0.6 0.8 %copy-start = (f32[8,16,128]{2,1,0:T(8,128)S(1)}, f32[8,16,128]{2,1,0:T(8,128)}, u32[]{:S(2)}) copy-start(f32[8,16,128]{2,1,0:T(8,128)} %right_side.1) | copy-start | bytes 196612
  1.5 0.8 %copy-start.1 = (f32[8,16,128]{2,1,0:T(8,128)S(1)}, f32[8,16,128]{2,1,0:T(8,128)}, u32[]{:S(2)}) copy-start(f32[8,16,128]{2,1,0:T(8,128)} %coefficient.1) | copy-start | bytes 196612
  2.6 12.2 %collective-permute-start.4 = (f32[2,2,8,8,128]{4,3,2,1,0:T(8,128)S(1)}, f32[2,2,8,8,128]{4,3,2,1,0:T(8,128)S(1)}, u32[]{:S(2)}, u32[]{:S(2)}) collective-permute-start(f32[2,2,8,8,128]{4,3,2,1,0:T(8,128)S(1)} %split.1), channel_id=1, source_target_pairs={{0,16},{4,24},{8,20},{12,28},{16,0},{20,8},{24,4},{28,12},{1,17},{... | collective-permute-start | bytes 393224 | tf_op jit(solution)/shard_map/ppermute | solution.py:646
  4.7 10.0 %collective-permute-start.3 = (f32[2,2,8,8,128]{4,3,2,1,0:T(8,128)S(1)}, f32[2,2,8,8,128]{4,3,2,1,0:T(8,128)S(1)}, u32[]{:S(2)}, u32[]{:S(2)}) collective-permute-start(f32[2,2,8,8,128]{4,3,2,1,0:T(8,128)S(1)} %split.1), channel_id=1, source_target_pairs={{0,20},{4,16},{8,28},{12,24},{16,4},{20,0},{24,12},{28,8},{1,21},{... | collective-permute-start | bytes 393224 | tf_op jit(solution)/shard_map/ppermute | solution.py:645
  7.0 7.7 %collective-permute-start.2 = (f32[2,2,8,8,128]{4,3,2,1,0:T(8,128)S(1)}, f32[2,2,8,8,128]{4,3,2,1,0:T(8,128)S(1)}, u32[]{:S(2)}, u32[]{:S(2)}) collective-permute-start(f32[2,2,8,8,128]{4,3,2,1,0:T(8,128)S(1)} %split.1), channel_id=1, source_target_pairs={{0,0},{4,8},{8,4},{12,12},{1,1},{5,9},{9,5},{13,13},{2,2},{6,10},{... | collective-permute-start | bytes 393224 | tf_op jit(solution)/shard_map/ppermute | solution.py:644
  7.6 7.0 %collective-permute-start.1 = (f32[2,2,8,8,128]{4,3,2,1,0:T(8,128)S(1)}, f32[2,2,8,8,128]{4,3,2,1,0:T(8,128)S(1)}, u32[]{:S(2)}, u32[]{:S(2)}) collective-permute-start(f32[2,2,8,8,128]{4,3,2,1,0:T(8,128)S(1)} %split.1), channel_id=1, source_target_pairs={{0,4},{4,0},{8,12},{12,8},{1,5},{5,1},{9,13},{13,9},{2,6},{6,2},{1... | collective-permute-start | bytes 393224 | tf_op jit(solution)/shard_map/ppermute | solution.py:643
  10.5 4.1 %collective-permute-start = (f32[2,2,8,8,128]{4,3,2,1,0:T(8,128)S(1)}, f32[2,2,8,8,128]{4,3,2,1,0:T(8,128)S(1)}, u32[]{:S(2)}, u32[]{:S(2)}) collective-permute-start(f32[2,2,8,8,128]{4,3,2,1,0:T(8,128)S(1)} %split.1), channel_id=1, source_target_pairs={{0,16},{16,0},{1,17},{17,1},{2,18},{18,2},{3,19},{19,3},{4,20},{20... | collective-permute-start | bytes 393224 | tf_op jit(solution)/shard_map/ppermute | solution.py:642
  14.8 6.6 %collective-permute-start.5 = (f32[6,2,2,8,8,128]{5,4,3,2,0,1:T(8,128)S(1)}, f32[6,2,2,8,8,128]{5,4,3,2,0,1:T(8,128)S(1)}, u32[]{:S(2)}, u32[]{:S(2)}) collective-permute-start(f32[6,2,2,8,8,128]{5,4,3,2,0,1:T(8,128)S(1)} %bitcast_dynamic-update-slice_fusion), channel_id=1, source_target_pairs={{0,1},{1,0},{2,3},{3,2},{4,5},{5,4},{6,7},{7,6},{8,9},{9,8},{10,11... | collective-permute-start | bytes 2359304 | tf_op jit(solution)/shard_map/ppermute | solution.py:658
  18.2 9.1 %collective-permute-start.6 = (f32[6,2,8,8,128]{4,3,2,1,0:T(8,128)S(1)}, f32[6,2,8,8,128]{4,3,2,1,0:T(8,128)S(1)}, u32[]{:S(2)}, u32[]{:S(2)}) collective-permute-start(f32[6,2,8,8,128]{4,3,2,1,0:T(8,128)S(1)} %fusion), channel_id=1, source_target_pairs={{0,0},{1,2},{2,1},{3,3},{4,4},{5,6},{6,5},{7,7},{8,8},{9,10},{10,9... | collective-permute-start | bytes 1179656 | tf_op jit(solution)/shard_map/ppermute | solution.py:657
  35.5 5.8 %collective-permute-start.7 = (f32[2,2,8,8,128]{4,3,2,1,0:T(8,128)S(1)}, f32[2,2,8,8,128]{4,3,2,1,0:T(8,128)S(1)}, u32[]{:S(2)}, u32[]{:S(2)}) collective-permute-start(f32[2,2,8,8,128]{4,3,2,1,0:T(8,128)S(1)} %get-tuple-element.7.pay), channel_id=1, source_target_pairs={{0,8},{8,0},{4,12},{12,4},{1,9},{9,1},{5,13},{13,5},{2,10},{10,2},... | collective-permute-start | bytes 393224 | tf_op jit(solution)/shard_map/ppermute | solution.py:675
  36.5 3.2 %collective-permute-start.8 = (f32[2,8,8,128]{3,2,1,0:T(8,128)S(1)}, f32[2,8,8,128]{3,2,1,0:T(8,128)S(1)}, u32[]{:S(2)}, u32[]{:S(2)}) collective-permute-start(f32[2,8,8,128]{3,2,1,0:T(8,128)S(1)} %get-tuple-element.8), channel_id=1, source_target_pairs={{0,4},{4,0},{8,12},{12,8},{1,5},{5,1},{9,13},{13,9},{2,6},{6,2},{1... | collective-permute-start | bytes 196616 | tf_op jit(solution)/shard_map/ppermute | solution.py:676

commit v3 on v2

--- a/solution.py
+++ b/solution.py
@@ -208,8 +208,18 @@
     return (solution, residual)
 
 
+ORDER = (0, 1, 3, 5, 2, 4)
 UNROLL_FINE = 4
 UNROLL_COARSE = 16
+
+
+def place():
+    at_x, at_y, at_z = (lax.axis_index(name) for name in ("gx", "gy", "gz"))
+    return at_x, at_y, at_z, lax.rem(at_z, 2), lax.rem(at_y, 2)
+
+
+def in_the_middle(at):
+    return (at == 1) | (at == 2)
 
 
 def smoothing_weights():
@@ -395,59 +405,79 @@
     return jnp.where(hit, 1.0, 0.0).astype(jnp.float32)
 
 
-def split_kernel(right_side, coefficient, out, rows):
-    bx, by, bz = right_side.shape
+def split_kernel(fields, out, rows):
+    _, bx, by, bz = fields.shape
     matrix = parity_matrix(bz, False)
-    for which, ref in enumerate((right_side, coefficient)):
-        rows[...] = exact_dot(ref[...].reshape(bx * by, bz), matrix)
+    for which in (0, 1):
+        rows[which] = exact_dot(fields[which].reshape(bx * by, bz), matrix)
         for odd in (0, 1):
-            out[which, odd] = rows[pl.ds(odd, bx * by // 2, stride=2), :].reshape(bx, by // 2, bz)
-
-
-def down_kernel(pos, own, sib, mid, start_out, right_out, coef_out, pay_out, edge_out, *refs):
+            out[which, odd] = rows[which, pl.ds(odd, bx * by // 2, stride=2), :].reshape(bx, by // 2, bz)
+
+
+def pack_kernel(*refs):
+    *blocks, across_out, beside_out = refs
+    bx, rows, bz = blocks[0].shape[2:]
+    _, _, _, core, _ = place()
+    quarter = bz // 4
+    low = lax.broadcasted_iota(jnp.int32, (rows, bz), 1) % (bz // 2) < quarter
+
+    def body(x, carry):
+        for number, block in enumerate(blocks):
+            for odd_y in (0, 1):
+                right, coef = block[0, odd_y, x], block[1, odd_y, x]
+                first = jnp.where(low, right, turn(coef, quarter, 1))
+                last = jnp.where(low, turn(coef, -quarter, 1), right)
+                across_out[number, odd_y, x] = jnp.where(core == 0, first, last)
+                beside_out[number, odd_y, x] = jnp.where(core == 0, last, first)
+        return carry
+
+    lax.fori_loop(0, bx, body, 0, unroll=4)
+
+
+def down_kernel(own, mid, sib, start_out, right_out, coef_out, pay_out, edge_out, *refs):
     level = Level(refs[:8], True, True, 1, 1.0, UNROLL_FINE)
     sums, coefs = refs[8:]
     bx, rows, bz = own.shape[3:]
-    core, odd, at_x, middle_valid, next_valid = (pos[k] for k in (0, 1, 3, 4, 5))
+    at_x, at_y, at_z, core, odd = place()
     lane = lax.broadcasted_iota(jnp.int32, (rows, bz), 1)
     quarter = bz // 4
     is_own = lane < bz // 2
-    is_sib = (lane < 3 * quarter) == (core == 0)
+    low = lane % (bz // 2) < quarter
+    outside = (low == (core == 1)) & ~in_the_middle(at_z)
     level.clear_ends()
 
-    for block in range(6):
-        at = at_x * bx if block in (0, 2, 3) else (1 - at_x) * bx
-        row = {0: 1, 1: 1, 2: 2 * (1 - odd), 4: 2 * (1 - odd), 3: 2 * odd, 5: 2 * odd}[block] * rows
-        if block > 1:
+    for block, kind in enumerate(ORDER):
+        at = at_x * bx if kind in (0, 2, 3) else (1 - at_x) * bx
+        row = {0: 1, 1: 1, 2: 2 * (1 - odd), 4: 2 * (1 - odd), 3: 2 * odd, 5: 2 * odd}[kind] * rows
+        if kind > 1:
             row = pl.multiple_of(row, rows)
         window = pl.ds(row, rows)
 
-        def assemble(x, carry, block=block, at=at, window=window):
+        def assemble(x, carry, block=block, kind=kind, at=at, window=window):
             for odd_y in (0, 1):
-                packed = mid[block, odd_y, x]
-                once, back = turn(packed, quarter, 1), turn(packed, -quarter, 1)
-                swapped = turn(packed, bz // 2, 1)
-                for which in (0, 1):
-                    mine = own[block, which, odd_y, x]
-                    side = sib[block, which, odd_y, x]
-                    if which == 0:
-                        far = (swapped, packed)
-                    else:
-                        far = (jnp.where(core == 1, once, back), jnp.where(core == 1, back, once))
-                        far = [jnp.where(middle_valid == 1, value, 0.0) for value in far]
-                    for odd_z in (0, 1):
-                        value = jnp.where(
-                            is_own,
-                            turn(mine, bz // 2, 1) if odd_z else mine,
-                            jnp.where(is_sib, side if odd_z else turn(side, bz // 2, 1), far[odd_z]),
-                        )
-                        if which == 1 and block in (3, 5):
-                            value = jnp.where(next_valid == 1, value, 0.0)
-                        ref, shift = ((level.right, 0), (level.coef, 1))[which]
-                        ref[2 * odd_y + odd_z, at + x + shift, window, :] = value
+                over, beside = mid[block, odd_y, x], sib[block, odd_y, x]
+                first = jnp.where(core == 1, over, beside)
+                last = jnp.where(core == 1, beside, over)
+                side = jnp.where(low, first, last)
+                mine = own[block, 0, odd_y, x]
+                level.right[2 * odd_y, at + x, window, :] = jnp.where(is_own, mine, turn(side, bz // 2, 1))
+                level.right[2 * odd_y + 1, at + x, window, :] = jnp.where(is_own, turn(mine, bz // 2, 1), side)
+                side = jnp.where(low, last, first)
+                up, down = turn(side, quarter, 1), turn(side, -quarter, 1)
+                mine = own[block, 1, odd_y, x]
+                for odd_z in (0, 1):
+                    near = jnp.where(low, down, up) if odd_z else jnp.where(low, up, down)
+                    value = jnp.where(
+                        is_own,
+                        turn(mine, bz // 2, 1) if odd_z else mine,
+                        jnp.where(outside, 0.0, near),
+                    )
+                    if kind in (3, 5):
+                        value = jnp.where(in_the_middle(at_y), value, 0.0)
+                    level.coef[2 * odd_y + odd_z, at + x + 1, window, :] = value
             return carry
 
-        lax.fori_loop(0, bx, assemble, 0)
+        lax.fori_loop(0, bx, assemble, 0, unroll=2)
 
     def begin(i, here, inverse):
         level.from_zero(i, inverse)
@@ -489,20 +519,21 @@
     lax.fori_loop(0, level.count, copy_out, 0)
 
 
-def up_kernel(pos, pay, far, near, start, right, coef_in, solution_out, residual_out, *refs):
+def up_kernel(pay, far, near, start, right, coef_in, solution_out, residual_out, *refs):
     level1 = Level(refs[:8], True, False, 1, 0.25, UNROLL_COARSE)
     level2 = Level(refs[8:16], False, False, 2, 0.0625, UNROLL_COARSE)
     fine = Level((refs[16], right, *refs[17:23]), True, True, 1, 1.0, UNROLL_FINE)
     window, rows_out = refs[23:]
     n1, rows, bz = pay.shape[2:]
     edge = rows // 2
-    odd, upper, at_x, near_valid = (pos[k] for k in (1, 2, 3, 6))
+    at_x, at_y, _, _, odd = place()
+    upper = at_y // 2
     weights = smoothing_weights()
     for level in (level1, level2, fine):
         level.clear_ends()
 
     top = lax.broadcasted_iota(jnp.int32, (rows, bz), 0) < edge
-    near_here = (top == (odd == 0)) & (near_valid == 1)
+    near_here = (top == (odd == 0)) & in_the_middle(at_y)
     for j in range(n1):
         for which, (ref, shift) in enumerate(((level1.right, 0), (level1.coef, 1))):
             piece = near[which, j]
@@ -610,11 +641,6 @@
 def per_device_two_rounds(right_side, coefficient):
     bx, by, bz = right_side.shape
     rows = by // 2
-    at_x, at_y, at_z = (lax.axis_index(name) for name in ("gx", "gy", "gz"))
-    core = at_z % 2
-    middle_y, middle_z = ((at == 1) | (at == 2) for at in (at_y, at_z))
-    pos = jnp.stack([core, at_y % 2, at_y // 2, at_x, middle_z, middle_y, middle_y]).astype(jnp.int32)
-    in_smem = pl.BlockSpec(memory_space=pltpu.SMEM)
     in_vmem = pl.BlockSpec(memory_space=pltpu.VMEM)
     params = pltpu.CompilerParams(vmem_limit_bytes=24 * 2**20)
     shape = lambda *sizes: jax.ShapeDtypeStruct(sizes, jnp.float32)
@@ -622,12 +648,12 @@
     mine = pl.pallas_call(
         split_kernel,
         out_shape=shape(2, 2, bx, rows, bz),
-        in_specs=[in_vmem] * 2,
+        in_specs=[in_vmem],
         out_specs=in_vmem,
-        scratch_shapes=[vmem(bx * by, bz)],
+        scratch_shapes=[vmem(2, bx * by, bz)],
         compiler_params=params,
         name="split",
-    )(right_side, coefficient)
+    )(jnp.stack([right_side, coefficient]))
 
     pairs = [1, 0, 3, 2]
     inner = [0, 2, 1, 3]
@@ -636,33 +662,32 @@
     def both(partner):
         return [(4 * x + y, 4 * (1 - x) + partner[y]) for x in (0, 1) for y in range(4)]
 
-    blocks = jnp.stack(
-        [
-            mine,
-            lax.ppermute(mine, "gx", across),
-            lax.ppermute(mine, "gy", list(enumerate(pairs))),
-            lax.ppermute(mine, "gy", list(enumerate(inner))),
-            lax.ppermute(mine, ("gx", "gy"), both(pairs)),
-            lax.ppermute(mine, ("gx", "gy"), both(inner)),
-        ]
-    )
-    quarter = bz // 4
-    low_quarter = jnp.arange(bz) % (bz // 2) < quarter
-    right_blocks, coef_blocks = blocks[:, 0], blocks[:, 1]
-    packed = jnp.where(
-        core == 0,
-        jnp.where(low_quarter, right_blocks, jnp.roll(coef_blocks, quarter, axis=-1)),
-        jnp.where(low_quarter, jnp.roll(coef_blocks, -quarter, axis=-1), right_blocks),
-    )
-    mid = lax.ppermute(packed, "gz", list(enumerate(inner)))
-    sib = lax.ppermute(blocks, "gz", list(enumerate(pairs)))
+    swap_pairs, swap_inner = list(enumerate(pairs)), list(enumerate(inner))
+    other = lax.ppermute(mine, "gx", across)
+    by_pairs = lax.ppermute(mine, "gy", swap_pairs)
+    by_inner = lax.ppermute(mine, "gy", swap_inner)
+    other_pairs = lax.ppermute(mine, ("gx", "gy"), both(pairs))
+    other_inner = lax.ppermute(mine, ("gx", "gy"), both(inner))
+    blocks = (mine, other, by_pairs, by_inner, other_pairs, other_inner)
+    blocks = [blocks[kind] for kind in ORDER]
+    edges = shape(6, 2, bx, rows, bz)
+    to_mid, to_sib = pl.pallas_call(
+        pack_kernel,
+        out_shape=(edges, edges),
+        in_specs=[in_vmem] * 6,
+        out_specs=(in_vmem,) * 2,
+        compiler_params=params,
+        name="pack",
+    )(*blocks)
+    mid = lax.ppermute(to_mid, "gz", swap_inner)
+    sib = lax.ppermute(to_sib, "gz", swap_pairs)
 
     nx = 2 * bx
     window = shape(4, nx, 2 * rows, bz)
     start, right_wide, coef_wide, pay, edge = pl.pallas_call(
         down_kernel,
         out_shape=(window, window, window, shape(2, 2, bx, rows, bz), shape(2, bx, rows, bz)),
-        in_specs=[in_smem] + [in_vmem] * 3,
+        in_specs=[in_vmem] * 3,
         out_specs=(in_vmem,) * 5,
         scratch_shapes=[
             *level_scratch(4, nx, 3 * rows, bz, True),
@@ -671,13 +696,13 @@
         ],
         compiler_params=params,
         name="down",
-    )(pos, blocks, sib, mid)
+    )(jnp.stack(blocks), mid, sib)
     far = lax.ppermute(pay, "gy", [(0, 2), (2, 0), (1, 3), (3, 1)])
     near = lax.ppermute(edge, "gy", list(enumerate(pairs)))
     return pl.pallas_call(
         up_kernel,
         out_shape=(shape(bx, by, bz),) * 2,
-        in_specs=[in_smem] + [in_vmem] * 6,
+        in_specs=[in_vmem] * 6,
         out_specs=(in_vmem,) * 2,
         scratch_shapes=[
             *level_scratch(2, bx, 3 * rows, bz, True),
@@ -688,7 +713,7 @@
         ],
         compiler_params=params,
         name="up",
-    )(pos, pay, far, near, start, right_wide, coef_wide)
+    )(pay, far, near, start, right_wide, coef_wide)
 
 
 def two_rounds_fit(mesh, shape):

time: 48.3 us -> 42.8 us (0.89)
  starting transfers between devices: 16.3 us -> 13.5 us
  Pallas kernels: 15.2 us -> 12.8 us
  local copies, waits for them, and re-layouts: 2.32 us -> 0.07 us
  waiting for transfers between devices: 13.1 us -> 14.7 us
  other arithmetic: 0.28 us -> 0.88 us
    ppermute x7, starting transfers between devices: 14.9 us -> 9.85 us  [the longest x1 4.3 us: per_device_two_rounds(): mid = lax.ppermute(to_mid, 'gz', swap_inner)]
    ppermute x7, waiting for transfers between devices: 8.67 us -> 11.8 us  [the longest x1 5.27 us: per_device_two_rounds(): mid = lax.ppermute(to_mid, 'gz', swap_inner)]
    pallas_call x1, Pallas kernels: 8.24 us -> 5.94 us  [per_device_two_rounds(): pl.pallas_call(down_kernel, out_shape=(window, window, window, shape(2, 2...]
    ppermute x1, starting transfers between devices: 1 us -> 2.74 us  [per_device_two_rounds(): far = lax.ppermute(pay, 'gy', [(0, 2), (2, 0), (1, 3), (3, 1)])]
    unnamed x9 -> x5, local copies, waits for them, and re-layouts: 1.73 us -> 0.06 us
    ppermute x1, waiting for transfers between devices: 1.63 us -> 0.65 us  [per_device_two_rounds(): far = lax.ppermute(pay, 'gy', [(0, 2), (2, 0), (1, 3), (3, 1)])]
    another operation x0 -> x1, other arithmetic: none -> 0.88 us  [per_device_two_rounds(): jnp.stack([right_side, coefficient])]
    ppermute x1, waiting for transfers between devices: 2.79 us -> 2.19 us  [per_device_two_rounds(): near = lax.ppermute(edge, 'gy', list(enumerate(pairs)))]
  transfers between devices with their start and end apart: 9 -> 9, of which waited for: 4 -> 7; matrix products, arithmetic and copies ran while one was open for 2% -> 0% of each run, Pallas kernels for 0% -> 0%
where the time goes in v3:
time: 42.8 us; the launch traced here: 42.6 us
  waiting for transfers between devices  14.7 us (34%)
  starting transfers between devices  13.5 us (32%)
  Pallas kernels  12.8 us (30%)
  other arithmetic  0.88 us (2%)
  between operations  0.73 us (2%)
    pallas_call x1, Pallas kernels, per_device_two_rounds(): pl.pallas_call(up_kernel, out_shape=(shape(bx, by, bz),) * 2, in_specs=[i...  6.22 us
    pallas_call x1, Pallas kernels, per_device_two_rounds(): pl.pallas_call(down_kernel, out_shape=(window, window, window, shape(2, 2...  5.94 us
    ppermute x1, waiting for transfers between devices, per_device_two_rounds(): mid = lax.ppermute(to_mid, 'gz', swap_inner)  5.27 us
    ppermute x1, starting transfers between devices, per_device_two_rounds(): mid = lax.ppermute(to_mid, 'gz', swap_inner)  4.3 us
    ppermute x1, starting transfers between devices, per_device_two_rounds(): other_pairs = lax.ppermute(mine, ('gx', 'gy'), both(pairs))  3.12 us
    ppermute x1, waiting for transfers between devices, per_device_two_rounds(): other = lax.ppermute(mine, 'gx', across)  2.81 us
    ppermute x1, starting transfers between devices, per_device_two_rounds(): far = lax.ppermute(pay, 'gy', [(0, 2), (2, 0), (1, 3), (3, 1)])  2.74 us
    ppermute x1, waiting for transfers between devices, per_device_two_rounds(): by_pairs = lax.ppermute(mine, 'gy', swap_pairs)  2.65 us
  transfers between devices with their start and end apart: 9, of which 7 were waited for; matrix products, arithmetic and copies ran while one was open for 0% of the time, Pallas kernels for 0%

profile of v3, /device:TPU:1, one launch (start us, length us, event | category | flops | bytes accessed | tf_op | source)
XLA Modules:
  0.0 42.6 jit_solution(939873082906366862)
XLA Ops:
  0.6 0.9 %pad_maximum_fusion.fields = f32[2,8,16,128]{3,2,1,0:T(8,128)S(1)} fusion(f32[1,8,16,128]{3,2,1,0:T(8,128)} %bitcast.14, f32[1,8,16,128]{3,2,1,0:T(8,128)} %bitcast.15), kind=kLoop, calls=%fused_computation | loop fusion | flops 32768 | bytes 262144 | tf_op jit(solution)/shard_map/stack | solution.py:656
  1.5 0.3 split.1.refs_0_
  1.8 3.1 %collective-permute-start.4 = (f32[2,2,8,8,128]{4,3,2,1,0:T(8,128)S(1)}, f32[2,2,8,8,128]{4,3,2,1,0:T(8,128)S(1)}, u32[]{:S(2)}, u32[]{:S(2)}) collective-permute-start(f32[2,2,8,8,128]{4,3,2,1,0:T(8,128)S(1)} %split.1.refs_0_), channel_id=1, source_target_pairs={{0,20},{4,16},{8,28},{12,24},{16,4},{20,0},{24,12},{28,8},{1,21},{... | collective-permute-start | bytes 393224 | tf_op jit(solution)/shard_map/ppermute | solution.py:669
  4.9 0.2 collective-permute-start.3
  5.1 0.2 collective-permute-start.2
  5.3 0.7 %collective-permute-start.1 = (f32[2,2,8,8,128]{4,3,2,1,0:T(8,128)S(1)}, f32[2,2,8,8,128]{4,3,2,1,0:T(8,128)S(1)}, u32[]{:S(2)}, u32[]{:S(2)}) collective-permute-start(f32[2,2,8,8,128]{4,3,2,1,0:T(8,128)S(1)} %split.1.refs_0_), channel_id=1, source_target_pairs={{0,0},{4,8},{8,4},{12,12},{1,1},{5,9},{9,5},{13,13},{2,2},{6,10},{... | collective-permute-start | bytes 393224 | tf_op jit(solution)/shard_map/ppermute | solution.py:668
  5.9 1.3 %collective-permute-start = (f32[2,2,8,8,128]{4,3,2,1,0:T(8,128)S(1)}, f32[2,2,8,8,128]{4,3,2,1,0:T(8,128)S(1)}, u32[]{:S(2)}, u32[]{:S(2)}) collective-permute-start(f32[2,2,8,8,128]{4,3,2,1,0:T(8,128)S(1)} %split.1.refs_0_), channel_id=1, source_target_pairs={{0,16},{16,0},{1,17},{17,1},{2,18},{18,2},{3,19},{19,3},{4,20},{20... | collective-permute-start | bytes 393224 | tf_op jit(solution)/shard_map/ppermute | solution.py:666
  7.3 0.8 %collective-permute-done.4.refs_5_ = f32[2,2,8,8,128]{4,3,2,1,0:T(8,128)S(1)} collective-permute-done((f32[2,2,8,8,128]{4,3,2,1,0:T(8,128)S(1)}, f32[2,2,8,8,128]{4,3,2,1,0:T(8,128)S(1)}, u32[]{:S(2)}, u32[]{:S(2)}) %collective-permute-start.4) | collective-permute-done | bytes 131104 | tf_op jit(solution)/shard_map/ppermute | solution.py:669
  8.1 2.7 %collective-permute-done.3.refs_4_ = f32[2,2,8,8,128]{4,3,2,1,0:T(8,128)S(1)} collective-permute-done((f32[2,2,8,8,128]{4,3,2,1,0:T(8,128)S(1)}, f32[2,2,8,8,128]{4,3,2,1,0:T(8,128)S(1)}, u32[]{:S(2)}, u32[]{:S(2)}) %collective-permute-start.3) | collective-permute-done | bytes 131104 | tf_op jit(solution)/shard_map/ppermute | solution.py:667
  10.8 0.2 collective-permute-done.2.refs_3_
  11.0 0.0 collective-permute-done.1.refs_2_
  11.0 2.8 %collective-permute-done.refs_1_ = f32[2,2,8,8,128]{4,3,2,1,0:T(8,128)S(1)} collective-permute-done((f32[2,2,8,8,128]{4,3,2,1,0:T(8,128)S(1)}, f32[2,2,8,8,128]{4,3,2,1,0:T(8,128)S(1)}, u32[]{:S(2)}, u32[]{:S(2)}) %collective-permute-start) | collective-permute-done | bytes 131104 | tf_op jit(solution)/shard_map/ppermute | solution.py:666
  13.9 0.3 pack.1
  14.2 4.3 %collective-permute-start.5 = (f32[6,2,8,8,128]{4,3,2,1,0:T(8,128)S(1)}, f32[6,2,8,8,128]{4,3,2,1,0:T(8,128)S(1)}, u32[]{:S(2)}, u32[]{:S(2)}) collective-permute-start(f32[6,2,8,8,128]{4,3,2,1,0:T(8,128)S(1)} %get-tuple-element.9), channel_id=1, source_target_pairs={{0,0},{1,2},{2,1},{3,3},{4,4},{5,6},{6,5},{7,7},{8,8},{9,10},{10,9... | collective-permute-start | bytes 1179656 | tf_op jit(solution)/shard_map/ppermute | solution.py:682
  18.5 0.1 collective-permute-start.6
  18.7 5.3 %collective-permute-done.5.mid = f32[6,2,8,8,128]{4,3,2,1,0:T(8,128)S(1)} collective-permute-done((f32[6,2,8,8,128]{4,3,2,1,0:T(8,128)S(1)}, f32[6,2,8,8,128]{4,3,2,1,0:T(8,128)S(1)}, u32[]{:S(2)}, u32[]{:S(2)}) %collective-permute-start.5) | collective-permute-done | bytes 393248 | tf_op jit(solution)/shard_map/ppermute | solution.py:682
  24.0 0.0 collective-permute-done.6.sib
  24.0 5.9 %down.1 = (f32[4,16,16,128]{3,2,1,0:T(8,128)S(1)}, f32[4,16,16,128]{3,2,1,0:T(8,128)S(1)}, f32[4,16,16,128]{3,2,1,0:T(8,128)S(1)}, f32[2,2,8,8,128]{4,3,2,1,0:T(8,128)S(1)}, f32[2,8,8,128]{3,2,1,0:T(8,128)S(1)}) custom-call(f32[6,2,2,8,8,128]{5,4,3,2,1,0:T(8,128)S(1)} %bitcast_dynamic-update-slice_fusion.own, ...), custom_call_target="tpu_custom_call" | custom-call | tf_op jit(solution)/shard_map/down/pallas_call | solution.py:687
  29.9 2.7 %collective-permute-start.7 = (f32[2,2,8,8,128]{4,3,2,1,0:T(8,128)S(1)}, f32[2,2,8,8,128]{4,3,2,1,0:T(8,128)S(1)}, u32[]{:S(2)}, u32[]{:S(2)}) collective-permute-start(f32[2,2,8,8,128]{4,3,2,1,0:T(8,128)S(1)} %get-tuple-element.11.pay), channel_id=1, source_target_pairs={{0,8},{8,0},{4,12},{12,4},{1,9},{9,1},{5,13},{13,5},{2,10},{10,2},... | collective-permute-start | bytes 393224 | tf_op jit(solution)/shard_map/ppermute | solution.py:700
  32.7 0.9 %collective-permute-start.8 = (f32[2,8,8,128]{3,2,1,0:T(8,128)S(1)}, f32[2,8,8,128]{3,2,1,0:T(8,128)S(1)}, u32[]{:S(2)}, u32[]{:S(2)}) collective-permute-start(f32[2,8,8,128]{3,2,1,0:T(8,128)S(1)} %get-tuple-element.12), channel_id=1, source_target_pairs={{0,4},{4,0},{8,12},{12,8},{1,5},{5,1},{9,13},{13,9},{2,6},{6,2},{1... | collective-permute-start | bytes 196616 | tf_op jit(solution)/shard_map/ppermute | solution.py:701
  33.6 2.2 %collective-permute-done.8.near = f32[2,8,8,128]{3,2,1,0:T(8,128)S(1)} collective-permute-done((f32[2,8,8,128]{3,2,1,0:T(8,128)S(1)}, f32[2,8,8,128]{3,2,1,0:T(8,128)S(1)}, u32[]{:S(2)}, u32[]{:S(2)}) %collective-permute-start.8) | collective-permute-done | bytes 65568 | tf_op jit(solution)/shard_map/ppermute | solution.py:701
  35.8 0.6 %collective-permute-done.7.far = f32[2,2,8,8,128]{4,3,2,1,0:T(8,128)S(1)} collective-permute-done((f32[2,2,8,8,128]{4,3,2,1,0:T(8,128)S(1)}, f32[2,2,8,8,128]{4,3,2,1,0:T(8,128)S(1)}, u32[]{:S(2)}, u32[]{:S(2)}) %collective-permute-start.7) | collective-permute-done | bytes 131104 | tf_op jit(solution)/shard_map/ppermute | solution.py:700
  36.4 6.2 %up.1 = (f32[8,16,128]{2,1,0:T(8,128)}, f32[8,16,128]{2,1,0:T(8,128)}) custom-call(f32[2,2,8,8,128]{4,3,2,1,0:T(8,128)S(1)} %get-tuple-element.11.pay, f32[2,2,8,8,128]{4,3,2,1,0:T(8,128)S(1)} %collective-permute-done.7.far, f32[2,8,8,128]{3,2,1,0:T(8,128)S(1)} %collective-permute-done.8.near, f32[4,16,16,128]{3,2,1,0:T(8,128)S(1)} %get-tuple-element.13.start, ...), custom_call_target="tpu_custom_call" | custom-call | tf_op jit(solution)/shard_map/up/pallas_call | solution.py:702
  (6 shorter events, 0.1 us)
Async XLA Ops:
  1.8 6.3 %collective-permute-start.4 = (f32[2,2,8,8,128]{4,3,2,1,0:T(8,128)S(1)}, f32[2,2,8,8,128]{4,3,2,1,0:T(8,128)S(1)}, u32[]{:S(2)}, u32[]{:S(2)}) collective-permute-start(f32[2,2,8,8,128]{4,3,2,1,0:T(8,128)S(1)} %split.1.refs_0_), channel_id=1, source_target_pairs={{0,20},{4,16},{8,28},{12,24},{16,4},{20,0},{24,12},{28,8},{1,21},{... | collective-permute-start | bytes 393224 | tf_op jit(solution)/shard_map/ppermute | solution.py:669
  4.9 5.9 %collective-permute-start.3 = (f32[2,2,8,8,128]{4,3,2,1,0:T(8,128)S(1)}, f32[2,2,8,8,128]{4,3,2,1,0:T(8,128)S(1)}, u32[]{:S(2)}, u32[]{:S(2)}) collective-permute-start(f32[2,2,8,8,128]{4,3,2,1,0:T(8,128)S(1)} %split.1.refs_0_), channel_id=1, source_target_pairs={{0,4},{4,0},{8,12},{12,8},{1,5},{5,1},{9,13},{13,9},{2,6},{6,2},{1... | collective-permute-start | bytes 393224 | tf_op jit(solution)/shard_map/ppermute | solution.py:667
  5.1 6.0 %collective-permute-start.2 = (f32[2,2,8,8,128]{4,3,2,1,0:T(8,128)S(1)}, f32[2,2,8,8,128]{4,3,2,1,0:T(8,128)S(1)}, u32[]{:S(2)}, u32[]{:S(2)}) collective-permute-start(f32[2,2,8,8,128]{4,3,2,1,0:T(8,128)S(1)} %split.1.refs_0_), channel_id=1, source_target_pairs={{0,16},{4,24},{8,20},{12,28},{16,0},{20,8},{24,4},{28,12},{1,17},{... | collective-permute-start | bytes 393224 | tf_op jit(solution)/shard_map/ppermute | solution.py:670
  5.3 5.8 %collective-permute-start.1 = (f32[2,2,8,8,128]{4,3,2,1,0:T(8,128)S(1)}, f32[2,2,8,8,128]{4,3,2,1,0:T(8,128)S(1)}, u32[]{:S(2)}, u32[]{:S(2)}) collective-permute-start(f32[2,2,8,8,128]{4,3,2,1,0:T(8,128)S(1)} %split.1.refs_0_), channel_id=1, source_target_pairs={{0,0},{4,8},{8,4},{12,12},{1,1},{5,9},{9,5},{13,13},{2,2},{6,10},{... | collective-permute-start | bytes 393224 | tf_op jit(solution)/shard_map/ppermute | solution.py:668
  5.9 7.9 %collective-permute-start = (f32[2,2,8,8,128]{4,3,2,1,0:T(8,128)S(1)}, f32[2,2,8,8,128]{4,3,2,1,0:T(8,128)S(1)}, u32[]{:S(2)}, u32[]{:S(2)}) collective-permute-start(f32[2,2,8,8,128]{4,3,2,1,0:T(8,128)S(1)} %split.1.refs_0_), channel_id=1, source_target_pairs={{0,16},{16,0},{1,17},{17,1},{2,18},{18,2},{3,19},{19,3},{4,20},{20... | collective-permute-start | bytes 393224 | tf_op jit(solution)/shard_map/ppermute | solution.py:666
  14.2 9.8 %collective-permute-start.5 = (f32[6,2,8,8,128]{4,3,2,1,0:T(8,128)S(1)}, f32[6,2,8,8,128]{4,3,2,1,0:T(8,128)S(1)}, u32[]{:S(2)}, u32[]{:S(2)}) collective-permute-start(f32[6,2,8,8,128]{4,3,2,1,0:T(8,128)S(1)} %get-tuple-element.9), channel_id=1, source_target_pairs={{0,0},{1,2},{2,1},{3,3},{4,4},{5,6},{6,5},{7,7},{8,8},{9,10},{10,9... | collective-permute-start | bytes 1179656 | tf_op jit(solution)/shard_map/ppermute | solution.py:682
  18.5 5.4 %collective-permute-start.6 = (f32[6,2,8,8,128]{4,3,2,1,0:T(8,128)S(1)}, f32[6,2,8,8,128]{4,3,2,1,0:T(8,128)S(1)}, u32[]{:S(2)}, u32[]{:S(2)}) collective-permute-start(f32[6,2,8,8,128]{4,3,2,1,0:T(8,128)S(1)} %get-tuple-element.10), channel_id=1, source_target_pairs={{0,1},{1,0},{2,3},{3,2},{4,5},{5,4},{6,7},{7,6},{8,9},{9,8},{10,11... | collective-permute-start | bytes 1179656 | tf_op jit(solution)/shard_map/ppermute | solution.py:683
  29.9 6.5 %collective-permute-start.7 = (f32[2,2,8,8,128]{4,3,2,1,0:T(8,128)S(1)}, f32[2,2,8,8,128]{4,3,2,1,0:T(8,128)S(1)}, u32[]{:S(2)}, u32[]{:S(2)}) collective-permute-start(f32[2,2,8,8,128]{4,3,2,1,0:T(8,128)S(1)} %get-tuple-element.11.pay), channel_id=1, source_target_pairs={{0,8},{8,0},{4,12},{12,4},{1,9},{9,1},{5,13},{13,5},{2,10},{10,2},... | collective-permute-start | bytes 393224 | tf_op jit(solution)/shard_map/ppermute | solution.py:700
  32.7 3.1 %collective-permute-start.8 = (f32[2,8,8,128]{3,2,1,0:T(8,128)S(1)}, f32[2,8,8,128]{3,2,1,0:T(8,128)S(1)}, u32[]{:S(2)}, u32[]{:S(2)}) collective-permute-start(f32[2,8,8,128]{3,2,1,0:T(8,128)S(1)} %get-tuple-element.12), channel_id=1, source_target_pairs={{0,4},{4,0},{8,12},{12,8},{1,5},{5,1},{9,13},{13,9},{2,6},{6,2},{1... | collective-permute-start | bytes 196616 | tf_op jit(solution)/shard_map/ppermute | solution.py:701

commit v4 on v0

--- a/solution.py
+++ b/solution.py
@@ -1,6 +1,8 @@
 import jax
 import jax.numpy as jnp
 from jax import lax
+from jax.experimental import pallas as pl
+from jax.experimental.pallas import tpu as pltpu
 from jax.sharding import PartitionSpec as P
 
 LEVELS = 3
@@ -206,9 +208,531 @@
     return (solution, residual)
 
 
+UNROLL_FINE = 20
+UNROLL_COARSE = 64
+
+
+def place():
+    at_x, at_y, at_z = (lax.axis_index(name) for name in ("gx", "gy", "gz"))
+    return at_x, at_y, at_z, lax.rem(at_z, 2), lax.rem(at_y, 2)
+
+
+def in_the_middle(at):
+    return (at == 1) | (at == 2)
+
+
+def smoothing_weights():
+    centre = 0.5 * (cheb_high + cheb_low)
+    half_width = 0.5 * (cheb_high - cheb_low)
+    sigma_val = centre / half_width
+    rho_now = 1.0 / sigma_val
+    weights = [(0.0, 1.0 / centre)]
+    for _ in range(DEGREE - 1):
+        rho_next = 1.0 / (2.0 * sigma_val - rho_now)
+        weights.append((rho_next * rho_now, 2.0 * rho_next / half_width))
+        rho_now = rho_next
+    return weights
+
+
+def turn(values, shift, axis):
+    return pltpu.roll(values, shift % values.shape[axis], axis)
+
+
+def run(low, high, body, carry, unroll):
+    count = high - low
+    steps = -(-count // unroll)
+    unroll = -(-count // steps)
+
+    def several(start, state, rows):
+        pending = []
+        for k in range(rows):
+            state, stores = body(start + k, state)
+            pending += stores
+        for ref, i, values in pending:
+            for part, value in enumerate(values):
+                ref[part, i] = value
+        return state
+
+    whole = count // unroll
+    if whole == 1:
+        carry = several(low, carry, unroll)
+    else:
+        carry = lax.fori_loop(0, whole, lambda step, state: several(low + step * unroll, state, unroll), carry)
+    if count > whole * unroll:
+        carry = several(low + whole * unroll, carry, count - whole * unroll)
+    return carry
+
+
+def tile_place(shape, axis):
+    return lax.broadcasted_iota(jnp.int32, shape, axis)
+
+
+class Level:
+    def __init__(self, refs, split, step, scale, unroll):
+        self.coef, self.right, self.face_x, self.face_y, self.face_z, self.edge_x, self.inverse, self.values, self.update = refs
+        self.parts, self.rows = self.inverse.shape[:2]
+        self.tile = self.inverse.shape[2:]
+        self.split, self.step, self.half, self.unroll = split, step, 0.5 * scale, unroll
+        self.first = tile_place(self.tile, 0) < step
+        self.last = tile_place(self.tile, 0) >= self.tile[0] - step
+
+    def read(self, ref, i):
+        return [ref[part, i] for part in range(ref.shape[0])]
+
+    def clear_ends(self):
+        for ref in (self.coef, self.values):
+            for part in range(self.parts):
+                for i in (0, self.rows - 1):
+                    ref[part, i] = jnp.zeros(self.tile, jnp.float32)
+
+    def next_x(self, v, part):
+        if self.split and part < 2:
+            return v[part + 2]
+        return jnp.where(self.last, 0.0, turn(v[part - 2 if self.split else part], -self.step, 0))
+
+    def last_x(self, v, part, at_edge):
+        if self.split and part >= 2:
+            return v[part - 2]
+        return jnp.where(self.first, at_edge[part], turn(v[part + 2 if self.split else part], self.step, 0))
+
+    def next_z(self, v, part):
+        if self.split and part % 2 == 0:
+            return v[part + 1]
+        return turn(v[part - 1 if self.split else part], -self.step, 1)
+
+    def last_z(self, v, part):
+        if self.split and part % 2 == 1:
+            return v[part - 1]
+        return turn(v[part + 1 if self.split else part], self.step, 1)
+
+    def set_faces(self, use):
+        half = self.half
+        parts = range(self.parts)
+
+        def body(i, carry):
+            here, below = carry
+            above = self.read(self.coef, i + 1)
+            upper = [half * (here[p] + above[p]) for p in parts]
+            along_x = [half * (here[p] + self.next_x(here, p)) for p in parts]
+            along_z = [half * (here[p] + self.next_z(here, p)) for p in parts]
+            edge = [half * here[p] for p in range(self.edge_x.shape[0])]
+            inverse = []
+            for p in parts:
+                diagonal = (
+                    (below[p] + upper[p])
+                    + (along_x[p] + self.last_x(along_x, p, edge))
+                    + (along_z[p] + self.last_z(along_z, p))
+                )
+                inside = here[p] > 0.0
+                inverse.append(jnp.where(inside, 1.0 / jnp.where(inside, diagonal, 1.0), 0.0))
+            stores = [
+                (self.face_y, i, upper),
+                (self.face_x, i, along_x),
+                (self.face_z, i, along_z),
+                (self.edge_x, i, edge),
+                (self.inverse, i, inverse),
+            ]
+            return (above, upper), stores + use(i, here, inverse)
+
+        here, before = self.read(self.coef, 1), self.read(self.coef, 0)
+        face = [half * (here[p] + before[p]) for p in parts]
+        for p in parts:
+            self.face_y[p, 0] = face[p]
+        run(1, self.rows - 1, body, (here, face), self.unroll)
+
+    def sweep(self, low, high, use):
+        parts = range(self.parts)
+
+        def body(i, carry):
+            here, flux_low = carry
+            above = self.read(self.values, i + 1)
+            face_x, face_y, face_z, edge_x = (
+                self.read(ref, i) for ref in (self.face_x, self.face_y, self.face_z, self.edge_x)
+            )
+            flux_high = [face_y[p] * (above[p] - here[p]) for p in parts]
+            flux_x = [face_x[p] * (self.next_x(here, p) - here[p]) for p in parts]
+            flux_z = [face_z[p] * (self.next_z(here, p) - here[p]) for p in parts]
+            at_edge = [face * value for face, value in zip(edge_x, here)]
+            applied = [
+                (flux_low[p] - flux_high[p])
+                + (self.last_x(flux_x, p, at_edge) - flux_x[p])
+                + (self.last_z(flux_z, p) - flux_z[p])
+                for p in parts
+            ]
+            return (above, flux_high), use(i, applied, here)
+
+        here, before = self.read(self.values, low), self.read(self.values, low - 1)
+        face = self.read(self.face_y, low - 1)
+        run(low, high, body, (here, [face[p] * (here[p] - before[p]) for p in parts]), self.unroll)
+
+    def from_zero(self, i, inverse):
+        first = smoothing_weights()[0][1]
+        right = self.read(self.right, i)
+        step = [right[p] * (inverse[p] * first) for p in range(self.parts)]
+        return [(self.update, i, step), (self.values, i, step)]
+
+    def smooth(self, low, high, weight):
+        keep, gain = weight
+
+        def use(i, applied, here):
+            right = self.read(self.right, i)
+            inverse = self.read(self.inverse, i)
+            step = [(right[p] - applied[p]) * (inverse[p] * gain) for p in range(self.parts)]
+            if keep:
+                update = self.read(self.update, i)
+                step = [keep * update[p] + step[p] for p in range(self.parts)]
+            return [(self.update, i, step), (self.values, i, [here[p] + step[p] for p in range(self.parts)])]
+
+        self.sweep(low, high, use)
+
+
+def total(items):
+    items = list(items)
+    while len(items) > 1:
+        items = [sum(items[k : k + 2][1:], items[k]) for k in range(0, len(items), 2)]
+    return items[0]
+
+
+def exact_dot(left, right):
+    return jnp.dot(left, right, precision=lax.Precision.HIGHEST, preferred_element_type=jnp.float32)
+
+
+def parity_matrix(size, back):
+    row, column = tile_place((size, size), 0), tile_place((size, size), 1)
+    if back:
+        row, column = column, row
+    hit = column == row // 2 + (row % 2) * (size // 2)
+    return jnp.where(hit, 1.0, 0.0).astype(jnp.float32)
+
+
+def parity_place(x, count):
+    return x // 2 + (x % 2) * (count // 2)
+
+
+def halo_rows(by):
+    return 2 * (by // 4) + DEGREE + 1
+
+
+def split_kernel(fields, out, pair_out, inner_out, rows):
+    _, bx, by, bz = fields.shape
+    _, _, _, _, odd = place()
+    halo = halo_rows(by)
+    matrix = parity_matrix(bz, False)
+    for which in (0, 1):
+        moved = exact_dot(fields[which].reshape(bx * by, bz), matrix)
+        for x in range(bx):
+            at = parity_place(x, bx) * by
+            rows[which, at : at + by] = moved[x * by : (x + 1) * by]
+        for y in range(by):
+            out[which, y] = rows[which, pl.ds(y, bx, stride=by), :]
+    for which in (0, 1):
+        pair_out[which] = out[which, pl.ds((1 - odd) * (by - halo), halo)]
+        inner_out[which] = out[which, pl.ds(odd * (by - halo), halo)]
+
+
+def pack_kernel(*refs):
+    *blocks, across_out, beside_out = refs
+    _, _, _, core, _ = place()
+    tile = across_out.shape[1:]
+    quarter = tile[1] // 4
+    low = tile_place(tile, 1) % (2 * quarter) < quarter
+    at = 0
+    for block in blocks:
+        for y in range(block.shape[1]):
+            right, coef = block[0, y], block[1, y]
+            first = jnp.where(low, right, turn(coef, quarter, 1))
+            last = jnp.where(low, turn(coef, -quarter, 1), right)
+            across_out[at] = jnp.where(core == 0, first, last)
+            beside_out[at] = jnp.where(core == 0, last, first)
+            at += 1
+
+
+def down_kernel(mine, other, pair, pair_other, inner, inner_other, mid, sib, *refs):
+    right, face_x, face_y, face_z, edge_x, inverse, values, pay_out, near_out, coef, update, sums, coefs = refs
+    level = Level((coef, right, face_x, face_y, face_z, edge_x, inverse, values, update), True, 1, 1.0, UNROLL_FINE)
+    by, bx, bz = mine.shape[1:]
+    halo = pair.shape[1]
+    at_x, at_y, at_z, core, odd = place()
+    tile = (bx, bz)
+    lane = tile_place(tile, 1)
+    quarter = bz // 4
+    is_own = lane < bz // 2
+    low = lane % (bz // 2) < quarter
+    outside = (low == (core == 1)) & ~in_the_middle(at_z)
+    top = tile_place(tile, 0) < bx // 2
+
+    def columns(block, y, at):
+        over, beside = mid[at], sib[at]
+        first = jnp.where(core == 1, over, beside)
+        last = jnp.where(core == 1, beside, over)
+        side, own = jnp.where(low, first, last), block[0, y]
+        right_cells = [
+            jnp.where(is_own, own, turn(side, bz // 2, 1)),
+            jnp.where(is_own, turn(own, bz // 2, 1), side),
+        ]
+        side, own = jnp.where(low, last, first), block[1, y]
+        up, down = turn(side, quarter, 1), turn(side, -quarter, 1)
+        coef_cells = [
+            jnp.where(is_own, own, jnp.where(outside, 0.0, jnp.where(low, up, down))),
+            jnp.where(is_own, turn(own, bz // 2, 1), jnp.where(outside, 0.0, jnp.where(low, down, up))),
+        ]
+        return right_cells, coef_cells
+
+    at = 0
+    for near, far, row in (
+        (mine, other, halo),
+        (pair, pair_other, (1 - odd) * (halo + by)),
+        (inner, inner_other, odd * (halo + by)),
+    ):
+        count = near.shape[1]
+
+        def assemble(y, carry, near=near, far=far, row=row, at=at, count=count):
+            both = zip(columns(near, y, at + y), columns(far, y, at + count + y))
+            stores = []
+            for ref, (here, there) in zip((right, coef), both):
+                for odd_z in (0, 1):
+                    one = jnp.where(at_x == 0, here[odd_z], there[odd_z])
+                    two = jnp.where(at_x == 0, there[odd_z], here[odd_z])
+                    cells = jnp.where(top, one, turn(two, bx // 2, 0)), jnp.where(top, turn(one, bx // 2, 0), two)
+                    for odd_x in (0, 1):
+                        value = cells[odd_x]
+                        if ref is coef and near is inner:
+                            value = jnp.where(in_the_middle(at_y), value, 0.0)
+                        stores.append((ref.at[pl.ds(2 * odd_x + odd_z, 1)], row + y, [value]))
+            return carry, stores
+
+        run(0, count, assemble, 0, 4)
+        at += 2 * count
+
+    def begin(i, here, inverse):
+        return level.from_zero(i, inverse) + [(coefs, i, [total(here)])]
+
+    level.set_faces(begin)
+    edge = 1
+    for weight in smoothing_weights()[1:]:
+        edge += 1
+        level.smooth(edge, level.rows - edge, weight)
+
+    def leftover(i, applied, here):
+        right = level.read(level.right, i)
+        return [(sums, i, [total(right[p] - applied[p] for p in range(level.parts))])]
+
+    edge += 1
+    level.sweep(edge, level.rows - edge, leftover)
+    for which, ref in enumerate((sums, coefs)):
+        for y in range(by):
+            pay_out[which, y] = 0.125 * (ref[0, edge + 2 * y] + ref[0, edge + 2 * y + 1])
+        shared = by // 4
+        near_out[which] = pay_out[which, pl.ds(shared + odd * (by - 3 * shared), shared)]
+
+
+def up_kernel(pay, far, near, right, face_x, face_y, face_z, edge_x, inverse, start, solution_out, residual_out, *refs):
+    level1 = Level(refs[:9], False, 1, 0.25, UNROLL_COARSE)
+    level2 = Level(refs[9:18], False, 2, 0.0625, UNROLL_COARSE)
+    values, update, sums, moved, rows_out = refs[18:]
+    fine = Level((None, right, face_x, face_y, face_z, edge_x, inverse, values, update), True, 1, 1.0, UNROLL_FINE)
+    by, bx, bz = pay.shape[1:]
+    shared = near.shape[1]
+    at_x, at_y, _, _, odd = place()
+    upper = at_y // 2
+    weights = smoothing_weights()
+    tile = (bx, bz)
+    level1.clear_ends()
+    level2.clear_ends()
+
+    for which, ref in enumerate((level1.right, level1.coef)):
+        for y in range(by):
+            one, two = pay[which, y], far[which, y]
+            ref[0, 1 + shared * odd + y] = jnp.where(upper == 1, two, one)
+            ref[0, 1 + by + shared * odd + y] = jnp.where(upper == 1, one, two)
+        for y in range(shared):
+            ref[0, 1 + 2 * by * (1 - odd) + y] = jnp.where(in_the_middle(at_y), near[which, y], 0.0)
+
+    n1 = level1.rows - 1
+    n2 = level2.rows - 1
+    even_lane = tile_place(tile, 1) % 2 == 0
+    even_row = tile_place(tile, 0) % 2 == 0
+
+    def pair_cells(values):
+        values = values + jnp.where(even_lane, turn(values, -1, 1), turn(values, 1, 1))
+        return 0.125 * (values + jnp.where(even_row, turn(values, -1, 0), turn(values, 1, 0)))
+
+    level1.set_faces(lambda i, here, inverse: level1.from_zero(i, inverse))
+    for weight in weights[1:]:
+        level1.smooth(1, n1, weight)
+
+    def leftover1(i, applied, here):
+        return [(sums, i, [level1.right[0, i] - applied[0]])]
+
+    level1.sweep(1, n1, leftover1)
+    for j in range(1, n2):
+        level2.right[0, j] = pair_cells(sums[0, 2 * j - 1] + sums[0, 2 * j])
+        level2.coef[0, j] = pair_cells(level1.coef[0, 2 * j - 1] + level1.coef[0, 2 * j])
+
+    level2.set_faces(lambda i, here, inverse: level2.from_zero(i, inverse))
+    for weight in weights[1:]:
+        level2.smooth(1, n2, weight)
+
+    for j in range(1, n1):
+        level1.values[0, j] = level1.values[0, j] + level2.values[0, (j + 1) // 2]
+    for weight in weights:
+        level1.smooth(1, n1, weight)
+
+    halo = (fine.rows - by) // 2
+    reach = DEGREE + 1
+    base = 1 + (by // 2) * at_y + shared * (1 - odd)
+    for y in range(-reach, by + reach):
+        coarse = level1.values[0, base + y // 2]
+        for part in range(fine.parts):
+            values[part, halo + y] = start[part, halo + y] + coarse
+    for weight in weights:
+        reach -= 1
+        fine.smooth(halo - reach, halo + by + reach, weight)
+
+    own_lane = tile_place(tile, 1) < bz // 2
+    top = tile_place(tile, 0) < bx // 2
+
+    def finish(i, applied, here):
+        right_row = fine.read(right, i)
+        stores = []
+        for slot, field in enumerate((here, [right_row[p] - applied[p] for p in range(fine.parts)])):
+            cells = []
+            for odd_z in (0, 1):
+                one, two = field[odd_z], field[2 + odd_z]
+                cells.append(
+                    jnp.where(
+                        top,
+                        jnp.where(at_x == 0, one, turn(one, bx // 2, 0)),
+                        jnp.where(at_x == 0, turn(two, bx // 2, 0), two),
+                    )
+                )
+            stores.append((rows_out.at[pl.ds(slot, 1)], i - halo, [jnp.where(own_lane, cells[0], turn(cells[1], bz // 2, 1))]))
+        return stores
+
+    fine.sweep(halo, halo + by, finish)
+    matrix = parity_matrix(bz, True)
+    for slot, ref in enumerate((solution_out, residual_out)):
+        moved[slot] = exact_dot(rows_out[slot].reshape(by * bx, bz), matrix)
+        for x in range(bx):
+            ref[x] = moved[slot, pl.ds(parity_place(x, bx), by, stride=bx), :]
+
+
+def vmem(*shape):
+    return pltpu.VMEM(shape, jnp.float32)
+
+
+def per_device_two_rounds(right_side, coefficient):
+    bx, by, bz = right_side.shape
+    halo = halo_rows(by)
+    shared = by // 4
+    in_vmem = pl.BlockSpec(memory_space=pltpu.VMEM)
+    params = pltpu.CompilerParams(vmem_limit_bytes=24 * 2**20)
+    shape = lambda *sizes: jax.ShapeDtypeStruct(sizes, jnp.float32)
+
+    mine, for_pair, for_inner = pl.pallas_call(
+        split_kernel,
+        out_shape=(shape(2, by, bx, bz), shape(2, halo, bx, bz), shape(2, halo, bx, bz)),
+        in_specs=[in_vmem],
+        out_specs=(in_vmem,) * 3,
+        scratch_shapes=[vmem(2, bx * by, bz)],
+        compiler_params=params,
+        name="split",
+    )(jnp.stack([right_side, coefficient]))
+
+    pairs = [1, 0, 3, 2]
+    inner = [0, 2, 1, 3]
+    swap_pairs, swap_inner = list(enumerate(pairs)), list(enumerate(inner))
+
+    def across_x(partner):
+        return [(4 * x + y, 4 * (1 - x) + partner[y]) for x in (0, 1) for y in range(4)]
+
+    blocks = {
+        "mine": mine,
+        "other": lax.ppermute(mine, "gx", [(0, 1), (1, 0)]),
+        "pair": lax.ppermute(for_pair, "gy", swap_pairs),
+        "pair_other": lax.ppermute(for_pair, ("gx", "gy"), across_x(pairs)),
+        "inner": lax.ppermute(for_inner, "gy", swap_inner),
+        "inner_other": lax.ppermute(for_inner, ("gx", "gy"), across_x(inner)),
+    }
+    blocks = list(blocks.values())
+    edges = shape(2 * by + 4 * halo, bx, bz)
+    to_mid, to_sib = pl.pallas_call(
+        pack_kernel,
+        out_shape=(edges, edges),
+        in_specs=[in_vmem] * 6,
+        out_specs=(in_vmem,) * 2,
+        compiler_params=params,
+        name="pack",
+    )(*blocks)
+    mid = lax.ppermute(to_mid, "gz", swap_inner)
+    sib = lax.ppermute(to_sib, "gz", swap_pairs)
+
+    rows = by + 2 * halo
+    field, half_field = (4, rows, bx, bz), (2, rows, bx, bz)
+    *fine, pay, near = pl.pallas_call(
+        down_kernel,
+        out_shape=(
+            *(shape(*(half_field if number == 4 else field)) for number in range(7)),
+            shape(2, by, bx, bz),
+            shape(2, shared, bx, bz),
+        ),
+        in_specs=[in_vmem] * 8,
+        out_specs=(in_vmem,) * 9,
+        scratch_shapes=[vmem(*field), vmem(*field), vmem(1, rows, bx, bz), vmem(1, rows, bx, bz)],
+        compiler_params=params,
+        name="down",
+    )(*blocks, mid, sib)
+    far = lax.ppermute(pay, "gy", [(0, 2), (2, 0), (1, 3), (3, 1)])
+    near = lax.ppermute(near, "gy", swap_pairs)
+    rows1 = 2 * by + shared + 2
+    return pl.pallas_call(
+        up_kernel,
+        out_shape=(shape(bx, by, bz),) * 2,
+        in_specs=[in_vmem] * 10,
+        out_specs=(in_vmem,) * 2,
+        scratch_shapes=[
+            *[vmem(1, rows1, bx, bz)] * 9,
+            *[vmem(1, rows1 // 2 + 1, bx, bz)] * 9,
+            vmem(*field),
+            vmem(*field),
+            vmem(1, rows1, bx, bz),
+            vmem(2, bx * by, bz),
+            vmem(2, by, bx, bz),
+        ],
+        compiler_params=params,
+        name="up",
+    )(pay, far, near, *fine)
+
+
+def two_rounds_fit(mesh, shape):
+    counts = tuple(mesh.shape[name] for name in ("gx", "gy", "gz"))
+    bx, by, bz = (size // count for size, count in zip(shape, counts))
+    shared = by // 4
+    reach_coarse = 4 * DEGREE + 2
+    return (
+        counts == (2, 4, 4)
+        and LEVELS == 3
+        and bx == 8
+        and by % 8 == 0
+        and bz == 128
+        and halo_rows(by) <= by
+        and by // 2 + reach_coarse <= 2 * by - shared
+        and 2 * reach_coarse + DEGREE + 1 <= bz // 2
+    )
+
+
 def solution(mesh):
     in_specs = (P("gx", "gy", "gz"), P("gx", "gy", "gz"))
     out_specs = (P("gx", "gy", "gz"), P("gx", "gy", "gz"))
-    return jax.shard_map(
-        per_device, mesh=mesh, in_specs=in_specs, out_specs=out_specs, check_vma=False
-    )
+
+    def whole(right_side, coefficient):
+        fits = two_rounds_fit(mesh, right_side.shape)
+        return jax.shard_map(
+            per_device_two_rounds if fits else per_device,
+            mesh=mesh,
+            in_specs=in_specs,
+            out_specs=out_specs,
+            check_vma=False,
+        )(right_side, coefficient)
+
+    return whole

time: 393 us -> 38.5 us (0.10)
  starting transfers between devices: 241 us -> 13.7 us
  waiting for transfers between devices: 101 us -> 14.4 us
  local copies, waits for them, and re-layouts: 22.9 us -> 0 us
  other arithmetic: 23.1 us -> 0.88 us
  Pallas kernels: 0 us -> 8.67 us
    ppermute x96 -> x9, starting transfers between devices: 241 us -> 13.7 us  [the longest x1 4.02 us: per_device_two_rounds(): far = lax.ppermute(pay, 'gy', [(0, 2), (2, 0), (1, 3), (3, 1)])]
    ppermute x96 -> x9, waiting for transfers between devices: 101 us -> 14.4 us  [the longest x1 4.84 us: per_device_two_rounds(): mid = lax.ppermute(to_mid, 'gz', swap_inner)]
    reshape x5 -> x0, local copies, waits for them, and re-layouts: 16.6 us -> none  [the longest x3 12.4 us: restrict(): blocks = values.reshape(size_x // 2, 2, size_y // 2, 2, size_z // 2, 2)]
    mul x69 -> x0, other arithmetic: 9.4 us -> none  [the longest x20 2.91 us: apply_padded(): flux_z = face_z * (padded[1:-1, 1:-1, 1:] - padded[1:-1, 1:-1, :-1])]
    pallas_call x0 -> x4, Pallas kernels: none -> 8.67 us  [the longest x1 4.41 us: per_device_two_rounds(): pl.pallas_call(up_kernel, out_shape=(shape(bx, by, bz),) * 2, in_specs=[i...]
    reduce_sum x4 -> x0, other arithmetic: 5.34 us -> none  [restrict(): return jnp.mean(blocks, axis=(1, 3, 5))]
    add x19 -> x0, other arithmetic: 4.4 us -> none  [the longest x6 2.91 us: deep_smooth(): iterate = trim_cells(iterate, 1) + update]
  transfers between devices with their start and end apart: 96 -> 9, of which waited for: 45 -> 6; matrix products, arithmetic and copies ran while one was open for 7% -> 0% of each run, Pallas kernels for 0% -> 0%
where the time goes in v4:
time: 38.5 us; the launch traced here: 38.3 us
  waiting for transfers between devices  14.4 us (37%)
  starting transfers between devices  13.7 us (36%)
  Pallas kernels  8.67 us (23%)
  other arithmetic  0.88 us (2%)
  between operations  0.68 us (2%)
    ppermute x1, waiting for transfers between devices, per_device_two_rounds(): mid = lax.ppermute(to_mid, 'gz', swap_inner)  4.84 us
    pallas_call x1, Pallas kernels, per_device_two_rounds(): pl.pallas_call(up_kernel, out_shape=(shape(bx, by, bz),) * 2, in_specs=[i...  4.41 us
    ppermute x1, starting transfers between devices, per_device_two_rounds(): far = lax.ppermute(pay, 'gy', [(0, 2), (2, 0), (1, 3), (3, 1)])  4.02 us
    ppermute x1, starting transfers between devices, per_device_two_rounds(): mid = lax.ppermute(to_mid, 'gz', swap_inner)  3.96 us
    pallas_call x1, Pallas kernels, per_device_two_rounds(): pl.pallas_call(down_kernel, out_shape=(*(shape(*(half_field if number ==...  3.69 us
    ppermute x1, waiting for transfers between devices, per_device_two_rounds(): near = lax.ppermute(near, 'gy', swap_pairs)  3.4 us
    ppermute x1, starting transfers between devices, per_device_two_rounds(): lax.ppermute(mine, 'gx', [(0, 1), (1, 0)])  2.11 us
    ppermute x1, waiting for transfers between devices, per_device_two_rounds(): lax.ppermute(for_inner, ('gx', 'gy'), across_x(inner))  2.08 us
  transfers between devices with their start and end apart: 9, of which 6 were waited for; matrix products, arithmetic and copies ran while one was open for 0% of the time, Pallas kernels for 0%

profile of v4, /device:TPU:1, one launch (start us, length us, event | category | flops | bytes accessed | tf_op | source)
XLA Modules:
  0.0 38.3 jit_solution(13806572362457387600)
XLA Ops:
  0.6 0.9 %pad_maximum_fusion.fields = f32[2,8,16,128]{3,2,1,0:T(8,128)S(1)} fusion(f32[1,8,16,128]{3,2,1,0:T(8,128)} %bitcast.2, f32[1,8,16,128]{3,2,1,0:T(8,128)} %bitcast.3), kind=kLoop, calls=%fused_computation | loop fusion | flops 32768 | bytes 262144 | tf_op jit(solution)/shard_map/stack | solution.py:640
  1.5 0.3 split.1
  1.8 2.1 %collective-permute-start = (f32[2,16,8,128]{3,2,1,0:T(8,128)S(1)}, f32[2,16,8,128]{3,2,1,0:T(8,128)S(1)}, u32[]{:S(2)}, u32[]{:S(2)}) collective-permute-start(f32[2,16,8,128]{3,2,1,0:T(8,128)S(1)} %get-tuple-element.16.refs_0_.mine), channel_id=1, source_target_pairs={{0,16},{16,0},{1,17},{17,1},{2,18},{18,2},{3,19},{19,3},{4,20},{20... | collective-permute-start | bytes 393224 | tf_op jit(solution)/shard_map/ppermute | solution.py:651
  4.0 1.3 %collective-permute-start.2 = (f32[2,13,8,128]{3,2,1,0:T(8,128)S(1)}, f32[2,13,8,128]{3,2,1,0:T(8,128)S(1)}, u32[]{:S(2)}, u32[]{:S(2)}) collective-permute-start(f32[2,13,8,128]{3,2,1,0:T(8,128)S(1)} %get-tuple-element.17), channel_id=1, source_target_pairs={{0,20},{4,16},{8,28},{12,24},{16,4},{20,0},{24,12},{28,8},{1,21},{... | collective-permute-start | bytes 319496 | tf_op jit(solution)/shard_map/ppermute | solution.py:653
  5.2 0.0 collective-permute-start.1
  5.3 1.4 %collective-permute-start.4 = (f32[2,13,8,128]{3,2,1,0:T(8,128)S(1)}, f32[2,13,8,128]{3,2,1,0:T(8,128)S(1)}, u32[]{:S(2)}, u32[]{:S(2)}) collective-permute-start(f32[2,13,8,128]{3,2,1,0:T(8,128)S(1)} %get-tuple-element.18), channel_id=1, source_target_pairs={{0,16},{4,24},{8,20},{12,28},{16,0},{20,8},{24,4},{28,12},{1,17},{... | collective-permute-start | bytes 319496 | tf_op jit(solution)/shard_map/ppermute | solution.py:655
  6.6 0.7 %collective-permute-start.3 = (f32[2,13,8,128]{3,2,1,0:T(8,128)S(1)}, f32[2,13,8,128]{3,2,1,0:T(8,128)S(1)}, u32[]{:S(2)}, u32[]{:S(2)}) collective-permute-start(f32[2,13,8,128]{3,2,1,0:T(8,128)S(1)} %get-tuple-element.18), channel_id=1, source_target_pairs={{0,0},{4,8},{8,4},{12,12},{1,1},{5,9},{9,5},{13,13},{2,2},{6,10},{... | collective-permute-start | bytes 319496 | tf_op jit(solution)/shard_map/ppermute | solution.py:654
  7.3 1.2 %collective-permute-done.2.refs_3_.pair_other = f32[2,13,8,128]{3,2,1,0:T(8,128)S(1)} collective-permute-done((f32[2,13,8,128]{3,2,1,0:T(8,128)S(1)}, f32[2,13,8,128]{3,2,1,0:T(8,128)S(1)}, u32[]{:S(2)}, u32[]{:S(2)}) %collective-permute-start.2) | collective-permute-done | bytes 106528 | tf_op jit(solution)/shard_map/ppermute | solution.py:653
  8.5 1.7 %collective-permute-done.1.refs_2_.pair = f32[2,13,8,128]{3,2,1,0:T(8,128)S(1)} collective-permute-done((f32[2,13,8,128]{3,2,1,0:T(8,128)S(1)}, f32[2,13,8,128]{3,2,1,0:T(8,128)S(1)}, u32[]{:S(2)}, u32[]{:S(2)}) %collective-permute-start.1) | collective-permute-done | bytes 106528 | tf_op jit(solution)/shard_map/ppermute | solution.py:652
  10.2 2.1 %collective-permute-done.4.refs_5_.inner_other = f32[2,13,8,128]{3,2,1,0:T(8,128)S(1)} collective-permute-done((f32[2,13,8,128]{3,2,1,0:T(8,128)S(1)}, f32[2,13,8,128]{3,2,1,0:T(8,128)S(1)}, u32[]{:S(2)}, u32[]{:S(2)}) %collective-permute-start.4) | collective-permute-done | bytes 106528 | tf_op jit(solution)/shard_map/ppermute | solution.py:655
  12.3 0.0 collective-permute-done.3.refs_4_.inner
  12.3 0.0 collective-permute-done.refs_1_.other
  12.3 0.2 pack.1
  12.6 4.0 %collective-permute-start.5 = (f32[84,8,128]{2,1,0:T(8,128)S(1)}, f32[84,8,128]{2,1,0:T(8,128)S(1)}, u32[]{:S(2)}, u32[]{:S(2)}) collective-permute-start(f32[84,8,128]{2,1,0:T(8,128)S(1)} %get-tuple-element.19), channel_id=1, source_target_pairs={{0,0},{1,2},{2,1},{3,3},{4,4},{5,6},{6,5},{7,7},{8,8},{9,10},{10,9... | collective-permute-start | bytes 1032200 | tf_op jit(solution)/shard_map/ppermute | solution.py:667
  16.5 0.1 collective-permute-start.6
  16.6 4.8 %collective-permute-done.5.mid = f32[84,8,128]{2,1,0:T(8,128)S(1)} collective-permute-done((f32[84,8,128]{2,1,0:T(8,128)S(1)}, f32[84,8,128]{2,1,0:T(8,128)S(1)}, u32[]{:S(2)}, u32[]{:S(2)}) %collective-permute-start.5) | collective-permute-done | bytes 344096 | tf_op jit(solution)/shard_map/ppermute | solution.py:667
  21.4 0.0 collective-permute-done.6.sib
  21.4 3.7 %down.1 = (f32[4,42,8,128]{3,2,1,0:T(8,128)S(1)}, f32[4,42,8,128]{3,2,1,0:T(8,128)S(1)}, f32[4,42,8,128]{3,2,1,0:T(8,128)S(1)}, f32[4,42,8,128]{3,2,1,0:T(8,128)...) custom-call(f32[2,16,8,128]{3,2,1,0:T(8,128)S(1)} %get-tuple-element, ...), custom_call_target="tpu_custom_call" | custom-call | tf_op jit(solution)/shard_map/down/pallas_call | solution.py:672
  25.1 4.0 %collective-permute-start.7 = (f32[2,16,8,128]{3,2,1,0:T(8,128)S(1)}, f32[2,16,8,128]{3,2,1,0:T(8,128)S(1)}, u32[]{:S(2)}, u32[]{:S(2)}) collective-permute-start(f32[2,16,8,128]{3,2,1,0:T(8,128)S(1)} %get-tuple-element.21.pay), channel_id=1, source_target_pairs={{0,8},{8,0},{4,12},{12,4},{1,9},{9,1},{5,13},{13,5},{2,10},{10,2},... | collective-permute-start | bytes 393224 | tf_op jit(solution)/shard_map/ppermute | solution.py:685
  29.2 0.2 collective-permute-start.8
  29.4 3.4 %collective-permute-done.8.near = f32[2,4,8,128]{3,2,1,0:T(8,128)S(1)} collective-permute-done((f32[2,4,8,128]{3,2,1,0:T(8,128)S(1)}, f32[2,4,8,128]{3,2,1,0:T(8,128)S(1)}, u32[]{:S(2)}, u32[]{:S(2)}) %collective-permute-start.8) | collective-permute-done | bytes 32800 | tf_op jit(solution)/shard_map/ppermute | solution.py:686
  32.8 1.2 %collective-permute-done.7.far = f32[2,16,8,128]{3,2,1,0:T(8,128)S(1)} collective-permute-done((f32[2,16,8,128]{3,2,1,0:T(8,128)S(1)}, f32[2,16,8,128]{3,2,1,0:T(8,128)S(1)}, u32[]{:S(2)}, u32[]{:S(2)}) %collective-permute-start.7) | collective-permute-done | bytes 131104 | tf_op jit(solution)/shard_map/ppermute | solution.py:685
  33.9 4.4 %up.1 = (f32[8,16,128]{2,1,0:T(8,128)}, f32[8,16,128]{2,1,0:T(8,128)}) custom-call(f32[2,16,8,128]{3,2,1,0:T(8,128)S(1)} %get-tuple-element.21.pay, f32[2,16,8,128]{3,2,1,0:T(8,128)S(1)} %collective-permute-done.7.far, f32[2,4,8,128]{3,2,1,0:T(8,128)S(1)} %collective-permute-done.8.near, f32[4,42,8,128]{3,2,1,0:T(8,128)S(1)} %get-tuple-element.23.right, ...), custom_call_target="tpu_custom_call" | custom-call | tf_op jit(solution)/shard_map/up/pallas_call | solution.py:688
Async XLA Ops:
  1.8 10.4 %collective-permute-start = (f32[2,16,8,128]{3,2,1,0:T(8,128)S(1)}, f32[2,16,8,128]{3,2,1,0:T(8,128)S(1)}, u32[]{:S(2)}, u32[]{:S(2)}) collective-permute-start(f32[2,16,8,128]{3,2,1,0:T(8,128)S(1)} %get-tuple-element.16.refs_0_.mine), channel_id=1, source_target_pairs={{0,16},{16,0},{1,17},{17,1},{2,18},{18,2},{3,19},{19,3},{4,20},{20... | collective-permute-start | bytes 393224 | tf_op jit(solution)/shard_map/ppermute | solution.py:651
  4.0 4.6 %collective-permute-start.2 = (f32[2,13,8,128]{3,2,1,0:T(8,128)S(1)}, f32[2,13,8,128]{3,2,1,0:T(8,128)S(1)}, u32[]{:S(2)}, u32[]{:S(2)}) collective-permute-start(f32[2,13,8,128]{3,2,1,0:T(8,128)S(1)} %get-tuple-element.17), channel_id=1, source_target_pairs={{0,20},{4,16},{8,28},{12,24},{16,4},{20,0},{24,12},{28,8},{1,21},{... | collective-permute-start | bytes 319496 | tf_op jit(solution)/shard_map/ppermute | solution.py:653
  5.2 5.0 %collective-permute-start.1 = (f32[2,13,8,128]{3,2,1,0:T(8,128)S(1)}, f32[2,13,8,128]{3,2,1,0:T(8,128)S(1)}, u32[]{:S(2)}, u32[]{:S(2)}) collective-permute-start(f32[2,13,8,128]{3,2,1,0:T(8,128)S(1)} %get-tuple-element.17), channel_id=1, source_target_pairs={{0,4},{4,0},{8,12},{12,8},{1,5},{5,1},{9,13},{13,9},{2,6},{6,2},{1... | collective-permute-start | bytes 319496 | tf_op jit(solution)/shard_map/ppermute | solution.py:652
  5.3 7.0 %collective-permute-start.4 = (f32[2,13,8,128]{3,2,1,0:T(8,128)S(1)}, f32[2,13,8,128]{3,2,1,0:T(8,128)S(1)}, u32[]{:S(2)}, u32[]{:S(2)}) collective-permute-start(f32[2,13,8,128]{3,2,1,0:T(8,128)S(1)} %get-tuple-element.18), channel_id=1, source_target_pairs={{0,16},{4,24},{8,20},{12,28},{16,0},{20,8},{24,4},{28,12},{1,17},{... | collective-permute-start | bytes 319496 | tf_op jit(solution)/shard_map/ppermute | solution.py:655
  6.6 5.7 %collective-permute-start.3 = (f32[2,13,8,128]{3,2,1,0:T(8,128)S(1)}, f32[2,13,8,128]{3,2,1,0:T(8,128)S(1)}, u32[]{:S(2)}, u32[]{:S(2)}) collective-permute-start(f32[2,13,8,128]{3,2,1,0:T(8,128)S(1)} %get-tuple-element.18), channel_id=1, source_target_pairs={{0,0},{4,8},{8,4},{12,12},{1,1},{5,9},{9,5},{13,13},{2,2},{6,10},{... | collective-permute-start | bytes 319496 | tf_op jit(solution)/shard_map/ppermute | solution.py:654
  12.6 8.9 %collective-permute-start.5 = (f32[84,8,128]{2,1,0:T(8,128)S(1)}, f32[84,8,128]{2,1,0:T(8,128)S(1)}, u32[]{:S(2)}, u32[]{:S(2)}) collective-permute-start(f32[84,8,128]{2,1,0:T(8,128)S(1)} %get-tuple-element.19), channel_id=1, source_target_pairs={{0,0},{1,2},{2,1},{3,3},{4,4},{5,6},{6,5},{7,7},{8,8},{9,10},{10,9... | collective-permute-start | bytes 1032200 | tf_op jit(solution)/shard_map/ppermute | solution.py:667
  16.5 4.9 %collective-permute-start.6 = (f32[84,8,128]{2,1,0:T(8,128)S(1)}, f32[84,8,128]{2,1,0:T(8,128)S(1)}, u32[]{:S(2)}, u32[]{:S(2)}) collective-permute-start(f32[84,8,128]{2,1,0:T(8,128)S(1)} %get-tuple-element.20), channel_id=1, source_target_pairs={{0,1},{1,0},{2,3},{3,2},{4,5},{5,4},{6,7},{7,6},{8,9},{9,8},{10,11... | collective-permute-start | bytes 1032200 | tf_op jit(solution)/shard_map/ppermute | solution.py:668
  25.1 8.8 %collective-permute-start.7 = (f32[2,16,8,128]{3,2,1,0:T(8,128)S(1)}, f32[2,16,8,128]{3,2,1,0:T(8,128)S(1)}, u32[]{:S(2)}, u32[]{:S(2)}) collective-permute-start(f32[2,16,8,128]{3,2,1,0:T(8,128)S(1)} %get-tuple-element.21.pay), channel_id=1, source_target_pairs={{0,8},{8,0},{4,12},{12,4},{1,9},{9,1},{5,13},{13,5},{2,10},{10,2},... | collective-permute-start | bytes 393224 | tf_op jit(solution)/shard_map/ppermute | solution.py:685
  29.2 3.6 %collective-permute-start.8 = (f32[2,4,8,128]{3,2,1,0:T(8,128)S(1)}, f32[2,4,8,128]{3,2,1,0:T(8,128)S(1)}, u32[]{:S(2)}, u32[]{:S(2)}) collective-permute-start(f32[2,4,8,128]{3,2,1,0:T(8,128)S(1)} %get-tuple-element.22), channel_id=1, source_target_pairs={{0,4},{4,0},{8,12},{12,8},{1,5},{5,1},{9,13},{13,9},{2,6},{6,2},{1... | collective-permute-start | bytes 98312 | tf_op jit(solution)/shard_map/ppermute | solution.py:686

commit v5 on v4

--- a/solution.py
+++ b/solution.py
@@ -209,6 +209,7 @@
 
 
 UNROLL_FINE = 20
+GROUPS = ((0, 1, 2), (4, 5, 3))
 UNROLL_COARSE = 64
 
 
@@ -238,8 +239,7 @@
     return pltpu.roll(values, shift % values.shape[axis], axis)
 
 
-def run(low, high, body, carry, unroll):
-    count = high - low
+def run(low, count, body, carry, unroll):
     steps = -(-count // unroll)
     unroll = -(-count // steps)
 
@@ -268,22 +268,20 @@
 
 
 class Level:
-    def __init__(self, refs, split, step, scale, unroll):
+    def __init__(self, refs, split, step, scale, unroll, pad=1):
         self.coef, self.right, self.face_x, self.face_y, self.face_z, self.edge_x, self.inverse, self.values, self.update = refs
         self.parts, self.rows = self.inverse.shape[:2]
         self.tile = self.inverse.shape[2:]
-        self.split, self.step, self.half, self.unroll = split, step, 0.5 * scale, unroll
+        self.split, self.step, self.half, self.unroll, self.pad = split, step, 0.5 * scale, unroll, pad
         self.first = tile_place(self.tile, 0) < step
         self.last = tile_place(self.tile, 0) >= self.tile[0] - step
 
     def read(self, ref, i):
         return [ref[part, i] for part in range(ref.shape[0])]
 
-    def clear_ends(self):
-        for ref in (self.coef, self.values):
-            for part in range(self.parts):
-                for i in (0, self.rows - 1):
-                    ref[part, i] = jnp.zeros(self.tile, jnp.float32)
+    def clear(self):
+        for i in range(self.rows):
+            self.coef[0, i] = self.values[0, i] = self.right[0, i] = jnp.zeros(self.tile, jnp.float32)
 
     def next_x(self, v, part):
         if self.split and part < 2:
@@ -324,7 +322,7 @@
                     + (along_z[p] + self.last_z(along_z, p))
                 )
                 inside = here[p] > 0.0
-                inverse.append(jnp.where(inside, 1.0 / jnp.where(inside, diagonal, 1.0), 0.0))
+                inverse.append(jnp.where(inside, 1.0 / diagonal, 0.0))
             stores = [
                 (self.face_y, i, upper),
                 (self.face_x, i, along_x),
@@ -334,13 +332,14 @@
             ]
             return (above, upper), stores + use(i, here, inverse)
 
-        here, before = self.read(self.coef, 1), self.read(self.coef, 0)
+        low, high = self.pad, self.rows - self.pad
+        here, before = self.read(self.coef, low), self.read(self.coef, low - 1)
         face = [half * (here[p] + before[p]) for p in parts]
         for p in parts:
-            self.face_y[p, 0] = face[p]
-        run(1, self.rows - 1, body, (here, face), self.unroll)
-
-    def sweep(self, low, high, use):
+            self.face_y[p, low - 1] = face[p]
+        run(low, high - low, body, (here, face), self.unroll)
+
+    def sweep(self, low, count, use):
         parts = range(self.parts)
 
         def body(i, carry):
@@ -363,7 +362,7 @@
 
         here, before = self.read(self.values, low), self.read(self.values, low - 1)
         face = self.read(self.face_y, low - 1)
-        run(low, high, body, (here, [face[p] * (here[p] - before[p]) for p in parts]), self.unroll)
+        run(low, count, body, (here, [face[p] * (here[p] - before[p]) for p in parts]), self.unroll)
 
     def from_zero(self, i, inverse):
         first = smoothing_weights()[0][1]
@@ -371,7 +370,7 @@
         step = [right[p] * (inverse[p] * first) for p in range(self.parts)]
         return [(self.update, i, step), (self.values, i, step)]
 
-    def smooth(self, low, high, weight):
+    def smooth(self, low, count, weight):
         keep, gain = weight
 
         def use(i, applied, here):
@@ -383,7 +382,7 @@
                 step = [keep * update[p] + step[p] for p in range(self.parts)]
             return [(self.update, i, step), (self.values, i, [here[p] + step[p] for p in range(self.parts)])]
 
-        self.sweep(low, high, use)
+        self.sweep(low, count, use)
 
 
 def total(items):
@@ -447,8 +446,9 @@
             at += 1
 
 
-def down_kernel(mine, other, pair, pair_other, inner, inner_other, mid, sib, *refs):
-    right, face_x, face_y, face_z, edge_x, inverse, values, pay_out, near_out, coef, update, sums, coefs = refs
+def down_kernel(mine, other, pair, pair_other, inner, inner_other, *refs):
+    edges, refs = refs[: 2 * len(GROUPS)], refs[2 * len(GROUPS) :]
+    right, face_x, face_y, face_z, edge_x, inverse, values, pay_out, far_out, near_out, coef, update, sums, coefs = refs
     level = Level((coef, right, face_x, face_y, face_z, edge_x, inverse, values, update), True, 1, 1.0, UNROLL_FINE)
     by, bx, bz = mine.shape[1:]
     halo = pair.shape[1]
@@ -461,8 +461,12 @@
     outside = (low == (core == 1)) & ~in_the_middle(at_z)
     top = tile_place(tile, 0) < bx // 2
 
-    def columns(block, y, at):
-        over, beside = mid[at], sib[at]
+    def columns(block, y, kind):
+        blocks = (mine, other, pair, pair_other, inner, inner_other)
+        number = next(number for number, group in enumerate(GROUPS) if kind in group)
+        before = GROUPS[number][: GROUPS[number].index(kind)]
+        at = y + sum(blocks[earlier].shape[1] for earlier in before)
+        over, beside = edges[2 * number][at], edges[2 * number + 1][at]
         first = jnp.where(core == 1, over, beside)
         last = jnp.where(core == 1, beside, over)
         side, own = jnp.where(low, first, last), block[0, y]
@@ -478,16 +482,15 @@
         ]
         return right_cells, coef_cells
 
-    at = 0
-    for near, far, row in (
+    for kind, (near, far, row) in zip((0, 2, 4), (
         (mine, other, halo),
         (pair, pair_other, (1 - odd) * (halo + by)),
         (inner, inner_other, odd * (halo + by)),
-    ):
+    )):
         count = near.shape[1]
 
-        def assemble(y, carry, near=near, far=far, row=row, at=at, count=count):
-            both = zip(columns(near, y, at + y), columns(far, y, at + count + y))
+        def assemble(y, carry, near=near, far=far, row=row, kind=kind):
+            both = zip(columns(near, y, kind), columns(far, y, kind + 1))
             stores = []
             for ref, (here, there) in zip((right, coef), both):
                 for odd_z in (0, 1):
@@ -502,7 +505,6 @@
             return carry, stores
 
         run(0, count, assemble, 0, 4)
-        at += 2 * count
 
     def begin(i, here, inverse):
         return level.from_zero(i, inverse) + [(coefs, i, [total(here)])]
@@ -511,44 +513,44 @@
     edge = 1
     for weight in smoothing_weights()[1:]:
         edge += 1
-        level.smooth(edge, level.rows - edge, weight)
+        level.smooth(edge, level.rows - 2 * edge, weight)
 
     def leftover(i, applied, here):
         right = level.read(level.right, i)
         return [(sums, i, [total(right[p] - applied[p] for p in range(level.parts))])]
 
     edge += 1
-    level.sweep(edge, level.rows - edge, leftover)
+    level.sweep(edge, level.rows - 2 * edge, leftover)
     for which, ref in enumerate((sums, coefs)):
         for y in range(by):
             pay_out[which, y] = 0.125 * (ref[0, edge + 2 * y] + ref[0, edge + 2 * y + 1])
         shared = by // 4
-        near_out[which] = pay_out[which, pl.ds(shared + odd * (by - 3 * shared), shared)]
+        far_out[which] = pay_out[which, pl.ds(shared * (1 - odd), by - shared)]
+        near_out[which] = pay_out[which, pl.ds(shared * (1 + odd), shared)]
 
 
 def up_kernel(pay, far, near, right, face_x, face_y, face_z, edge_x, inverse, start, solution_out, residual_out, *refs):
-    level1 = Level(refs[:9], False, 1, 0.25, UNROLL_COARSE)
+    level1 = Level(refs[:9], False, 1, 0.25, UNROLL_COARSE, near.shape[1])
     level2 = Level(refs[9:18], False, 2, 0.0625, UNROLL_COARSE)
     values, update, sums, moved, rows_out = refs[18:]
     fine = Level((None, right, face_x, face_y, face_z, edge_x, inverse, values, update), True, 1, 1.0, UNROLL_FINE)
     by, bx, bz = pay.shape[1:]
     shared = near.shape[1]
     at_x, at_y, _, _, odd = place()
-    upper = at_y // 2
     weights = smoothing_weights()
     tile = (bx, bz)
-    level1.clear_ends()
-    level2.clear_ends()
-
+    level1.clear()
+    level2.clear()
+
+    own1 = (by // 2) * at_y
+    far1 = (by // 2) * (at_y + 2 - 4 * (at_y // 2)) + shared * (1 - odd)
+    near1 = (by // 2) * (at_y + 1 - 2 * odd) + shared + shared * (1 - odd)
     for which, ref in enumerate((level1.right, level1.coef)):
-        for y in range(by):
-            one, two = pay[which, y], far[which, y]
-            ref[0, 1 + shared * odd + y] = jnp.where(upper == 1, two, one)
-            ref[0, 1 + by + shared * odd + y] = jnp.where(upper == 1, one, two)
-        for y in range(shared):
-            ref[0, 1 + 2 * by * (1 - odd) + y] = jnp.where(in_the_middle(at_y), near[which, y], 0.0)
-
-    n1 = level1.rows - 1
+        for piece, at in ((pay, own1), (far, far1), (near, near1)):
+            for y in range(piece.shape[1]):
+                ref[0, at + y] = piece[which, y]
+
+    low1, high1 = level1.pad, level1.rows - level1.pad
     n2 = level2.rows - 1
     even_lane = tile_place(tile, 1) % 2 == 0
     even_row = tile_place(tile, 0) % 2 == 0
@@ -559,35 +561,39 @@
 
     level1.set_faces(lambda i, here, inverse: level1.from_zero(i, inverse))
     for weight in weights[1:]:
-        level1.smooth(1, n1, weight)
+        level1.smooth(low1, high1 - low1, weight)
 
     def leftover1(i, applied, here):
         return [(sums, i, [level1.right[0, i] - applied[0]])]
 
-    level1.sweep(1, n1, leftover1)
+    level1.sweep(low1, high1 - low1, leftover1)
     for j in range(1, n2):
-        level2.right[0, j] = pair_cells(sums[0, 2 * j - 1] + sums[0, 2 * j])
-        level2.coef[0, j] = pair_cells(level1.coef[0, 2 * j - 1] + level1.coef[0, 2 * j])
+        level2.right[0, j] = pair_cells(sums[0, low1 + 2 * j - 2] + sums[0, low1 + 2 * j - 1])
+        level2.coef[0, j] = pair_cells(level1.coef[0, low1 + 2 * j - 2] + level1.coef[0, low1 + 2 * j - 1])
 
     level2.set_faces(lambda i, here, inverse: level2.from_zero(i, inverse))
     for weight in weights[1:]:
-        level2.smooth(1, n2, weight)
-
-    for j in range(1, n1):
-        level1.values[0, j] = level1.values[0, j] + level2.values[0, (j + 1) // 2]
+        level2.smooth(1, n2 - 1, weight)
+
+    for j in range(low1, high1):
+        level1.values[0, j] = level1.values[0, j] + level2.values[0, 1 + (j - low1) // 2]
+    reach = DEGREE + (DEGREE + 2) // 2
     for weight in weights:
-        level1.smooth(1, n1, weight)
+        reach -= 1
+        count = by // 2 + 2 * reach
+        start1 = jnp.clip(shared + own1 - reach, low1, high1 - count)
+        level1.smooth(start1, count, weight)
 
     halo = (fine.rows - by) // 2
     reach = DEGREE + 1
-    base = 1 + (by // 2) * at_y + shared * (1 - odd)
+    base = shared + own1
     for y in range(-reach, by + reach):
         coarse = level1.values[0, base + y // 2]
         for part in range(fine.parts):
             values[part, halo + y] = start[part, halo + y] + coarse
     for weight in weights:
         reach -= 1
-        fine.smooth(halo - reach, halo + by + reach, weight)
+        fine.smooth(halo - reach, by + 2 * reach, weight)
 
     own_lane = tile_place(tile, 1) < bz // 2
     top = tile_place(tile, 0) < bx // 2
@@ -609,7 +615,7 @@
             stores.append((rows_out.at[pl.ds(slot, 1)], i - halo, [jnp.where(own_lane, cells[0], turn(cells[1], bz // 2, 1))]))
         return stores
 
-    fine.sweep(halo, halo + by, finish)
+    fine.sweep(halo, by, finish)
     matrix = parity_matrix(bz, True)
     for slot, ref in enumerate((solution_out, residual_out)):
         moved[slot] = exact_dot(rows_out[slot].reshape(by * bx, bz), matrix)
@@ -655,36 +661,40 @@
         "inner_other": lax.ppermute(for_inner, ("gx", "gy"), across_x(inner)),
     }
     blocks = list(blocks.values())
-    edges = shape(2 * by + 4 * halo, bx, bz)
-    to_mid, to_sib = pl.pallas_call(
-        pack_kernel,
-        out_shape=(edges, edges),
-        in_specs=[in_vmem] * 6,
-        out_specs=(in_vmem,) * 2,
-        compiler_params=params,
-        name="pack",
-    )(*blocks)
-    mid = lax.ppermute(to_mid, "gz", swap_inner)
-    sib = lax.ppermute(to_sib, "gz", swap_pairs)
+    def share(group):
+        edges = shape(sum(block.shape[1] for block in group), bx, bz)
+        to_mid, to_sib = pl.pallas_call(
+            pack_kernel,
+            out_shape=(edges, edges),
+            in_specs=[in_vmem] * len(group),
+            out_specs=(in_vmem,) * 2,
+            compiler_params=params,
+            name="pack",
+        )(*group)
+        return lax.ppermute(to_mid, "gz", swap_inner), lax.ppermute(to_sib, "gz", swap_pairs)
+
+    edges = [part for group in GROUPS for part in share([blocks[kind] for kind in group])]
 
     rows = by + 2 * halo
     field, half_field = (4, rows, bx, bz), (2, rows, bx, bz)
-    *fine, pay, near = pl.pallas_call(
+    *fine, pay, far, near = pl.pallas_call(
         down_kernel,
         out_shape=(
             *(shape(*(half_field if number == 4 else field)) for number in range(7)),
             shape(2, by, bx, bz),
+            shape(2, by - shared, bx, bz),
             shape(2, shared, bx, bz),
         ),
-        in_specs=[in_vmem] * 8,
-        out_specs=(in_vmem,) * 9,
+        in_specs=[in_vmem] * (6 + 2 * len(GROUPS)),
+        out_specs=(in_vmem,) * 10,
         scratch_shapes=[vmem(*field), vmem(*field), vmem(1, rows, bx, bz), vmem(1, rows, bx, bz)],
         compiler_params=params,
         name="down",
-    )(*blocks, mid, sib)
-    far = lax.ppermute(pay, "gy", [(0, 2), (2, 0), (1, 3), (3, 1)])
+    )(*blocks, *edges)
+    far = lax.ppermute(far, "gy", [(0, 2), (2, 0), (1, 3), (3, 1)])
     near = lax.ppermute(near, "gy", swap_pairs)
-    rows1 = 2 * by + shared + 2
+    rows1 = by // 2 * lax.axis_size("gy") + 2 * shared
+    rows2 = by // 4 * lax.axis_size("gy") + 2
     return pl.pallas_call(
         up_kernel,
         out_shape=(shape(bx, by, bz),) * 2,
@@ -692,7 +702,7 @@
         out_specs=(in_vmem,) * 2,
         scratch_shapes=[
             *[vmem(1, rows1, bx, bz)] * 9,
-            *[vmem(1, rows1 // 2 + 1, bx, bz)] * 9,
+            *[vmem(1, rows2, bx, bz)] * 9,
             vmem(*field),
             vmem(*field),
             vmem(1, rows1, bx, bz),
@@ -716,7 +726,7 @@
         and by % 8 == 0
         and bz == 128
         and halo_rows(by) <= by
-        and by // 2 + reach_coarse <= 2 * by - shared
+        and by // 2 + reach_coarse + 1 <= 2 * by - shared
         and 2 * reach_coarse + DEGREE + 1 <= bz // 2
     )
 

time: 38.5 us -> 35.7 us (0.927)
  waiting for transfers between devices: 14.4 us -> 7.52 us
  starting transfers between devices: 13.7 us -> 17.8 us
    ppermute x3 -> x5, starting transfers between devices: 8.05 us -> 11.8 us  [the longest x2 8.16 us: share(): lax.ppermute(to_mid, 'gz', swap_inner)]
    ppermute x1, waiting for transfers between devices: 2.08 us -> 0.01 us  [per_device_two_rounds(): lax.ppermute(for_inner, ('gx', 'gy'), across_x(inner))]
    ppermute x3 -> x5, waiting for transfers between devices: 5.99 us -> 4.2 us  [the longest x2 4.19 us: share(): lax.ppermute(to_mid, 'gz', swap_inner)]
    ppermute x1, starting transfers between devices: 0.03 us -> 1.3 us  [per_device_two_rounds(): lax.ppermute(for_pair, 'gy', swap_pairs)]
    ppermute x1, starting transfers between devices: 1.27 us -> 0.01 us  [per_device_two_rounds(): lax.ppermute(for_pair, ('gx', 'gy'), across_x(pairs))]
    ppermute x1, waiting for transfers between devices: 1.25 us -> 0.01 us  [per_device_two_rounds(): lax.ppermute(for_pair, ('gx', 'gy'), across_x(pairs))]
    ppermute x1, waiting for transfers between devices: 1.69 us -> 0.54 us  [per_device_two_rounds(): lax.ppermute(for_pair, 'gy', swap_pairs)]
    ppermute x1, waiting for transfers between devices: 3.4 us -> 2.77 us  [per_device_two_rounds(): near = lax.ppermute(near, 'gy', swap_pairs)]
  transfers between devices with their start and end apart: 9 -> 11, of which waited for: 6 -> 3; matrix products, arithmetic and copies ran while one was open for 0% -> 0% of each run, Pallas kernels for 0% -> 1%
where the time goes in v5:
time: 35.7 us; the launch traced here: 35.5 us
  starting transfers between devices  17.8 us (50%)
  Pallas kernels  8.57 us (24%)
  waiting for transfers between devices  7.52 us (21%)
  other arithmetic  0.88 us (2%)
  between operations  0.73 us (2%)
    ppermute x2, starting transfers between devices, share(): lax.ppermute(to_mid, 'gz', swap_inner)  8.16 us
    pallas_call x1, Pallas kernels, per_device_two_rounds(): pl.pallas_call(up_kernel, out_shape=(shape(bx, by, bz),) * 2, in_specs=[i...  4.25 us
    ppermute x2, waiting for transfers between devices, share(): lax.ppermute(to_mid, 'gz', swap_inner)  4.19 us
    pallas_call x1, Pallas kernels, per_device_two_rounds(): pl.pallas_call(down_kernel, out_shape=(*(shape(*(half_field if number ==...  3.69 us
    ppermute x1, starting transfers between devices, per_device_two_rounds(): far = lax.ppermute(far, 'gy', [(0, 2), (2, 0), (1, 3), (3, 1)])  3.55 us
    ppermute x1, waiting for transfers between devices, per_device_two_rounds(): near = lax.ppermute(near, 'gy', swap_pairs)  2.77 us
    ppermute x1, starting transfers between devices, per_device_two_rounds(): lax.ppermute(mine, 'gx', [(0, 1), (1, 0)])  2.11 us
    ppermute x1, starting transfers between devices, per_device_two_rounds(): lax.ppermute(for_inner, ('gx', 'gy'), across_x(inner))  1.35 us
  transfers between devices with their start and end apart: 11, of which 3 were waited for; matrix products, arithmetic and copies ran while one was open for 0% of the time, Pallas kernels for 1%

profile of v5, /device:TPU:1, one launch (start us, length us, event | category | flops | bytes accessed | tf_op | source)
XLA Modules:
  0.0 35.5 jit_solution(3176295776369701209)
XLA Ops:
  0.6 0.9 %pad_maximum_fusion.fields = f32[2,8,16,128]{3,2,1,0:T(8,128)S(1)} fusion(f32[1,8,16,128]{3,2,1,0:T(8,128)} %bitcast.2, f32[1,8,16,128]{3,2,1,0:T(8,128)} %bitcast.3), kind=kLoop, calls=%fused_computation | loop fusion | flops 32768 | bytes 262144 | tf_op jit(solution)/shard_map/stack | solution.py:646
  1.5 0.3 split.1
  1.8 2.1 %collective-permute-start = (f32[2,16,8,128]{3,2,1,0:T(8,128)S(1)}, f32[2,16,8,128]{3,2,1,0:T(8,128)S(1)}, u32[]{:S(2)}, u32[]{:S(2)}) collective-permute-start(f32[2,16,8,128]{3,2,1,0:T(8,128)S(1)} %get-tuple-element.19.refs_0_.mine), channel_id=1, source_target_pairs={{0,16},{16,0},{1,17},{17,1},{2,18},{18,2},{3,19},{19,3},{4,20},{20... | collective-permute-start | bytes 393224 | tf_op jit(solution)/shard_map/ppermute | solution.py:657
  4.0 1.3 %collective-permute-start.1 = (f32[2,13,8,128]{3,2,1,0:T(8,128)S(1)}, f32[2,13,8,128]{3,2,1,0:T(8,128)S(1)}, u32[]{:S(2)}, u32[]{:S(2)}) collective-permute-start(f32[2,13,8,128]{3,2,1,0:T(8,128)S(1)} %get-tuple-element.20), channel_id=1, source_target_pairs={{0,4},{4,0},{8,12},{12,8},{1,5},{5,1},{9,13},{13,9},{2,6},{6,2},{1... | collective-permute-start | bytes 319496 | tf_op jit(solution)/shard_map/ppermute | solution.py:658
  5.3 0.0 collective-permute-start.2
  5.3 1.4 %collective-permute-start.4 = (f32[2,13,8,128]{3,2,1,0:T(8,128)S(1)}, f32[2,13,8,128]{3,2,1,0:T(8,128)S(1)}, u32[]{:S(2)}, u32[]{:S(2)}) collective-permute-start(f32[2,13,8,128]{3,2,1,0:T(8,128)S(1)} %get-tuple-element.21), channel_id=1, source_target_pairs={{0,16},{4,24},{8,20},{12,28},{16,0},{20,8},{24,4},{28,12},{1,17},{... | collective-permute-start | bytes 319496 | tf_op jit(solution)/shard_map/ppermute | solution.py:661
  6.6 0.7 %collective-permute-start.3 = (f32[2,13,8,128]{3,2,1,0:T(8,128)S(1)}, f32[2,13,8,128]{3,2,1,0:T(8,128)S(1)}, u32[]{:S(2)}, u32[]{:S(2)}) collective-permute-start(f32[2,13,8,128]{3,2,1,0:T(8,128)S(1)} %get-tuple-element.21), channel_id=1, source_target_pairs={{0,0},{4,8},{8,4},{12,12},{1,1},{5,9},{9,5},{13,13},{2,2},{6,10},{... | collective-permute-start | bytes 319496 | tf_op jit(solution)/shard_map/ppermute | solution.py:660
  7.3 0.5 %collective-permute-done.1.refs_2_.pair = f32[2,13,8,128]{3,2,1,0:T(8,128)S(1)} collective-permute-done((f32[2,13,8,128]{3,2,1,0:T(8,128)S(1)}, f32[2,13,8,128]{3,2,1,0:T(8,128)S(1)}, u32[]{:S(2)}, u32[]{:S(2)}) %collective-permute-start.1) | collective-permute-done | bytes 106528 | tf_op jit(solution)/shard_map/ppermute | solution.py:658
  7.8 0.0 collective-permute-done.refs_1_.other
  7.8 0.2 pack.2
  8.0 5.8 %collective-permute-start.5 = (f32[45,8,128]{2,1,0:T(8,128)S(1)}, f32[45,8,128]{2,1,0:T(8,128)S(1)}, u32[]{:S(2)}, u32[]{:S(2)}) collective-permute-start(f32[45,8,128]{2,1,0:T(8,128)S(1)} %get-tuple-element.22), channel_id=1, source_target_pairs={{0,0},{1,2},{2,1},{3,3},{4,4},{5,6},{6,5},{7,7},{8,8},{9,10},{10,9... | collective-permute-start | bytes 552968 | tf_op jit(solution)/shard_map/ppermute | solution.py:674
  13.8 0.1 collective-permute-start.6
  13.9 0.0 collective-permute-done.2.refs_2_.pair_other
  13.9 0.0 collective-permute-done.3.refs_0_.inner
  13.9 0.1 pack.3
  14.1 2.3 %collective-permute-start.7 = (f32[39,8,128]{2,1,0:T(8,128)S(1)}, f32[39,8,128]{2,1,0:T(8,128)S(1)}, u32[]{:S(2)}, u32[]{:S(2)}) collective-permute-start(f32[39,8,128]{2,1,0:T(8,128)S(1)} %get-tuple-element.24), channel_id=1, source_target_pairs={{0,0},{1,2},{2,1},{3,3},{4,4},{5,6},{6,5},{7,7},{8,8},{9,10},{10,9... | collective-permute-start | bytes 479240 | tf_op jit(solution)/shard_map/ppermute | solution.py:674
  16.4 0.1 collective-permute-start.8
  16.5 4.2 %collective-permute-done.7.refs_2_ = f32[39,8,128]{2,1,0:T(8,128)S(1)} collective-permute-done((f32[39,8,128]{2,1,0:T(8,128)S(1)}, f32[39,8,128]{2,1,0:T(8,128)S(1)}, u32[]{:S(2)}, u32[]{:S(2)}) %collective-permute-start.7) | collective-permute-done | bytes 159776 | tf_op jit(solution)/shard_map/ppermute | solution.py:674
  20.7 3.7 %down.1 = (f32[4,42,8,128]{3,2,1,0:T(8,128)S(1)}, f32[4,42,8,128]{3,2,1,0:T(8,128)S(1)}, f32[4,42,8,128]{3,2,1,0:T(8,128)S(1)}, f32[4,42,8,128]{3,2,1,0:T(8,128)...) custom-call(f32[2,16,8,128]{3,2,1,0:T(8,128)S(1)} %get-tuple-element, ...), custom_call_target="tpu_custom_call" | custom-call | tf_op jit(solution)/shard_map/down/pallas_call | solution.py:680
  24.4 3.5 %collective-permute-start.9 = (f32[2,12,8,128]{3,2,1,0:T(8,128)S(1)}, f32[2,12,8,128]{3,2,1,0:T(8,128)S(1)}, u32[]{:S(2)}, u32[]{:S(2)}) collective-permute-start(f32[2,12,8,128]{3,2,1,0:T(8,128)S(1)} %get-tuple-element.27), channel_id=1, source_target_pairs={{0,8},{8,0},{4,12},{12,4},{1,9},{9,1},{5,13},{13,5},{2,10},{10,2},... | collective-permute-start | bytes 294920 | tf_op jit(solution)/shard_map/ppermute | solution.py:694
  27.9 0.5 %collective-permute-start.10 = (f32[2,4,8,128]{3,2,1,0:T(8,128)S(1)}, f32[2,4,8,128]{3,2,1,0:T(8,128)S(1)}, u32[]{:S(2)}, u32[]{:S(2)}) collective-permute-start(f32[2,4,8,128]{3,2,1,0:T(8,128)S(1)} %get-tuple-element.28), channel_id=1, source_target_pairs={{0,4},{4,0},{8,12},{12,8},{1,5},{5,1},{9,13},{13,9},{2,6},{6,2},{1... | collective-permute-start | bytes 98312 | tf_op jit(solution)/shard_map/ppermute | solution.py:695
  28.4 2.8 %collective-permute-done.10.near = f32[2,4,8,128]{3,2,1,0:T(8,128)S(1)} collective-permute-done((f32[2,4,8,128]{3,2,1,0:T(8,128)S(1)}, f32[2,4,8,128]{3,2,1,0:T(8,128)S(1)}, u32[]{:S(2)}, u32[]{:S(2)}) %collective-permute-start.10) | collective-permute-done | bytes 32800 | tf_op jit(solution)/shard_map/ppermute | solution.py:695
  31.2 0.0 collective-permute-done.9.far
  31.2 4.2 %up.1 = (f32[8,16,128]{2,1,0:T(8,128)}, f32[8,16,128]{2,1,0:T(8,128)}) custom-call(f32[2,16,8,128]{3,2,1,0:T(8,128)S(1)} %get-tuple-element.26.pay, f32[2,12,8,128]{3,2,1,0:T(8,128)S(1)} %collective-permute-done.9.far, f32[2,4,8,128]{3,2,1,0:T(8,128)S(1)} %collective-permute-done.10.near, f32[4,42,8,128]{3,2,1,0:T(8,128)S(1)} %get-tuple-element.29.right, ...), custom_call_target="tpu_custom_call" | custom-call | tf_op jit(solution)/shard_map/up/pallas_call | solution.py:698
  (4 shorter events, 0.0 us)
Async XLA Ops:
  1.8 6.0 %collective-permute-start = (f32[2,16,8,128]{3,2,1,0:T(8,128)S(1)}, f32[2,16,8,128]{3,2,1,0:T(8,128)S(1)}, u32[]{:S(2)}, u32[]{:S(2)}) collective-permute-start(f32[2,16,8,128]{3,2,1,0:T(8,128)S(1)} %get-tuple-element.19.refs_0_.mine), channel_id=1, source_target_pairs={{0,16},{16,0},{1,17},{17,1},{2,18},{18,2},{3,19},{19,3},{4,20},{20... | collective-permute-start | bytes 393224 | tf_op jit(solution)/shard_map/ppermute | solution.py:657
  4.0 3.9 %collective-permute-start.1 = (f32[2,13,8,128]{3,2,1,0:T(8,128)S(1)}, f32[2,13,8,128]{3,2,1,0:T(8,128)S(1)}, u32[]{:S(2)}, u32[]{:S(2)}) collective-permute-start(f32[2,13,8,128]{3,2,1,0:T(8,128)S(1)} %get-tuple-element.20), channel_id=1, source_target_pairs={{0,4},{4,0},{8,12},{12,8},{1,5},{5,1},{9,13},{13,9},{2,6},{6,2},{1... | collective-permute-start | bytes 319496 | tf_op jit(solution)/shard_map/ppermute | solution.py:658
  5.3 8.7 %collective-permute-start.2 = (f32[2,13,8,128]{3,2,1,0:T(8,128)S(1)}, f32[2,13,8,128]{3,2,1,0:T(8,128)S(1)}, u32[]{:S(2)}, u32[]{:S(2)}) collective-permute-start(f32[2,13,8,128]{3,2,1,0:T(8,128)S(1)} %get-tuple-element.20), channel_id=1, source_target_pairs={{0,20},{4,16},{8,28},{12,24},{16,4},{20,0},{24,12},{28,8},{1,21},{... | collective-permute-start | bytes 319496 | tf_op jit(solution)/shard_map/ppermute | solution.py:659
  5.3 8.7 %collective-permute-start.4 = (f32[2,13,8,128]{3,2,1,0:T(8,128)S(1)}, f32[2,13,8,128]{3,2,1,0:T(8,128)S(1)}, u32[]{:S(2)}, u32[]{:S(2)}) collective-permute-start(f32[2,13,8,128]{3,2,1,0:T(8,128)S(1)} %get-tuple-element.21), channel_id=1, source_target_pairs={{0,16},{4,24},{8,20},{12,28},{16,0},{20,8},{24,4},{28,12},{1,17},{... | collective-permute-start | bytes 319496 | tf_op jit(solution)/shard_map/ppermute | solution.py:661
  6.6 7.3 %collective-permute-start.3 = (f32[2,13,8,128]{3,2,1,0:T(8,128)S(1)}, f32[2,13,8,128]{3,2,1,0:T(8,128)S(1)}, u32[]{:S(2)}, u32[]{:S(2)}) collective-permute-start(f32[2,13,8,128]{3,2,1,0:T(8,128)S(1)} %get-tuple-element.21), channel_id=1, source_target_pairs={{0,0},{4,8},{8,4},{12,12},{1,1},{5,9},{9,5},{13,13},{2,2},{6,10},{... | collective-permute-start | bytes 319496 | tf_op jit(solution)/shard_map/ppermute | solution.py:660
  8.0 12.7 %collective-permute-start.5 = (f32[45,8,128]{2,1,0:T(8,128)S(1)}, f32[45,8,128]{2,1,0:T(8,128)S(1)}, u32[]{:S(2)}, u32[]{:S(2)}) collective-permute-start(f32[45,8,128]{2,1,0:T(8,128)S(1)} %get-tuple-element.22), channel_id=1, source_target_pairs={{0,0},{1,2},{2,1},{3,3},{4,4},{5,6},{6,5},{7,7},{8,8},{9,10},{10,9... | collective-permute-start | bytes 552968 | tf_op jit(solution)/shard_map/ppermute | solution.py:674
  13.8 6.9 %collective-permute-start.6 = (f32[45,8,128]{2,1,0:T(8,128)S(1)}, f32[45,8,128]{2,1,0:T(8,128)S(1)}, u32[]{:S(2)}, u32[]{:S(2)}) collective-permute-start(f32[45,8,128]{2,1,0:T(8,128)S(1)} %get-tuple-element.23), channel_id=1, source_target_pairs={{0,1},{1,0},{2,3},{3,2},{4,5},{5,4},{6,7},{7,6},{8,9},{9,8},{10,11... | collective-permute-start | bytes 552968 | tf_op jit(solution)/shard_map/ppermute | solution.py:674
  14.1 6.6 %collective-permute-start.7 = (f32[39,8,128]{2,1,0:T(8,128)S(1)}, f32[39,8,128]{2,1,0:T(8,128)S(1)}, u32[]{:S(2)}, u32[]{:S(2)}) collective-permute-start(f32[39,8,128]{2,1,0:T(8,128)S(1)} %get-tuple-element.24), channel_id=1, source_target_pairs={{0,0},{1,2},{2,1},{3,3},{4,4},{5,6},{6,5},{7,7},{8,8},{9,10},{10,9... | collective-permute-start | bytes 479240 | tf_op jit(solution)/shard_map/ppermute | solution.py:674
  16.4 4.3 %collective-permute-start.8 = (f32[39,8,128]{2,1,0:T(8,128)S(1)}, f32[39,8,128]{2,1,0:T(8,128)S(1)}, u32[]{:S(2)}, u32[]{:S(2)}) collective-permute-start(f32[39,8,128]{2,1,0:T(8,128)S(1)} %get-tuple-element.25), channel_id=1, source_target_pairs={{0,1},{1,0},{2,3},{3,2},{4,5},{5,4},{6,7},{7,6},{8,9},{9,8},{10,11... | collective-permute-start | bytes 479240 | tf_op jit(solution)/shard_map/ppermute | solution.py:674
  24.4 6.8 %collective-permute-start.9 = (f32[2,12,8,128]{3,2,1,0:T(8,128)S(1)}, f32[2,12,8,128]{3,2,1,0:T(8,128)S(1)}, u32[]{:S(2)}, u32[]{:S(2)}) collective-permute-start(f32[2,12,8,128]{3,2,1,0:T(8,128)S(1)} %get-tuple-element.27), channel_id=1, source_target_pairs={{0,8},{8,0},{4,12},{12,4},{1,9},{9,1},{5,13},{13,5},{2,10},{10,2},... | collective-permute-start | bytes 294920 | tf_op jit(solution)/shard_map/ppermute | solution.py:694
  27.9 3.3 %collective-permute-start.10 = (f32[2,4,8,128]{3,2,1,0:T(8,128)S(1)}, f32[2,4,8,128]{3,2,1,0:T(8,128)S(1)}, u32[]{:S(2)}, u32[]{:S(2)}) collective-permute-start(f32[2,4,8,128]{3,2,1,0:T(8,128)S(1)} %get-tuple-element.28), channel_id=1, source_target_pairs={{0,4},{4,0},{8,12},{12,8},{1,5},{5,1},{9,13},{13,9},{2,6},{6,2},{1... | collective-permute-start | bytes 98312 | tf_op jit(solution)/shard_map/ppermute | solution.py:695

commit v6 on v5

--- a/solution.py
+++ b/solution.py
@@ -208,7 +208,7 @@
     return (solution, residual)
 
 
-UNROLL_FINE = 20
+UNROLL_FINE = 26
 GROUPS = ((0, 1, 2), (4, 5, 3))
 UNROLL_COARSE = 64
 
@@ -504,7 +504,7 @@
                         stores.append((ref.at[pl.ds(2 * odd_x + odd_z, 1)], row + y, [value]))
             return carry, stores
 
-        run(0, count, assemble, 0, 4)
+        run(0, count, assemble, 0, 16)
 
     def begin(i, here, inverse):
         return level.from_zero(i, inverse) + [(coefs, i, [total(here)])]

time: 35.7 us -> 34.6 us (0.969)
  Pallas kernels: 8.57 us -> 7.51 us
    pallas_call x1, Pallas kernels: 3.69 us -> 2.9 us  [per_device_two_rounds(): pl.pallas_call(down_kernel, out_shape=(*(shape(*(half_field if number ==...]
where the time goes in v6:
time: 34.6 us; the launch traced here: 34.4 us
  starting transfers between devices  17.8 us (51%)
  Pallas kernels  7.51 us (22%)
  waiting for transfers between devices  7.51 us (22%)
  other arithmetic  0.88 us (3%)
  between operations  0.73 us (2%)
    ppermute x2, starting transfers between devices, share(): lax.ppermute(to_mid, 'gz', swap_inner)  8.16 us
    ppermute x2, waiting for transfers between devices, share(): lax.ppermute(to_mid, 'gz', swap_inner)  4.19 us
    pallas_call x1, Pallas kernels, per_device_two_rounds(): pl.pallas_call(up_kernel, out_shape=(shape(bx, by, bz),) * 2, in_specs=[i...  3.97 us
    ppermute x1, starting transfers between devices, per_device_two_rounds(): far = lax.ppermute(far, 'gy', [(0, 2), (2, 0), (1, 3), (3, 1)])  3.55 us
    pallas_call x1, Pallas kernels, per_device_two_rounds(): pl.pallas_call(down_kernel, out_shape=(*(shape(*(half_field if number ==...  2.9 us
    ppermute x1, waiting for transfers between devices, per_device_two_rounds(): near = lax.ppermute(near, 'gy', swap_pairs)  2.77 us
    ppermute x1, starting transfers between devices, per_device_two_rounds(): lax.ppermute(mine, 'gx', [(0, 1), (1, 0)])  2.11 us
    ppermute x1, starting transfers between devices, per_device_two_rounds(): lax.ppermute(for_inner, ('gx', 'gy'), across_x(inner))  1.35 us
  transfers between devices with their start and end apart: 11, of which 3 were waited for; matrix products, arithmetic and copies ran while one was open for 0% of the time, Pallas kernels for 1%

profile of v6, /device:TPU:1, one launch (start us, length us, event | category | flops | bytes accessed | tf_op | source)
XLA Modules:
  0.0 34.4 jit_solution(2050511560762834229)
XLA Ops:
  0.6 0.9 %pad_maximum_fusion.fields = f32[2,8,16,128]{3,2,1,0:T(8,128)S(1)} fusion(f32[1,8,16,128]{3,2,1,0:T(8,128)} %bitcast.2, f32[1,8,16,128]{3,2,1,0:T(8,128)} %bitcast.3), kind=kLoop, calls=%fused_computation | loop fusion | flops 32768 | bytes 262144 | tf_op jit(solution)/shard_map/stack | solution.py:646
  1.5 0.3 split.1
  1.8 2.1 %collective-permute-start = (f32[2,16,8,128]{3,2,1,0:T(8,128)S(1)}, f32[2,16,8,128]{3,2,1,0:T(8,128)S(1)}, u32[]{:S(2)}, u32[]{:S(2)}) collective-permute-start(f32[2,16,8,128]{3,2,1,0:T(8,128)S(1)} %get-tuple-element.19.refs_0_.mine), channel_id=1, source_target_pairs={{0,16},{16,0},{1,17},{17,1},{2,18},{18,2},{3,19},{19,3},{4,20},{20... | collective-permute-start | bytes 393224 | tf_op jit(solution)/shard_map/ppermute | solution.py:657
  4.0 1.3 %collective-permute-start.1 = (f32[2,13,8,128]{3,2,1,0:T(8,128)S(1)}, f32[2,13,8,128]{3,2,1,0:T(8,128)S(1)}, u32[]{:S(2)}, u32[]{:S(2)}) collective-permute-start(f32[2,13,8,128]{3,2,1,0:T(8,128)S(1)} %get-tuple-element.20), channel_id=1, source_target_pairs={{0,4},{4,0},{8,12},{12,8},{1,5},{5,1},{9,13},{13,9},{2,6},{6,2},{1... | collective-permute-start | bytes 319496 | tf_op jit(solution)/shard_map/ppermute | solution.py:658
  5.3 1.4 %collective-permute-start.4 = (f32[2,13,8,128]{3,2,1,0:T(8,128)S(1)}, f32[2,13,8,128]{3,2,1,0:T(8,128)S(1)}, u32[]{:S(2)}, u32[]{:S(2)}) collective-permute-start(f32[2,13,8,128]{3,2,1,0:T(8,128)S(1)} %get-tuple-element.21), channel_id=1, source_target_pairs={{0,16},{4,24},{8,20},{12,28},{16,0},{20,8},{24,4},{28,12},{1,17},{... | collective-permute-start | bytes 319496 | tf_op jit(solution)/shard_map/ppermute | solution.py:661
  6.6 0.7 %collective-permute-start.3 = (f32[2,13,8,128]{3,2,1,0:T(8,128)S(1)}, f32[2,13,8,128]{3,2,1,0:T(8,128)S(1)}, u32[]{:S(2)}, u32[]{:S(2)}) collective-permute-start(f32[2,13,8,128]{3,2,1,0:T(8,128)S(1)} %get-tuple-element.21), channel_id=1, source_target_pairs={{0,0},{4,8},{8,4},{12,12},{1,1},{5,9},{9,5},{13,13},{2,2},{6,10},{... | collective-permute-start | bytes 319496 | tf_op jit(solution)/shard_map/ppermute | solution.py:660
  7.3 0.5 %collective-permute-done.1.refs_2_.pair = f32[2,13,8,128]{3,2,1,0:T(8,128)S(1)} collective-permute-done((f32[2,13,8,128]{3,2,1,0:T(8,128)S(1)}, f32[2,13,8,128]{3,2,1,0:T(8,128)S(1)}, u32[]{:S(2)}, u32[]{:S(2)}) %collective-permute-start.1) | collective-permute-done | bytes 106528 | tf_op jit(solution)/shard_map/ppermute | solution.py:658
  7.8 0.0 collective-permute-done.refs_1_.other
  7.8 0.2 pack.2
  8.0 5.8 %collective-permute-start.5 = (f32[45,8,128]{2,1,0:T(8,128)S(1)}, f32[45,8,128]{2,1,0:T(8,128)S(1)}, u32[]{:S(2)}, u32[]{:S(2)}) collective-permute-start(f32[45,8,128]{2,1,0:T(8,128)S(1)} %get-tuple-element.22), channel_id=1, source_target_pairs={{0,0},{1,2},{2,1},{3,3},{4,4},{5,6},{6,5},{7,7},{8,8},{9,10},{10,9... | collective-permute-start | bytes 552968 | tf_op jit(solution)/shard_map/ppermute | solution.py:674
  13.8 0.1 collective-permute-start.6
  13.9 0.0 collective-permute-done.4.refs_1_.inner_other
  13.9 0.1 pack.3
  14.1 2.3 %collective-permute-start.7 = (f32[39,8,128]{2,1,0:T(8,128)S(1)}, f32[39,8,128]{2,1,0:T(8,128)S(1)}, u32[]{:S(2)}, u32[]{:S(2)}) collective-permute-start(f32[39,8,128]{2,1,0:T(8,128)S(1)} %get-tuple-element.24), channel_id=1, source_target_pairs={{0,0},{1,2},{2,1},{3,3},{4,4},{5,6},{6,5},{7,7},{8,8},{9,10},{10,9... | collective-permute-start | bytes 479240 | tf_op jit(solution)/shard_map/ppermute | solution.py:674
  16.4 0.1 collective-permute-start.8
  16.5 4.2 %collective-permute-done.7.refs_2_ = f32[39,8,128]{2,1,0:T(8,128)S(1)} collective-permute-done((f32[39,8,128]{2,1,0:T(8,128)S(1)}, f32[39,8,128]{2,1,0:T(8,128)S(1)}, u32[]{:S(2)}, u32[]{:S(2)}) %collective-permute-start.7) | collective-permute-done | bytes 159776 | tf_op jit(solution)/shard_map/ppermute | solution.py:674
  20.7 0.0 collective-permute-done.8.refs_3_
  20.7 0.0 collective-permute-done.5.refs_0_
  20.7 0.0 collective-permute-done.6.refs_1_
  20.7 2.9 %down.1 = (f32[4,42,8,128]{3,2,1,0:T(8,128)S(1)}, f32[4,42,8,128]{3,2,1,0:T(8,128)S(1)}, f32[4,42,8,128]{3,2,1,0:T(8,128)S(1)}, f32[4,42,8,128]{3,2,1,0:T(8,128)...) custom-call(f32[2,16,8,128]{3,2,1,0:T(8,128)S(1)} %get-tuple-element, ...), custom_call_target="tpu_custom_call" | custom-call | tf_op jit(solution)/shard_map/down/pallas_call | solution.py:680
  23.6 3.5 %collective-permute-start.9 = (f32[2,12,8,128]{3,2,1,0:T(8,128)S(1)}, f32[2,12,8,128]{3,2,1,0:T(8,128)S(1)}, u32[]{:S(2)}, u32[]{:S(2)}) collective-permute-start(f32[2,12,8,128]{3,2,1,0:T(8,128)S(1)} %get-tuple-element.27), channel_id=1, source_target_pairs={{0,8},{8,0},{4,12},{12,4},{1,9},{9,1},{5,13},{13,5},{2,10},{10,2},... | collective-permute-start | bytes 294920 | tf_op jit(solution)/shard_map/ppermute | solution.py:694
  27.2 0.5 %collective-permute-start.10 = (f32[2,4,8,128]{3,2,1,0:T(8,128)S(1)}, f32[2,4,8,128]{3,2,1,0:T(8,128)S(1)}, u32[]{:S(2)}, u32[]{:S(2)}) collective-permute-start(f32[2,4,8,128]{3,2,1,0:T(8,128)S(1)} %get-tuple-element.28), channel_id=1, source_target_pairs={{0,4},{4,0},{8,12},{12,8},{1,5},{5,1},{9,13},{13,9},{2,6},{6,2},{1... | collective-permute-start | bytes 98312 | tf_op jit(solution)/shard_map/ppermute | solution.py:695
  27.7 2.8 %collective-permute-done.10.near = f32[2,4,8,128]{3,2,1,0:T(8,128)S(1)} collective-permute-done((f32[2,4,8,128]{3,2,1,0:T(8,128)S(1)}, f32[2,4,8,128]{3,2,1,0:T(8,128)S(1)}, u32[]{:S(2)}, u32[]{:S(2)}) %collective-permute-start.10) | collective-permute-done | bytes 32800 | tf_op jit(solution)/shard_map/ppermute | solution.py:695
  30.4 4.0 %up.1 = (f32[8,16,128]{2,1,0:T(8,128)}, f32[8,16,128]{2,1,0:T(8,128)}) custom-call(f32[2,16,8,128]{3,2,1,0:T(8,128)S(1)} %get-tuple-element.26.pay, f32[2,12,8,128]{3,2,1,0:T(8,128)S(1)} %collective-permute-done.9.far, f32[2,4,8,128]{3,2,1,0:T(8,128)S(1)} %collective-permute-done.10.near, f32[4,42,8,128]{3,2,1,0:T(8,128)S(1)} %get-tuple-element.29.right, ...), custom_call_target="tpu_custom_call" | custom-call | tf_op jit(solution)/shard_map/up/pallas_call | solution.py:698
  (4 shorter events, 0.0 us)
Async XLA Ops:
  1.8 6.0 %collective-permute-start = (f32[2,16,8,128]{3,2,1,0:T(8,128)S(1)}, f32[2,16,8,128]{3,2,1,0:T(8,128)S(1)}, u32[]{:S(2)}, u32[]{:S(2)}) collective-permute-start(f32[2,16,8,128]{3,2,1,0:T(8,128)S(1)} %get-tuple-element.19.refs_0_.mine), channel_id=1, source_target_pairs={{0,16},{16,0},{1,17},{17,1},{2,18},{18,2},{3,19},{19,3},{4,20},{20... | collective-permute-start | bytes 393224 | tf_op jit(solution)/shard_map/ppermute | solution.py:657
  4.0 3.9 %collective-permute-start.1 = (f32[2,13,8,128]{3,2,1,0:T(8,128)S(1)}, f32[2,13,8,128]{3,2,1,0:T(8,128)S(1)}, u32[]{:S(2)}, u32[]{:S(2)}) collective-permute-start(f32[2,13,8,128]{3,2,1,0:T(8,128)S(1)} %get-tuple-element.20), channel_id=1, source_target_pairs={{0,4},{4,0},{8,12},{12,8},{1,5},{5,1},{9,13},{13,9},{2,6},{6,2},{1... | collective-permute-start | bytes 319496 | tf_op jit(solution)/shard_map/ppermute | solution.py:658
  5.3 8.7 %collective-permute-start.2 = (f32[2,13,8,128]{3,2,1,0:T(8,128)S(1)}, f32[2,13,8,128]{3,2,1,0:T(8,128)S(1)}, u32[]{:S(2)}, u32[]{:S(2)}) collective-permute-start(f32[2,13,8,128]{3,2,1,0:T(8,128)S(1)} %get-tuple-element.20), channel_id=1, source_target_pairs={{0,20},{4,16},{8,28},{12,24},{16,4},{20,0},{24,12},{28,8},{1,21},{... | collective-permute-start | bytes 319496 | tf_op jit(solution)/shard_map/ppermute | solution.py:659
  5.3 8.7 %collective-permute-start.4 = (f32[2,13,8,128]{3,2,1,0:T(8,128)S(1)}, f32[2,13,8,128]{3,2,1,0:T(8,128)S(1)}, u32[]{:S(2)}, u32[]{:S(2)}) collective-permute-start(f32[2,13,8,128]{3,2,1,0:T(8,128)S(1)} %get-tuple-element.21), channel_id=1, source_target_pairs={{0,16},{4,24},{8,20},{12,28},{16,0},{20,8},{24,4},{28,12},{1,17},{... | collective-permute-start | bytes 319496 | tf_op jit(solution)/shard_map/ppermute | solution.py:661
  6.6 7.3 %collective-permute-start.3 = (f32[2,13,8,128]{3,2,1,0:T(8,128)S(1)}, f32[2,13,8,128]{3,2,1,0:T(8,128)S(1)}, u32[]{:S(2)}, u32[]{:S(2)}) collective-permute-start(f32[2,13,8,128]{3,2,1,0:T(8,128)S(1)} %get-tuple-element.21), channel_id=1, source_target_pairs={{0,0},{4,8},{8,4},{12,12},{1,1},{5,9},{9,5},{13,13},{2,2},{6,10},{... | collective-permute-start | bytes 319496 | tf_op jit(solution)/shard_map/ppermute | solution.py:660
  8.0 12.7 %collective-permute-start.5 = (f32[45,8,128]{2,1,0:T(8,128)S(1)}, f32[45,8,128]{2,1,0:T(8,128)S(1)}, u32[]{:S(2)}, u32[]{:S(2)}) collective-permute-start(f32[45,8,128]{2,1,0:T(8,128)S(1)} %get-tuple-element.22), channel_id=1, source_target_pairs={{0,0},{1,2},{2,1},{3,3},{4,4},{5,6},{6,5},{7,7},{8,8},{9,10},{10,9... | collective-permute-start | bytes 552968 | tf_op jit(solution)/shard_map/ppermute | solution.py:674
  13.8 6.9 %collective-permute-start.6 = (f32[45,8,128]{2,1,0:T(8,128)S(1)}, f32[45,8,128]{2,1,0:T(8,128)S(1)}, u32[]{:S(2)}, u32[]{:S(2)}) collective-permute-start(f32[45,8,128]{2,1,0:T(8,128)S(1)} %get-tuple-element.23), channel_id=1, source_target_pairs={{0,1},{1,0},{2,3},{3,2},{4,5},{5,4},{6,7},{7,6},{8,9},{9,8},{10,11... | collective-permute-start | bytes 552968 | tf_op jit(solution)/shard_map/ppermute | solution.py:674
  14.1 6.6 %collective-permute-start.7 = (f32[39,8,128]{2,1,0:T(8,128)S(1)}, f32[39,8,128]{2,1,0:T(8,128)S(1)}, u32[]{:S(2)}, u32[]{:S(2)}) collective-permute-start(f32[39,8,128]{2,1,0:T(8,128)S(1)} %get-tuple-element.24), channel_id=1, source_target_pairs={{0,0},{1,2},{2,1},{3,3},{4,4},{5,6},{6,5},{7,7},{8,8},{9,10},{10,9... | collective-permute-start | bytes 479240 | tf_op jit(solution)/shard_map/ppermute | solution.py:674
  16.4 4.3 %collective-permute-start.8 = (f32[39,8,128]{2,1,0:T(8,128)S(1)}, f32[39,8,128]{2,1,0:T(8,128)S(1)}, u32[]{:S(2)}, u32[]{:S(2)}) collective-permute-start(f32[39,8,128]{2,1,0:T(8,128)S(1)} %get-tuple-element.25), channel_id=1, source_target_pairs={{0,1},{1,0},{2,3},{3,2},{4,5},{5,4},{6,7},{7,6},{8,9},{9,8},{10,11... | collective-permute-start | bytes 479240 | tf_op jit(solution)/shard_map/ppermute | solution.py:674
  23.6 6.8 %collective-permute-start.9 = (f32[2,12,8,128]{3,2,1,0:T(8,128)S(1)}, f32[2,12,8,128]{3,2,1,0:T(8,128)S(1)}, u32[]{:S(2)}, u32[]{:S(2)}) collective-permute-start(f32[2,12,8,128]{3,2,1,0:T(8,128)S(1)} %get-tuple-element.27), channel_id=1, source_target_pairs={{0,8},{8,0},{4,12},{12,4},{1,9},{9,1},{5,13},{13,5},{2,10},{10,2},... | collective-permute-start | bytes 294920 | tf_op jit(solution)/shard_map/ppermute | solution.py:694
  27.2 3.3 %collective-permute-start.10 = (f32[2,4,8,128]{3,2,1,0:T(8,128)S(1)}, f32[2,4,8,128]{3,2,1,0:T(8,128)S(1)}, u32[]{:S(2)}, u32[]{:S(2)}) collective-permute-start(f32[2,4,8,128]{3,2,1,0:T(8,128)S(1)} %get-tuple-element.28), channel_id=1, source_target_pairs={{0,4},{4,0},{8,12},{12,8},{1,5},{5,1},{9,13},{13,9},{2,6},{6,2},{1... | collective-permute-start | bytes 98312 | tf_op jit(solution)/shard_map/ppermute | solution.py:695

commit v7 on v6

--- a/solution.py
+++ b/solution.py
@@ -269,9 +269,9 @@
 
 class Level:
     def __init__(self, refs, split, step, scale, unroll, pad=1):
-        self.coef, self.right, self.face_x, self.face_y, self.face_z, self.edge_x, self.inverse, self.values, self.update = refs
-        self.parts, self.rows = self.inverse.shape[:2]
-        self.tile = self.inverse.shape[2:]
+        self.right, self.diagonal, *self.sides, self.values, self.update, self.coef, self.source = refs
+        self.parts, self.rows = self.right.shape[:2]
+        self.tile = self.right.shape[2:]
         self.split, self.step, self.half, self.unroll, self.pad = split, step, 0.5 * scale, unroll, pad
         self.first = tile_place(self.tile, 0) < step
         self.last = tile_place(self.tile, 0) >= self.tile[0] - step
@@ -281,17 +281,17 @@
 
     def clear(self):
         for i in range(self.rows):
-            self.coef[0, i] = self.values[0, i] = self.right[0, i] = jnp.zeros(self.tile, jnp.float32)
+            self.coef[0, i] = self.values[0, i] = self.source[0, i] = jnp.zeros(self.tile, jnp.float32)
 
     def next_x(self, v, part):
         if self.split and part < 2:
             return v[part + 2]
-        return jnp.where(self.last, 0.0, turn(v[part - 2 if self.split else part], -self.step, 0))
-
-    def last_x(self, v, part, at_edge):
+        return turn(v[part - 2 if self.split else part], -self.step, 0)
+
+    def last_x(self, v, part):
         if self.split and part >= 2:
             return v[part - 2]
-        return jnp.where(self.first, at_edge[part], turn(v[part + 2 if self.split else part], self.step, 0))
+        return turn(v[part + 2 if self.split else part], self.step, 0)
 
     def next_z(self, v, part):
         if self.split and part % 2 == 0:
@@ -303,86 +303,77 @@
             return v[part - 1]
         return turn(v[part + 1 if self.split else part], self.step, 1)
 
-    def set_faces(self, use):
+    def begin(self, use):
         half = self.half
         parts = range(self.parts)
+        first = smoothing_weights()[0][1]
 
         def body(i, carry):
             here, below = carry
             above = self.read(self.coef, i + 1)
+            source = self.read(self.source, i)
             upper = [half * (here[p] + above[p]) for p in parts]
-            along_x = [half * (here[p] + self.next_x(here, p)) for p in parts]
+            to_next = [here[p] + self.next_x(here, p) for p in parts]
+            along_x = []
+            for p in parts:
+                at_end = not self.split or p >= 2
+                along_x.append(half * (jnp.where(self.last, here[p], to_next[p]) if at_end else to_next[p]))
             along_z = [half * (here[p] + self.next_z(here, p)) for p in parts]
-            edge = [half * here[p] for p in range(self.edge_x.shape[0])]
-            inverse = []
+            fields = [[] for _ in range(8)]
             for p in parts:
-                diagonal = (
-                    (below[p] + upper[p])
-                    + (along_x[p] + self.last_x(along_x, p, edge))
-                    + (along_z[p] + self.last_z(along_z, p))
-                )
-                inside = here[p] > 0.0
-                inverse.append(jnp.where(inside, 1.0 / diagonal, 0.0))
-            stores = [
-                (self.face_y, i, upper),
-                (self.face_x, i, along_x),
-                (self.face_z, i, along_z),
-                (self.edge_x, i, edge),
-                (self.inverse, i, inverse),
-            ]
-            return (above, upper), stores + use(i, here, inverse)
+                to_last = self.last_x(along_x, p)
+                faces = [upper[p], below[p], along_x[p], to_last, along_z[p], self.last_z(along_z, p)]
+                inner = list(faces)
+                if not self.split or p >= 2:
+                    inner[2] = jnp.where(self.last, 0.0, faces[2])
+                if not self.split or p < 2:
+                    faces[3] = jnp.where(self.first, half * here[p], to_last)
+                    inner[3] = jnp.where(self.first, 0.0, to_last)
+                diagonal = (faces[0] + faces[1]) + (faces[2] + faces[3]) + (faces[4] + faces[5])
+                inverse = jnp.where(here[p] > 0.0, 1.0 / diagonal, 0.0)
+                for field, value in zip(fields, [source[p] * inverse, diagonal, *(face * inverse for face in inner)]):
+                    field.append(value)
+            step = [value * first for value in fields[0]]
+            refs = (self.right, self.diagonal, *self.sides, self.values, self.update)
+            stores = [(ref, i, field) for ref, field in zip(refs, [*fields, step, step])]
+            return (above, upper), stores + use(i, here)
 
         low, high = self.pad, self.rows - self.pad
         here, before = self.read(self.coef, low), self.read(self.coef, low - 1)
-        face = [half * (here[p] + before[p]) for p in parts]
-        for p in parts:
-            self.face_y[p, low - 1] = face[p]
-        run(low, high - low, body, (here, face), self.unroll)
+        run(low, high - low, body, (here, [half * (here[p] + before[p]) for p in parts]), self.unroll)
 
     def sweep(self, low, count, use):
         parts = range(self.parts)
 
         def body(i, carry):
-            here, flux_low = carry
+            below, here = carry
             above = self.read(self.values, i + 1)
-            face_x, face_y, face_z, edge_x = (
-                self.read(ref, i) for ref in (self.face_x, self.face_y, self.face_z, self.edge_x)
-            )
-            flux_high = [face_y[p] * (above[p] - here[p]) for p in parts]
-            flux_x = [face_x[p] * (self.next_x(here, p) - here[p]) for p in parts]
-            flux_z = [face_z[p] * (self.next_z(here, p) - here[p]) for p in parts]
-            at_edge = [face * value for face, value in zip(edge_x, here)]
-            applied = [
-                (flux_low[p] - flux_high[p])
-                + (self.last_x(flux_x, p, at_edge) - flux_x[p])
-                + (self.last_z(flux_z, p) - flux_z[p])
+            right = self.read(self.right, i)
+            up, down, ahead, behind, right_z, left_z = (self.read(ref, i) for ref in self.sides)
+            left = [
+                ((right[p] - here[p]) + (up[p] * above[p] + down[p] * below[p]))
+                + (ahead[p] * self.next_x(here, p) + behind[p] * self.last_x(here, p))
+                + (right_z[p] * self.next_z(here, p) + left_z[p] * self.last_z(here, p))
                 for p in parts
             ]
-            return (above, flux_high), use(i, applied, here)
-
-        here, before = self.read(self.values, low), self.read(self.values, low - 1)
-        face = self.read(self.face_y, low - 1)
-        run(low, count, body, (here, [face[p] * (here[p] - before[p]) for p in parts]), self.unroll)
-
-    def from_zero(self, i, inverse):
-        first = smoothing_weights()[0][1]
-        right = self.read(self.right, i)
-        step = [right[p] * (inverse[p] * first) for p in range(self.parts)]
-        return [(self.update, i, step), (self.values, i, step)]
+            return (here, above), use(i, left, here)
+
+        run(low, count, body, (self.read(self.values, low - 1), self.read(self.values, low)), self.unroll)
 
     def smooth(self, low, count, weight):
         keep, gain = weight
 
-        def use(i, applied, here):
-            right = self.read(self.right, i)
-            inverse = self.read(self.inverse, i)
-            step = [(right[p] - applied[p]) * (inverse[p] * gain) for p in range(self.parts)]
+        def use(i, left, here):
+            step = [gain * left[p] for p in range(self.parts)]
             if keep:
                 update = self.read(self.update, i)
                 step = [keep * update[p] + step[p] for p in range(self.parts)]
             return [(self.update, i, step), (self.values, i, [here[p] + step[p] for p in range(self.parts)])]
 
         self.sweep(low, count, use)
+
+    def residual(self, i, left):
+        return [value * factor for value, factor in zip(left, self.read(self.diagonal, i))]
 
 
 def total(items):
@@ -448,8 +439,8 @@
 
 def down_kernel(mine, other, pair, pair_other, inner, inner_other, *refs):
     edges, refs = refs[: 2 * len(GROUPS)], refs[2 * len(GROUPS) :]
-    right, face_x, face_y, face_z, edge_x, inverse, values, pay_out, far_out, near_out, coef, update, sums, coefs = refs
-    level = Level((coef, right, face_x, face_y, face_z, edge_x, inverse, values, update), True, 1, 1.0, UNROLL_FINE)
+    fields, (pay_out, far_out, near_out), (update, coef, right, sums, coefs) = refs[:9], refs[9:12], refs[12:]
+    level = Level((*fields, update, coef, right), True, 1, 1.0, UNROLL_FINE)
     by, bx, bz = mine.shape[1:]
     halo = pair.shape[1]
     at_x, at_y, at_z, core, odd = place()
@@ -506,18 +497,14 @@
 
         run(0, count, assemble, 0, 16)
 
-    def begin(i, here, inverse):
-        return level.from_zero(i, inverse) + [(coefs, i, [total(here)])]
-
-    level.set_faces(begin)
+    level.begin(lambda i, here: [(coefs, i, [total(here)])])
     edge = 1
     for weight in smoothing_weights()[1:]:
         edge += 1
         level.smooth(edge, level.rows - 2 * edge, weight)
 
-    def leftover(i, applied, here):
-        right = level.read(level.right, i)
-        return [(sums, i, [total(right[p] - applied[p] for p in range(level.parts))])]
+    def leftover(i, left, here):
+        return [(sums, i, [total(level.residual(i, left))])]
 
     edge += 1
     level.sweep(edge, level.rows - 2 * edge, leftover)
@@ -529,11 +516,12 @@
         near_out[which] = pay_out[which, pl.ds(shared * (1 + odd), shared)]
 
 
-def up_kernel(pay, far, near, right, face_x, face_y, face_z, edge_x, inverse, start, solution_out, residual_out, *refs):
-    level1 = Level(refs[:9], False, 1, 0.25, UNROLL_COARSE, near.shape[1])
-    level2 = Level(refs[9:18], False, 2, 0.0625, UNROLL_COARSE)
-    values, update, sums, moved, rows_out = refs[18:]
-    fine = Level((None, right, face_x, face_y, face_z, edge_x, inverse, values, update), True, 1, 1.0, UNROLL_FINE)
+def up_kernel(pay, far, near, *refs):
+    fields, start, (solution_out, residual_out), refs = refs[:8], refs[8], refs[9:11], refs[11:]
+    level1 = Level(refs[:12], False, 1, 0.25, UNROLL_COARSE, near.shape[1])
+    level2 = Level(refs[12:24], False, 2, 0.0625, UNROLL_COARSE)
+    values, update, sums, moved, rows_out = refs[24:]
+    fine = Level((*fields, values, update, None, None), True, 1, 1.0, UNROLL_FINE)
     by, bx, bz = pay.shape[1:]
     shared = near.shape[1]
     at_x, at_y, _, _, odd = place()
@@ -545,7 +533,7 @@
     own1 = (by // 2) * at_y
     far1 = (by // 2) * (at_y + 2 - 4 * (at_y // 2)) + shared * (1 - odd)
     near1 = (by // 2) * (at_y + 1 - 2 * odd) + shared + shared * (1 - odd)
-    for which, ref in enumerate((level1.right, level1.coef)):
+    for which, ref in enumerate((level1.source, level1.coef)):
         for piece, at in ((pay, own1), (far, far1), (near, near1)):
             for y in range(piece.shape[1]):
                 ref[0, at + y] = piece[which, y]
@@ -559,19 +547,19 @@
         values = values + jnp.where(even_lane, turn(values, -1, 1), turn(values, 1, 1))
         return 0.125 * (values + jnp.where(even_row, turn(values, -1, 0), turn(values, 1, 0)))
 
-    level1.set_faces(lambda i, here, inverse: level1.from_zero(i, inverse))
+    level1.begin(lambda i, here: [])
     for weight in weights[1:]:
         level1.smooth(low1, high1 - low1, weight)
 
-    def leftover1(i, applied, here):
-        return [(sums, i, [level1.right[0, i] - applied[0]])]
+    def leftover1(i, left, here):
+        return [(sums, i, level1.residual(i, left))]
 
     level1.sweep(low1, high1 - low1, leftover1)
     for j in range(1, n2):
-        level2.right[0, j] = pair_cells(sums[0, low1 + 2 * j - 2] + sums[0, low1 + 2 * j - 1])
+        level2.source[0, j] = pair_cells(sums[0, low1 + 2 * j - 2] + sums[0, low1 + 2 * j - 1])
         level2.coef[0, j] = pair_cells(level1.coef[0, low1 + 2 * j - 2] + level1.coef[0, low1 + 2 * j - 1])
 
-    level2.set_faces(lambda i, here, inverse: level2.from_zero(i, inverse))
+    level2.begin(lambda i, here: [])
     for weight in weights[1:]:
         level2.smooth(1, n2 - 1, weight)
 
@@ -598,10 +586,9 @@
     own_lane = tile_place(tile, 1) < bz // 2
     top = tile_place(tile, 0) < bx // 2
 
-    def finish(i, applied, here):
-        right_row = fine.read(right, i)
+    def finish(i, left, here):
         stores = []
-        for slot, field in enumerate((here, [right_row[p] - applied[p] for p in range(fine.parts)])):
+        for slot, field in enumerate((here, fine.residual(i, left))):
             cells = []
             for odd_z in (0, 1):
                 one, two = field[odd_z], field[2 + odd_z]
@@ -676,18 +663,18 @@
     edges = [part for group in GROUPS for part in share([blocks[kind] for kind in group])]
 
     rows = by + 2 * halo
-    field, half_field = (4, rows, bx, bz), (2, rows, bx, bz)
+    field = (4, rows, bx, bz)
     *fine, pay, far, near = pl.pallas_call(
         down_kernel,
         out_shape=(
-            *(shape(*(half_field if number == 4 else field)) for number in range(7)),
+            *[shape(*field)] * 9,
             shape(2, by, bx, bz),
             shape(2, by - shared, bx, bz),
             shape(2, shared, bx, bz),
         ),
         in_specs=[in_vmem] * (6 + 2 * len(GROUPS)),
-        out_specs=(in_vmem,) * 10,
-        scratch_shapes=[vmem(*field), vmem(*field), vmem(1, rows, bx, bz), vmem(1, rows, bx, bz)],
+        out_specs=(in_vmem,) * 12,
+        scratch_shapes=[*[vmem(*field)] * 3, vmem(1, rows, bx, bz), vmem(1, rows, bx, bz)],
         compiler_params=params,
         name="down",
     )(*blocks, *edges)
@@ -698,11 +685,11 @@
     return pl.pallas_call(
         up_kernel,
         out_shape=(shape(bx, by, bz),) * 2,
-        in_specs=[in_vmem] * 10,
+        in_specs=[in_vmem] * 12,
         out_specs=(in_vmem,) * 2,
         scratch_shapes=[
-            *[vmem(1, rows1, bx, bz)] * 9,
-            *[vmem(1, rows2, bx, bz)] * 9,
+            *[vmem(1, rows1, bx, bz)] * 12,
+            *[vmem(1, rows2, bx, bz)] * 12,
             vmem(*field),
             vmem(*field),
             vmem(1, rows1, bx, bz),

time: 34.6 us -> 34.1 us (0.986)
  Pallas kernels: 7.51 us -> 6.97 us
    pallas_call x1, Pallas kernels: 3.97 us -> 3.37 us  [per_device_two_rounds(): pl.pallas_call(up_kernel, out_shape=(shape(bx, by, bz),) * 2, in_specs=[i...]
where the time goes in v7:
time: 34.1 us; the launch traced here: 33.9 us
  starting transfers between devices  17.8 us (52%)
  waiting for transfers between devices  7.51 us (22%)
  Pallas kernels  6.97 us (20%)
  other arithmetic  0.88 us (3%)
  between operations  0.73 us (2%)
    ppermute x2, starting transfers between devices, share(): lax.ppermute(to_mid, 'gz', swap_inner)  8.16 us
    ppermute x2, waiting for transfers between devices, share(): lax.ppermute(to_mid, 'gz', swap_inner)  4.19 us
    ppermute x1, starting transfers between devices, per_device_two_rounds(): far = lax.ppermute(far, 'gy', [(0, 2), (2, 0), (1, 3), (3, 1)])  3.55 us
    pallas_call x1, Pallas kernels, per_device_two_rounds(): pl.pallas_call(up_kernel, out_shape=(shape(bx, by, bz),) * 2, in_specs=[i...  3.37 us
    pallas_call x1, Pallas kernels, per_device_two_rounds(): pl.pallas_call(down_kernel, out_shape=(*[shape(*field)] * 9, shape(2, by,...  2.96 us
    ppermute x1, waiting for transfers between devices, per_device_two_rounds(): near = lax.ppermute(near, 'gy', swap_pairs)  2.77 us
    ppermute x1, starting transfers between devices, per_device_two_rounds(): lax.ppermute(mine, 'gx', [(0, 1), (1, 0)])  2.11 us
    ppermute x1, starting transfers between devices, per_device_two_rounds(): lax.ppermute(for_inner, ('gx', 'gy'), across_x(inner))  1.35 us
  transfers between devices with their start and end apart: 11, of which 3 were waited for; matrix products, arithmetic and copies ran while one was open for 0% of the time, Pallas kernels for 1%

profile of v7, /device:TPU:1, one launch (start us, length us, event | category | flops | bytes accessed | tf_op | source)
XLA Modules:
  0.0 33.9 jit_solution(6200102268855556150)
XLA Ops:
  0.6 0.9 %pad_maximum_fusion.fields = f32[2,8,16,128]{3,2,1,0:T(8,128)S(1)} fusion(f32[1,8,16,128]{3,2,1,0:T(8,128)} %bitcast.2, f32[1,8,16,128]{3,2,1,0:T(8,128)} %bitcast.3), kind=kLoop, calls=%fused_computation | loop fusion | flops 32768 | bytes 262144 | tf_op jit(solution)/shard_map/stack | solution.py:633
  1.5 0.3 split.1
  1.8 2.1 %collective-permute-start = (f32[2,16,8,128]{3,2,1,0:T(8,128)S(1)}, f32[2,16,8,128]{3,2,1,0:T(8,128)S(1)}, u32[]{:S(2)}, u32[]{:S(2)}) collective-permute-start(f32[2,16,8,128]{3,2,1,0:T(8,128)S(1)} %get-tuple-element.21.refs_0_.mine), channel_id=1, source_target_pairs={{0,16},{16,0},{1,17},{17,1},{2,18},{18,2},{3,19},{19,3},{4,20},{20... | collective-permute-start | bytes 393224 | tf_op jit(solution)/shard_map/ppermute | solution.py:644
  4.0 1.3 %collective-permute-start.1 = (f32[2,13,8,128]{3,2,1,0:T(8,128)S(1)}, f32[2,13,8,128]{3,2,1,0:T(8,128)S(1)}, u32[]{:S(2)}, u32[]{:S(2)}) collective-permute-start(f32[2,13,8,128]{3,2,1,0:T(8,128)S(1)} %get-tuple-element.22), channel_id=1, source_target_pairs={{0,4},{4,0},{8,12},{12,8},{1,5},{5,1},{9,13},{13,9},{2,6},{6,2},{1... | collective-permute-start | bytes 319496 | tf_op jit(solution)/shard_map/ppermute | solution.py:645
  5.3 1.4 %collective-permute-start.4 = (f32[2,13,8,128]{3,2,1,0:T(8,128)S(1)}, f32[2,13,8,128]{3,2,1,0:T(8,128)S(1)}, u32[]{:S(2)}, u32[]{:S(2)}) collective-permute-start(f32[2,13,8,128]{3,2,1,0:T(8,128)S(1)} %get-tuple-element.23), channel_id=1, source_target_pairs={{0,16},{4,24},{8,20},{12,28},{16,0},{20,8},{24,4},{28,12},{1,17},{... | collective-permute-start | bytes 319496 | tf_op jit(solution)/shard_map/ppermute | solution.py:648
  6.6 0.7 %collective-permute-start.3 = (f32[2,13,8,128]{3,2,1,0:T(8,128)S(1)}, f32[2,13,8,128]{3,2,1,0:T(8,128)S(1)}, u32[]{:S(2)}, u32[]{:S(2)}) collective-permute-start(f32[2,13,8,128]{3,2,1,0:T(8,128)S(1)} %get-tuple-element.23), channel_id=1, source_target_pairs={{0,0},{4,8},{8,4},{12,12},{1,1},{5,9},{9,5},{13,13},{2,2},{6,10},{... | collective-permute-start | bytes 319496 | tf_op jit(solution)/shard_map/ppermute | solution.py:647
  7.3 0.5 %collective-permute-done.1.refs_2_.pair = f32[2,13,8,128]{3,2,1,0:T(8,128)S(1)} collective-permute-done((f32[2,13,8,128]{3,2,1,0:T(8,128)S(1)}, f32[2,13,8,128]{3,2,1,0:T(8,128)S(1)}, u32[]{:S(2)}, u32[]{:S(2)}) %collective-permute-start.1) | collective-permute-done | bytes 106528 | tf_op jit(solution)/shard_map/ppermute | solution.py:645
  7.8 0.0 collective-permute-done.refs_1_.other
  7.8 0.2 pack.2
  8.0 5.8 %collective-permute-start.5 = (f32[45,8,128]{2,1,0:T(8,128)S(1)}, f32[45,8,128]{2,1,0:T(8,128)S(1)}, u32[]{:S(2)}, u32[]{:S(2)}) collective-permute-start(f32[45,8,128]{2,1,0:T(8,128)S(1)} %get-tuple-element.24), channel_id=1, source_target_pairs={{0,0},{1,2},{2,1},{3,3},{4,4},{5,6},{6,5},{7,7},{8,8},{9,10},{10,9... | collective-permute-start | bytes 552968 | tf_op jit(solution)/shard_map/ppermute | solution.py:661
  13.8 0.1 collective-permute-start.6
  13.9 0.0 collective-permute-done.4.refs_1_.inner_other
  13.9 0.0 collective-permute-done.3.refs_0_.inner
  13.9 0.1 pack.3
  14.1 2.3 %collective-permute-start.7 = (f32[39,8,128]{2,1,0:T(8,128)S(1)}, f32[39,8,128]{2,1,0:T(8,128)S(1)}, u32[]{:S(2)}, u32[]{:S(2)}) collective-permute-start(f32[39,8,128]{2,1,0:T(8,128)S(1)} %get-tuple-element.26), channel_id=1, source_target_pairs={{0,0},{1,2},{2,1},{3,3},{4,4},{5,6},{6,5},{7,7},{8,8},{9,10},{10,9... | collective-permute-start | bytes 479240 | tf_op jit(solution)/shard_map/ppermute | solution.py:661
  16.4 0.1 collective-permute-start.8
  16.5 4.2 %collective-permute-done.7.refs_2_ = f32[39,8,128]{2,1,0:T(8,128)S(1)} collective-permute-done((f32[39,8,128]{2,1,0:T(8,128)S(1)}, f32[39,8,128]{2,1,0:T(8,128)S(1)}, u32[]{:S(2)}, u32[]{:S(2)}) %collective-permute-start.7) | collective-permute-done | bytes 159776 | tf_op jit(solution)/shard_map/ppermute | solution.py:661
  20.7 0.0 collective-permute-done.8.refs_3_
  20.7 0.0 collective-permute-done.5.refs_0_
  20.7 3.0 %down.1 = (f32[4,42,8,128]{3,2,1,0:T(8,128)S(1)}, f32[4,42,8,128]{3,2,1,0:T(8,128)S(1)}, f32[4,42,8,128]{3,2,1,0:T(8,128)S(1)}, f32[4,42,8,128]{3,2,1,0:T(8,128)...) custom-call(f32[2,16,8,128]{3,2,1,0:T(8,128)S(1)} %get-tuple-element, ...), custom_call_target="tpu_custom_call" | custom-call | tf_op jit(solution)/shard_map/down/pallas_call | solution.py:667
  23.7 3.5 %collective-permute-start.9 = (f32[2,12,8,128]{3,2,1,0:T(8,128)S(1)}, f32[2,12,8,128]{3,2,1,0:T(8,128)S(1)}, u32[]{:S(2)}, u32[]{:S(2)}) collective-permute-start(f32[2,12,8,128]{3,2,1,0:T(8,128)S(1)} %get-tuple-element.29), channel_id=1, source_target_pairs={{0,8},{8,0},{4,12},{12,4},{1,9},{9,1},{5,13},{13,5},{2,10},{10,2},... | collective-permute-start | bytes 294920 | tf_op jit(solution)/shard_map/ppermute | solution.py:681
  27.2 0.5 %collective-permute-start.10 = (f32[2,4,8,128]{3,2,1,0:T(8,128)S(1)}, f32[2,4,8,128]{3,2,1,0:T(8,128)S(1)}, u32[]{:S(2)}, u32[]{:S(2)}) collective-permute-start(f32[2,4,8,128]{3,2,1,0:T(8,128)S(1)} %get-tuple-element.30), channel_id=1, source_target_pairs={{0,4},{4,0},{8,12},{12,8},{1,5},{5,1},{9,13},{13,9},{2,6},{6,2},{1... | collective-permute-start | bytes 98312 | tf_op jit(solution)/shard_map/ppermute | solution.py:682
  27.7 2.8 %collective-permute-done.10.near = f32[2,4,8,128]{3,2,1,0:T(8,128)S(1)} collective-permute-done((f32[2,4,8,128]{3,2,1,0:T(8,128)S(1)}, f32[2,4,8,128]{3,2,1,0:T(8,128)S(1)}, u32[]{:S(2)}, u32[]{:S(2)}) %collective-permute-start.10) | collective-permute-done | bytes 32800 | tf_op jit(solution)/shard_map/ppermute | solution.py:682
  30.5 3.4 %up.1 = (f32[8,16,128]{2,1,0:T(8,128)}, f32[8,16,128]{2,1,0:T(8,128)}) custom-call(f32[2,16,8,128]{3,2,1,0:T(8,128)S(1)} %get-tuple-element.28.pay, f32[2,12,8,128]{3,2,1,0:T(8,128)S(1)} %collective-permute-done.9.far, f32[2,4,8,128]{3,2,1,0:T(8,128)S(1)} %collective-permute-done.10.near, f32[4,42,8,128]{3,2,1,0:T(8,128)S(1)} %get-tuple-element.31.refs_0_, ...), custom_call_target="tpu_custom_call" | custom-call | tf_op jit(solution)/shard_map/up/pallas_call | solution.py:685
  (4 shorter events, 0.0 us)
Async XLA Ops:
  1.8 6.0 %collective-permute-start = (f32[2,16,8,128]{3,2,1,0:T(8,128)S(1)}, f32[2,16,8,128]{3,2,1,0:T(8,128)S(1)}, u32[]{:S(2)}, u32[]{:S(2)}) collective-permute-start(f32[2,16,8,128]{3,2,1,0:T(8,128)S(1)} %get-tuple-element.21.refs_0_.mine), channel_id=1, source_target_pairs={{0,16},{16,0},{1,17},{17,1},{2,18},{18,2},{3,19},{19,3},{4,20},{20... | collective-permute-start | bytes 393224 | tf_op jit(solution)/shard_map/ppermute | solution.py:644
  4.0 3.9 %collective-permute-start.1 = (f32[2,13,8,128]{3,2,1,0:T(8,128)S(1)}, f32[2,13,8,128]{3,2,1,0:T(8,128)S(1)}, u32[]{:S(2)}, u32[]{:S(2)}) collective-permute-start(f32[2,13,8,128]{3,2,1,0:T(8,128)S(1)} %get-tuple-element.22), channel_id=1, source_target_pairs={{0,4},{4,0},{8,12},{12,8},{1,5},{5,1},{9,13},{13,9},{2,6},{6,2},{1... | collective-permute-start | bytes 319496 | tf_op jit(solution)/shard_map/ppermute | solution.py:645
  5.3 8.7 %collective-permute-start.2 = (f32[2,13,8,128]{3,2,1,0:T(8,128)S(1)}, f32[2,13,8,128]{3,2,1,0:T(8,128)S(1)}, u32[]{:S(2)}, u32[]{:S(2)}) collective-permute-start(f32[2,13,8,128]{3,2,1,0:T(8,128)S(1)} %get-tuple-element.22), channel_id=1, source_target_pairs={{0,20},{4,16},{8,28},{12,24},{16,4},{20,0},{24,12},{28,8},{1,21},{... | collective-permute-start | bytes 319496 | tf_op jit(solution)/shard_map/ppermute | solution.py:646
  5.3 8.7 %collective-permute-start.4 = (f32[2,13,8,128]{3,2,1,0:T(8,128)S(1)}, f32[2,13,8,128]{3,2,1,0:T(8,128)S(1)}, u32[]{:S(2)}, u32[]{:S(2)}) collective-permute-start(f32[2,13,8,128]{3,2,1,0:T(8,128)S(1)} %get-tuple-element.23), channel_id=1, source_target_pairs={{0,16},{4,24},{8,20},{12,28},{16,0},{20,8},{24,4},{28,12},{1,17},{... | collective-permute-start | bytes 319496 | tf_op jit(solution)/shard_map/ppermute | solution.py:648
  6.6 7.3 %collective-permute-start.3 = (f32[2,13,8,128]{3,2,1,0:T(8,128)S(1)}, f32[2,13,8,128]{3,2,1,0:T(8,128)S(1)}, u32[]{:S(2)}, u32[]{:S(2)}) collective-permute-start(f32[2,13,8,128]{3,2,1,0:T(8,128)S(1)} %get-tuple-element.23), channel_id=1, source_target_pairs={{0,0},{4,8},{8,4},{12,12},{1,1},{5,9},{9,5},{13,13},{2,2},{6,10},{... | collective-permute-start | bytes 319496 | tf_op jit(solution)/shard_map/ppermute | solution.py:647
  8.0 12.7 %collective-permute-start.5 = (f32[45,8,128]{2,1,0:T(8,128)S(1)}, f32[45,8,128]{2,1,0:T(8,128)S(1)}, u32[]{:S(2)}, u32[]{:S(2)}) collective-permute-start(f32[45,8,128]{2,1,0:T(8,128)S(1)} %get-tuple-element.24), channel_id=1, source_target_pairs={{0,0},{1,2},{2,1},{3,3},{4,4},{5,6},{6,5},{7,7},{8,8},{9,10},{10,9... | collective-permute-start | bytes 552968 | tf_op jit(solution)/shard_map/ppermute | solution.py:661
  13.8 6.9 %collective-permute-start.6 = (f32[45,8,128]{2,1,0:T(8,128)S(1)}, f32[45,8,128]{2,1,0:T(8,128)S(1)}, u32[]{:S(2)}, u32[]{:S(2)}) collective-permute-start(f32[45,8,128]{2,1,0:T(8,128)S(1)} %get-tuple-element.25), channel_id=1, source_target_pairs={{0,1},{1,0},{2,3},{3,2},{4,5},{5,4},{6,7},{7,6},{8,9},{9,8},{10,11... | collective-permute-start | bytes 552968 | tf_op jit(solution)/shard_map/ppermute | solution.py:661
  14.1 6.6 %collective-permute-start.7 = (f32[39,8,128]{2,1,0:T(8,128)S(1)}, f32[39,8,128]{2,1,0:T(8,128)S(1)}, u32[]{:S(2)}, u32[]{:S(2)}) collective-permute-start(f32[39,8,128]{2,1,0:T(8,128)S(1)} %get-tuple-element.26), channel_id=1, source_target_pairs={{0,0},{1,2},{2,1},{3,3},{4,4},{5,6},{6,5},{7,7},{8,8},{9,10},{10,9... | collective-permute-start | bytes 479240 | tf_op jit(solution)/shard_map/ppermute | solution.py:661
  16.4 4.3 %collective-permute-start.8 = (f32[39,8,128]{2,1,0:T(8,128)S(1)}, f32[39,8,128]{2,1,0:T(8,128)S(1)}, u32[]{:S(2)}, u32[]{:S(2)}) collective-permute-start(f32[39,8,128]{2,1,0:T(8,128)S(1)} %get-tuple-element.27), channel_id=1, source_target_pairs={{0,1},{1,0},{2,3},{3,2},{4,5},{5,4},{6,7},{7,6},{8,9},{9,8},{10,11... | collective-permute-start | bytes 479240 | tf_op jit(solution)/shard_map/ppermute | solution.py:661
  23.7 6.8 %collective-permute-start.9 = (f32[2,12,8,128]{3,2,1,0:T(8,128)S(1)}, f32[2,12,8,128]{3,2,1,0:T(8,128)S(1)}, u32[]{:S(2)}, u32[]{:S(2)}) collective-permute-start(f32[2,12,8,128]{3,2,1,0:T(8,128)S(1)} %get-tuple-element.29), channel_id=1, source_target_pairs={{0,8},{8,0},{4,12},{12,4},{1,9},{9,1},{5,13},{13,5},{2,10},{10,2},... | collective-permute-start | bytes 294920 | tf_op jit(solution)/shard_map/ppermute | solution.py:681
  27.2 3.3 %collective-permute-start.10 = (f32[2,4,8,128]{3,2,1,0:T(8,128)S(1)}, f32[2,4,8,128]{3,2,1,0:T(8,128)S(1)}, u32[]{:S(2)}, u32[]{:S(2)}) collective-permute-start(f32[2,4,8,128]{3,2,1,0:T(8,128)S(1)} %get-tuple-element.30), channel_id=1, source_target_pairs={{0,4},{4,0},{8,12},{12,8},{1,5},{5,1},{9,13},{13,9},{2,6},{6,2},{1... | collective-permute-start | bytes 98312 | tf_op jit(solution)/shard_map/ppermute | solution.py:682

commit v8 on v7

--- a/solution.py
+++ b/solution.py
@@ -634,17 +634,19 @@
 
     pairs = [1, 0, 3, 2]
     inner = [0, 2, 1, 3]
-    swap_pairs, swap_inner = list(enumerate(pairs)), list(enumerate(inner))
+    swap_pairs = list(enumerate(pairs))
 
     def across_x(partner):
         return [(4 * x + y, 4 * (1 - x) + partner[y]) for x in (0, 1) for y in range(4)]
+
+    swap_inner = [(4 * x + y, 4 * (1 - x if inner[y] == y else x) + inner[y]) for x in (0, 1) for y in range(4)]
 
     blocks = {
         "mine": mine,
         "other": lax.ppermute(mine, "gx", [(0, 1), (1, 0)]),
         "pair": lax.ppermute(for_pair, "gy", swap_pairs),
         "pair_other": lax.ppermute(for_pair, ("gx", "gy"), across_x(pairs)),
-        "inner": lax.ppermute(for_inner, "gy", swap_inner),
+        "inner": lax.ppermute(for_inner, "gy", list(enumerate(inner))),
         "inner_other": lax.ppermute(for_inner, ("gx", "gy"), across_x(inner)),
     }
     blocks = list(blocks.values())
@@ -658,7 +660,7 @@
             compiler_params=params,
             name="pack",
         )(*group)
-        return lax.ppermute(to_mid, "gz", swap_inner), lax.ppermute(to_sib, "gz", swap_pairs)
+        return lax.ppermute(to_mid, ("gx", "gz"), swap_inner), lax.ppermute(to_sib, "gz", swap_pairs)
 
     edges = [part for group in GROUPS for part in share([blocks[kind] for kind in group])]
 

time: 34.1 us -> 33.4 us (0.979)
  the two profiles are of different devices: /device:TPU:1 before, /device:TPU:0 now
where the time goes in v8:
time: 33.4 us; the launch traced here: 33.2 us
  starting transfers between devices  16.6 us (50%)
  waiting for transfers between devices  8.11 us (24%)
  Pallas kernels  6.96 us (21%)
  other arithmetic  0.88 us (3%)
  between operations  0.68 us (2%)
    ppermute x1, starting transfers between devices, per_device_two_rounds(): far = lax.ppermute(far, 'gy', [(0, 2), (2, 0), (1, 3), (3, 1)])  4.55 us
    ppermute x1, waiting for transfers between devices, per_device_two_rounds(): near = lax.ppermute(near, 'gy', swap_pairs)  3.72 us
    pallas_call x1, Pallas kernels, per_device_two_rounds(): pl.pallas_call(up_kernel, out_shape=(shape(bx, by, bz),) * 2, in_specs=[i...  3.37 us
    ppermute x1, starting transfers between devices, per_device_two_rounds(): lax.ppermute(mine, 'gx', [(0, 1), (1, 0)])  3 us
    pallas_call x1, Pallas kernels, per_device_two_rounds(): pl.pallas_call(down_kernel, out_shape=(*[shape(*field)] * 9, shape(2, by,...  2.96 us
    ppermute x2, starting transfers between devices, share(): lax.ppermute(to_sib, 'gz', swap_pairs)  2.41 us
    ppermute x2, waiting for transfers between devices, share(): lax.ppermute(to_mid, ('gx', 'gz'), swap_inner)  2.35 us
    ppermute x2, starting transfers between devices, share(): lax.ppermute(to_mid, ('gx', 'gz'), swap_inner)  2.29 us
  transfers between devices with their start and end apart: 11, of which 4 were waited for; matrix products, arithmetic and copies ran while one was open for 0% of the time, Pallas kernels for 1%

profile of v8, /device:TPU:0, one launch (start us, length us, event | category | flops | bytes accessed | tf_op | source)
XLA Modules:
  0.0 33.2 jit_solution(2713046144307265866)
XLA Ops:
  0.6 0.9 %pad_maximum_fusion.fields = f32[2,8,16,128]{3,2,1,0:T(8,128)S(1)} fusion(f32[1,8,16,128]{3,2,1,0:T(8,128)} %bitcast.2, f32[1,8,16,128]{3,2,1,0:T(8,128)} %bitcast.3), kind=kLoop, calls=%fused_computation | loop fusion | flops 32768 | bytes 262144 | tf_op jit(solution)/shard_map/stack | solution.py:633
  1.5 0.3 split.1
  1.8 3.0 %collective-permute-start = (f32[2,16,8,128]{3,2,1,0:T(8,128)S(1)}, f32[2,16,8,128]{3,2,1,0:T(8,128)S(1)}, u32[]{:S(2)}, u32[]{:S(2)}) collective-permute-start(f32[2,16,8,128]{3,2,1,0:T(8,128)S(1)} %get-tuple-element.21.refs_0_.mine), channel_id=1, source_target_pairs={{0,16},{16,0},{1,17},{17,1},{2,18},{18,2},{3,19},{19,3},{4,20},{20... | collective-permute-start | bytes 393224 | tf_op jit(solution)/shard_map/ppermute | solution.py:646
  4.9 1.6 %collective-permute-start.1 = (f32[2,13,8,128]{3,2,1,0:T(8,128)S(1)}, f32[2,13,8,128]{3,2,1,0:T(8,128)S(1)}, u32[]{:S(2)}, u32[]{:S(2)}) collective-permute-start(f32[2,13,8,128]{3,2,1,0:T(8,128)S(1)} %get-tuple-element.22), channel_id=1, source_target_pairs={{0,4},{4,0},{8,12},{12,8},{1,5},{5,1},{9,13},{13,9},{2,6},{6,2},{1... | collective-permute-start | bytes 319496 | tf_op jit(solution)/shard_map/ppermute | solution.py:647
  6.4 0.0 collective-permute-start.2
  6.4 1.9 %collective-permute-start.4 = (f32[2,13,8,128]{3,2,1,0:T(8,128)S(1)}, f32[2,13,8,128]{3,2,1,0:T(8,128)S(1)}, u32[]{:S(2)}, u32[]{:S(2)}) collective-permute-start(f32[2,13,8,128]{3,2,1,0:T(8,128)S(1)} %get-tuple-element.23), channel_id=1, source_target_pairs={{0,16},{4,24},{8,20},{12,28},{16,0},{20,8},{24,4},{28,12},{1,17},{... | collective-permute-start | bytes 319496 | tf_op jit(solution)/shard_map/ppermute | solution.py:650
  8.3 0.7 %collective-permute-start.3 = (f32[2,13,8,128]{3,2,1,0:T(8,128)S(1)}, f32[2,13,8,128]{3,2,1,0:T(8,128)S(1)}, u32[]{:S(2)}, u32[]{:S(2)}) collective-permute-start(f32[2,13,8,128]{3,2,1,0:T(8,128)S(1)} %get-tuple-element.23), channel_id=1, source_target_pairs={{0,0},{4,8},{8,4},{12,12},{1,1},{5,9},{9,5},{13,13},{2,2},{6,10},{... | collective-permute-start | bytes 319496 | tf_op jit(solution)/shard_map/ppermute | solution.py:649
  9.0 1.5 %collective-permute-done.1.refs_2_.pair = f32[2,13,8,128]{3,2,1,0:T(8,128)S(1)} collective-permute-done((f32[2,13,8,128]{3,2,1,0:T(8,128)S(1)}, f32[2,13,8,128]{3,2,1,0:T(8,128)S(1)}, u32[]{:S(2)}, u32[]{:S(2)}) %collective-permute-start.1) | collective-permute-done | bytes 106528 | tf_op jit(solution)/shard_map/ppermute | solution.py:647
  10.6 0.2 pack.2
  10.7 0.5 %collective-permute-start.5 = (f32[45,8,128]{2,1,0:T(8,128)S(1)}, f32[45,8,128]{2,1,0:T(8,128)S(1)}, u32[]{:S(2)}, u32[]{:S(2)}) collective-permute-start(f32[45,8,128]{2,1,0:T(8,128)S(1)} %get-tuple-element.24), channel_id=1, source_target_pairs={{0,16},{1,2},{2,1},{3,19},{16,0},{17,18},{18,17},{19,3},{4,20},{5,... | collective-permute-start | bytes 552968 | tf_op jit(solution)/shard_map/ppermute | solution.py:663
  11.2 1.2 %collective-permute-start.6 = (f32[45,8,128]{2,1,0:T(8,128)S(1)}, f32[45,8,128]{2,1,0:T(8,128)S(1)}, u32[]{:S(2)}, u32[]{:S(2)}) collective-permute-start(f32[45,8,128]{2,1,0:T(8,128)S(1)} %get-tuple-element.25), channel_id=1, source_target_pairs={{0,1},{1,0},{2,3},{3,2},{4,5},{5,4},{6,7},{7,6},{8,9},{9,8},{10,11... | collective-permute-start | bytes 552968 | tf_op jit(solution)/shard_map/ppermute | solution.py:663
  12.4 0.5 %collective-permute-done.4.refs_1_.inner_other = f32[2,13,8,128]{3,2,1,0:T(8,128)S(1)} collective-permute-done((f32[2,13,8,128]{3,2,1,0:T(8,128)S(1)}, f32[2,13,8,128]{3,2,1,0:T(8,128)S(1)}, u32[]{:S(2)}, u32[]{:S(2)}) %collective-permute-start.4) | collective-permute-done | bytes 106528 | tf_op jit(solution)/shard_map/ppermute | solution.py:650
  12.9 0.0 collective-permute-done.3.refs_0_.inner
  12.9 0.1 pack.3
  13.1 1.8 %collective-permute-start.7 = (f32[39,8,128]{2,1,0:T(8,128)S(1)}, f32[39,8,128]{2,1,0:T(8,128)S(1)}, u32[]{:S(2)}, u32[]{:S(2)}) collective-permute-start(f32[39,8,128]{2,1,0:T(8,128)S(1)} %get-tuple-element.26), channel_id=1, source_target_pairs={{0,16},{1,2},{2,1},{3,19},{16,0},{17,18},{18,17},{19,3},{4,20},{5,... | collective-permute-start | bytes 479240 | tf_op jit(solution)/shard_map/ppermute | solution.py:663
  14.9 1.2 %collective-permute-start.8 = (f32[39,8,128]{2,1,0:T(8,128)S(1)}, f32[39,8,128]{2,1,0:T(8,128)S(1)}, u32[]{:S(2)}, u32[]{:S(2)}) collective-permute-start(f32[39,8,128]{2,1,0:T(8,128)S(1)} %get-tuple-element.27), channel_id=1, source_target_pairs={{0,1},{1,0},{2,3},{3,2},{4,5},{5,4},{6,7},{7,6},{8,9},{9,8},{10,11... | collective-permute-start | bytes 479240 | tf_op jit(solution)/shard_map/ppermute | solution.py:663
  16.1 2.3 %collective-permute-done.7.refs_2_ = f32[39,8,128]{2,1,0:T(8,128)S(1)} collective-permute-done((f32[39,8,128]{2,1,0:T(8,128)S(1)}, f32[39,8,128]{2,1,0:T(8,128)S(1)}, u32[]{:S(2)}, u32[]{:S(2)}) %collective-permute-start.7) | collective-permute-done | bytes 159776 | tf_op jit(solution)/shard_map/ppermute | solution.py:663
  18.4 0.0 collective-permute-done.6.refs_1_
  18.4 3.0 %down.1 = (f32[4,42,8,128]{3,2,1,0:T(8,128)S(1)}, f32[4,42,8,128]{3,2,1,0:T(8,128)S(1)}, f32[4,42,8,128]{3,2,1,0:T(8,128)S(1)}, f32[4,42,8,128]{3,2,1,0:T(8,128)...) custom-call(f32[2,16,8,128]{3,2,1,0:T(8,128)S(1)} %get-tuple-element, ...), custom_call_target="tpu_custom_call" | custom-call | tf_op jit(solution)/shard_map/down/pallas_call | solution.py:669
  21.4 4.5 %collective-permute-start.9 = (f32[2,12,8,128]{3,2,1,0:T(8,128)S(1)}, f32[2,12,8,128]{3,2,1,0:T(8,128)S(1)}, u32[]{:S(2)}, u32[]{:S(2)}) collective-permute-start(f32[2,12,8,128]{3,2,1,0:T(8,128)S(1)} %get-tuple-element.29), channel_id=1, source_target_pairs={{0,8},{8,0},{4,12},{12,4},{1,9},{9,1},{5,13},{13,5},{2,10},{10,2},... | collective-permute-start | bytes 294920 | tf_op jit(solution)/shard_map/ppermute | solution.py:683
  25.9 0.2 collective-permute-start.10
  26.1 3.7 %collective-permute-done.10.near = f32[2,4,8,128]{3,2,1,0:T(8,128)S(1)} collective-permute-done((f32[2,4,8,128]{3,2,1,0:T(8,128)S(1)}, f32[2,4,8,128]{3,2,1,0:T(8,128)S(1)}, u32[]{:S(2)}, u32[]{:S(2)}) %collective-permute-start.10) | collective-permute-done | bytes 32800 | tf_op jit(solution)/shard_map/ppermute | solution.py:684
  29.9 0.0 collective-permute-done.9.far
  29.9 3.4 %up.1 = (f32[8,16,128]{2,1,0:T(8,128)}, f32[8,16,128]{2,1,0:T(8,128)}) custom-call(f32[2,16,8,128]{3,2,1,0:T(8,128)S(1)} %get-tuple-element.28.pay, f32[2,12,8,128]{3,2,1,0:T(8,128)S(1)} %collective-permute-done.9.far, f32[2,4,8,128]{3,2,1,0:T(8,128)S(1)} %collective-permute-done.10.near, f32[4,42,8,128]{3,2,1,0:T(8,128)S(1)} %get-tuple-element.31.refs_0_, ...), custom_call_target="tpu_custom_call" | custom-call | tf_op jit(solution)/shard_map/up/pallas_call | solution.py:687
  (4 shorter events, 0.0 us)
Async XLA Ops:
  1.8 8.7 %collective-permute-start = (f32[2,16,8,128]{3,2,1,0:T(8,128)S(1)}, f32[2,16,8,128]{3,2,1,0:T(8,128)S(1)}, u32[]{:S(2)}, u32[]{:S(2)}) collective-permute-start(f32[2,16,8,128]{3,2,1,0:T(8,128)S(1)} %get-tuple-element.21.refs_0_.mine), channel_id=1, source_target_pairs={{0,16},{16,0},{1,17},{17,1},{2,18},{18,2},{3,19},{19,3},{4,20},{20... | collective-permute-start | bytes 393224 | tf_op jit(solution)/shard_map/ppermute | solution.py:646
  4.9 5.7 %collective-permute-start.1 = (f32[2,13,8,128]{3,2,1,0:T(8,128)S(1)}, f32[2,13,8,128]{3,2,1,0:T(8,128)S(1)}, u32[]{:S(2)}, u32[]{:S(2)}) collective-permute-start(f32[2,13,8,128]{3,2,1,0:T(8,128)S(1)} %get-tuple-element.22), channel_id=1, source_target_pairs={{0,4},{4,0},{8,12},{12,8},{1,5},{5,1},{9,13},{13,9},{2,6},{6,2},{1... | collective-permute-start | bytes 319496 | tf_op jit(solution)/shard_map/ppermute | solution.py:647
  6.4 6.0 %collective-permute-start.2 = (f32[2,13,8,128]{3,2,1,0:T(8,128)S(1)}, f32[2,13,8,128]{3,2,1,0:T(8,128)S(1)}, u32[]{:S(2)}, u32[]{:S(2)}) collective-permute-start(f32[2,13,8,128]{3,2,1,0:T(8,128)S(1)} %get-tuple-element.22), channel_id=1, source_target_pairs={{0,20},{4,16},{8,28},{12,24},{16,4},{20,0},{24,12},{28,8},{1,21},{... | collective-permute-start | bytes 319496 | tf_op jit(solution)/shard_map/ppermute | solution.py:648
  6.4 6.5 %collective-permute-start.4 = (f32[2,13,8,128]{3,2,1,0:T(8,128)S(1)}, f32[2,13,8,128]{3,2,1,0:T(8,128)S(1)}, u32[]{:S(2)}, u32[]{:S(2)}) collective-permute-start(f32[2,13,8,128]{3,2,1,0:T(8,128)S(1)} %get-tuple-element.23), channel_id=1, source_target_pairs={{0,16},{4,24},{8,20},{12,28},{16,0},{20,8},{24,4},{28,12},{1,17},{... | collective-permute-start | bytes 319496 | tf_op jit(solution)/shard_map/ppermute | solution.py:650
  8.3 4.6 %collective-permute-start.3 = (f32[2,13,8,128]{3,2,1,0:T(8,128)S(1)}, f32[2,13,8,128]{3,2,1,0:T(8,128)S(1)}, u32[]{:S(2)}, u32[]{:S(2)}) collective-permute-start(f32[2,13,8,128]{3,2,1,0:T(8,128)S(1)} %get-tuple-element.23), channel_id=1, source_target_pairs={{0,0},{4,8},{8,4},{12,12},{1,1},{5,9},{9,5},{13,13},{2,2},{6,10},{... | collective-permute-start | bytes 319496 | tf_op jit(solution)/shard_map/ppermute | solution.py:649
  10.7 7.7 %collective-permute-start.5 = (f32[45,8,128]{2,1,0:T(8,128)S(1)}, f32[45,8,128]{2,1,0:T(8,128)S(1)}, u32[]{:S(2)}, u32[]{:S(2)}) collective-permute-start(f32[45,8,128]{2,1,0:T(8,128)S(1)} %get-tuple-element.24), channel_id=1, source_target_pairs={{0,16},{1,2},{2,1},{3,19},{16,0},{17,18},{18,17},{19,3},{4,20},{5,... | collective-permute-start | bytes 552968 | tf_op jit(solution)/shard_map/ppermute | solution.py:663
  11.2 7.2 %collective-permute-start.6 = (f32[45,8,128]{2,1,0:T(8,128)S(1)}, f32[45,8,128]{2,1,0:T(8,128)S(1)}, u32[]{:S(2)}, u32[]{:S(2)}) collective-permute-start(f32[45,8,128]{2,1,0:T(8,128)S(1)} %get-tuple-element.25), channel_id=1, source_target_pairs={{0,1},{1,0},{2,3},{3,2},{4,5},{5,4},{6,7},{7,6},{8,9},{9,8},{10,11... | collective-permute-start | bytes 552968 | tf_op jit(solution)/shard_map/ppermute | solution.py:663
  13.1 5.3 %collective-permute-start.7 = (f32[39,8,128]{2,1,0:T(8,128)S(1)}, f32[39,8,128]{2,1,0:T(8,128)S(1)}, u32[]{:S(2)}, u32[]{:S(2)}) collective-permute-start(f32[39,8,128]{2,1,0:T(8,128)S(1)} %get-tuple-element.26), channel_id=1, source_target_pairs={{0,16},{1,2},{2,1},{3,19},{16,0},{17,18},{18,17},{19,3},{4,20},{5,... | collective-permute-start | bytes 479240 | tf_op jit(solution)/shard_map/ppermute | solution.py:663
  14.9 3.5 %collective-permute-start.8 = (f32[39,8,128]{2,1,0:T(8,128)S(1)}, f32[39,8,128]{2,1,0:T(8,128)S(1)}, u32[]{:S(2)}, u32[]{:S(2)}) collective-permute-start(f32[39,8,128]{2,1,0:T(8,128)S(1)} %get-tuple-element.27), channel_id=1, source_target_pairs={{0,1},{1,0},{2,3},{3,2},{4,5},{5,4},{6,7},{7,6},{8,9},{9,8},{10,11... | collective-permute-start | bytes 479240 | tf_op jit(solution)/shard_map/ppermute | solution.py:663
  21.4 8.5 %collective-permute-start.9 = (f32[2,12,8,128]{3,2,1,0:T(8,128)S(1)}, f32[2,12,8,128]{3,2,1,0:T(8,128)S(1)}, u32[]{:S(2)}, u32[]{:S(2)}) collective-permute-start(f32[2,12,8,128]{3,2,1,0:T(8,128)S(1)} %get-tuple-element.29), channel_id=1, source_target_pairs={{0,8},{8,0},{4,12},{12,4},{1,9},{9,1},{5,13},{13,5},{2,10},{10,2},... | collective-permute-start | bytes 294920 | tf_op jit(solution)/shard_map/ppermute | solution.py:683
  25.9 3.9 %collective-permute-start.10 = (f32[2,4,8,128]{3,2,1,0:T(8,128)S(1)}, f32[2,4,8,128]{3,2,1,0:T(8,128)S(1)}, u32[]{:S(2)}, u32[]{:S(2)}) collective-permute-start(f32[2,4,8,128]{3,2,1,0:T(8,128)S(1)} %get-tuple-element.30), channel_id=1, source_target_pairs={{0,4},{4,0},{8,12},{12,8},{1,5},{5,1},{9,13},{13,9},{2,6},{6,2},{1... | collective-permute-start | bytes 98312 | tf_op jit(solution)/shard_map/ppermute | solution.py:684
